TPU v7x, 256 devices: a whole 4x4x8 slice. The times are simulated.
256 devices in a mesh: utt: 8 (over y, core), tm: 32 (over z, x).
Axes of the slice: x: 4, y: 4, z: 8, core: 2. Of those that a mesh axis runs over, the one named last changes fastest.
Arguments:
- glu_out: bfloat16 [131072, 1536], P(('utt', 'tm')), may hold values from -6 to 6
- cotangent: bfloat16 [131072, 1536], P(('utt', 'tm')), may hold values from -12 to 12
- kernel: float32 [31, 1536], replicated, may hold values from -1 to 1
- conv_bias: float32 [1536], replicated, may hold values from -3 to 3
- out_weight: bfloat16 [1536, 1536], P('tm'), may hold values from -0.15625 to 0.15625
- blocks: int32 [8, 8], P('utt'), may hold values from 1 to 64, 128 in all within a row
- last_fill: int32 [8, 8], P('utt'), may hold values from 1 to 128
- noise_draws: float32 [8, 32, 1536], P(None, 'utt', 'tm'), may hold values from -6 to 6
- band_coef: float32 [8], replicated, may hold values from 0.05 to 1
Outputs:
- block_out: bfloat16 [131072, 1536], P(('utt', 'tm'))
- mean_grad: float32 [32, 1536], P('utt', 'tm')
Inputs may be any that keep to these rules, and one draw needn't show every extreme that they name: Each row of blocks sums to exactly 128, and its largest entry is exactly 64.
All inputs are finite; a program needn't handle non-finite values.
Results may differ from a plain program's by a relative error of at most 0.0049.
Values may be sent and summed in bfloat16 or wider, within the bound.
No kernel may reach another device: no remote copies, remote signals or barrier semaphores. Data moves between devices by JAX's collectives and lax.ppermute only.
A program may use at most 64 MiB of HBM per device.

v0:
```python
import math

import jax
import jax.numpy as jnp
from jax import lax
from jax.sharding import PartitionSpec as P

BLOCK = 128


def with_halo(block, sides, width):
    for axis, dim in sides:
        count = lax.axis_size(axis)
        forward = [(i, i + 1) for i in range(count - 1)]
        backward = [(target, source) for source, target in forward]
        low = lax.ppermute(
            lax.slice_in_dim(block, block.shape[dim] - width, None, axis=dim), axis, forward
        )
        high = lax.ppermute(lax.slice_in_dim(block, 0, width, axis=dim), axis, backward)
        block = jnp.concatenate([low, block, high], axis=dim)
    return block


def carried_in(value, axis, combine, identity):
    length, position = (lax.axis_size(axis), lax.axis_index(axis))
    everything = jax.tree.map(lambda part: lax.all_gather(part, axis), value)
    start = jax.tree.map(
        lambda part, zero: jnp.broadcast_to(jnp.asarray(zero, part.dtype), part.shape),
        value,
        identity,
    )

    def hop(k, before):
        reached = k < position
        new = combine(before, jax.tree.map(lambda part: part[k], everything))
        return jax.tree.map(lambda a, b: jnp.where(reached, a, b), new, before)

    return lax.fori_loop(0, length, hop, start)


def utt_ids(counts, blk_index):
    cumul = jnp.cumsum(counts)
    return jnp.sum(
        (cumul[None, :] <= blk_index[:, None]).astype(jnp.int32), axis=1, dtype=jnp.int32
    )


def utt_tables(counts, last_fills, blk_index):
    cumul = jnp.cumsum(counts)
    utt_of = utt_ids(counts, blk_index)
    chosen = (utt_of[:, None] == jnp.arange(counts.shape[0], dtype=jnp.int32)[None, :]).astype(
        jnp.int32
    )
    end_of = jnp.sum(chosen * cumul[None, :], axis=1, dtype=jnp.int32)
    length_of = jnp.sum(chosen * counts[None, :], axis=1, dtype=jnp.int32)
    fill_of = jnp.sum(chosen * last_fills[None, :], axis=1, dtype=jnp.int32)
    return (utt_of, end_of, length_of, fill_of)


def frame_valid(blk_index, end_of, fill_of):
    limit = jnp.where(end_of - 1 == blk_index, fill_of, BLOCK)
    return jnp.arange(BLOCK, dtype=jnp.int32)[None, :] < limit[:, None]


def segment_join(earlier, latter):
    return (latter[0] + (1.0 - latter[1]) * earlier[0], jnp.maximum(earlier[1], latter[1]))


def per_device(
    glu_out, cotangent, kernel, conv_bias, out_weight, blocks, last_fill, noise_draws, band_coef
):
    tap_count = kernel.shape[0]
    rim_width = tap_count // 2
    frames, width = glu_out.shape
    blk_count = frames // BLOCK
    shards = lax.axis_size("tm")
    device = lax.axis_index("tm")
    counts = blocks[0]
    last_fills = last_fill[0]
    first_blk = device * blk_count
    blk_index = first_blk + jnp.arange(blk_count, dtype=jnp.int32)
    utt_of, end_of, length_of, fill_of = utt_tables(counts, last_fills, blk_index)
    valid_mask = frame_valid(blk_index, end_of, fill_of).reshape(frames)
    seg_ids = jnp.repeat(utt_of, BLOCK, total_repeat_length=frames)
    padded_pos = first_blk * BLOCK - rim_width + jnp.arange(frames + 2 * rim_width, dtype=jnp.int32)
    inside = (padded_pos >= 0) & (padded_pos < shards * frames)
    padded_seg = jnp.where(inside, utt_ids(counts, jnp.floor_divide(padded_pos, BLOCK)), -1)
    masked_in = glu_out * valid_mask[:, None].astype(jnp.bfloat16)
    padded_in = with_halo(masked_in, (("tm", 0),), rim_width)
    conv_out = jnp.zeros((frames, width), jnp.float32) + conv_bias[None, :]
    for tap_idx in range(tap_count):
        same_utt = (padded_seg[tap_idx : tap_idx + frames] == seg_ids).astype(jnp.float32)[:, None]
        conv_out = (
            conv_out
            + kernel[tap_idx][None, :]
            * padded_in[tap_idx : tap_idx + frames].astype(jnp.float32)
            * same_utt
        )
    keep_mask = valid_mask.astype(jnp.float32)[:, None]
    hidden = (jax.nn.silu(conv_out) * keep_mask).astype(jnp.bfloat16)
    full_weight = lax.all_gather(out_weight, "tm", axis=0, tiled=True)
    block_out = jnp.dot(hidden, full_weight, preferred_element_type=jnp.float32)
    hidden_grad = lax.dot_general(
        cotangent, full_weight, (((1,), (1,)), ((), ())), preferred_element_type=jnp.float32
    )
    logistic = jax.nn.sigmoid(conv_out)
    conv_grad = hidden_grad * logistic * (1.0 + conv_out * (1.0 - logistic)) * keep_mask
    tap_rows = []
    for tap_idx in range(tap_count):
        same_utt = (padded_seg[tap_idx : tap_idx + frames] == seg_ids).astype(jnp.float32)[:, None]
        product = conv_grad * padded_in[tap_idx : tap_idx + frames].astype(jnp.float32) * same_utt
        tap_rows.append(jnp.sum(product.reshape(blk_count, BLOCK, width), axis=1))
    tap_rows.append(jnp.sum(conv_grad.reshape(blk_count, BLOCK, width), axis=1))
    block_grads = jnp.stack(tap_rows, axis=1)
    starts = end_of - length_of
    continues = starts[0] < first_blk
    starts_here = (starts[blk_count - 1] >= first_blk).astype(jnp.float32)
    tail_weight = (utt_of == utt_of[blk_count - 1]).astype(jnp.float32)
    tail_sum = jnp.einsum("b,bkc->kc", tail_weight, block_grads, precision=lax.Precision.HIGHEST)
    incoming, flag_seen = carried_in(
        (tail_sum, starts_here), "tm", segment_join, (jnp.zeros_like(tail_sum), jnp.float32(0.0))
    )
    is_end = end_of - 1 == blk_index
    same_blocks = ((utt_of[:, None] == utt_of[None, :]) & is_end[:, None]).astype(jnp.float32)
    full_grads = jnp.einsum(
        "ab,bkc->akc", same_blocks, block_grads, precision=lax.Precision.HIGHEST
    )
    joined = (is_end & (utt_of == utt_of[0]) & continues).astype(jnp.float32)
    full_grads = full_grads + joined[:, None, None] * incoming[None, :, :]
    grad_norm = jnp.sqrt(jnp.sum(full_grads * full_grads, axis=(1, 2)))
    clip_bound = 300.0 * math.sqrt(width)
    factor = clip_bound / jnp.maximum(grad_norm, clip_bound)
    contrib = jnp.einsum(
        "a,akc->kc",
        factor * is_end.astype(jnp.float32),
        full_grads,
        precision=lax.Precision.HIGHEST,
    )
    groups_utt = lax.axis_size("utt")
    col_part = lax.psum_scatter(contrib, "tm", scatter_dimension=1, tiled=True)
    own_share = lax.psum_scatter(col_part, "utt", scatter_dimension=0, tiled=True)
    mixture = jnp.sum(band_coef[:, None, None] * noise_draws, axis=0)
    mean_grad = (own_share + 0.1 * clip_bound * mixture) / (counts.shape[0] * groups_utt)
    return (block_out.astype(jnp.bfloat16), mean_grad)


def solution(mesh):
    return jax.shard_map(
        per_device,
        mesh=mesh,
        in_specs=(
            P(("utt", "tm"), None),
            P(("utt", "tm"), None),
            P(),
            P(),
            P("tm", None),
            P("utt", None),
            P("utt", None),
            P(None, "utt", "tm"),
            P(),
        ),
        out_specs=(P(("utt", "tm"), None), P("utt", "tm")),
        check_vma=False,
    )
```

profile of v0, /device:TPU:1, one launch (start us, length us, event | category | flops | bytes accessed | tf_op | source)
XLA Modules:
  0.0 546.1 jit_solution(12561590370782603819)
XLA Ops:
  11.8 1.2 and_convert_fusion
  13.6 1.6 broadcast_multiply_fusion
  15.2 1.3 collective-permute-start.1
  16.5 4.6 collective-permute-start
  22.1 2.5 compare_select_fusion.1
  26.8 33.8 %fusion.82 = f32[512,1536]{1,0:T(8,128)} fusion(bf16[512,1536]{1,0:T(8,128)(2,1)S(1)} %broadcast_multiply_fusion, bf16[15,1536]{1,0:T(8,128)(2,1)S(1)} %collective-permute-done.1, bf16[15,1536]{1,0:T(8,128)(2,1)S(1)} %collective-permute-done, f32[512]{0:T(512)} %get-tuple-element.208, f32[1536]{0:T(1024)} %get-tuple-element.188, f32[512]{0:T(512)} %get-tuple-element.209, ...), kind=kLoop, calls=%fused_computation.174 | loop fusion | flops 168296448 | bytes 5070848 | tf_op jit(solution)/shard_map/add | solution.py:94
  60.6 34.8 %all-gather.4.cloned.1.call-done = bf16[1536,1536]{1,0:T(8,128)(2,1)} async-done(((bf16[48,1536]{1,0:T(8,128)(2,1)}), bf16[1536,1536]{1,0:T(8,128)(2,1)}) %all-gather.4.cloned.1.call-update) | async-done | bytes 4718608 | tf_op jit(solution)/shard_map/all_gather | solution.py:101
  95.5 8.2 %bitcast_reduce_fusion.29 = (f32[4,1536]{1,0:T(4,128)S(1)}, f32[4,1536]{1,0:T(4,128)S(1)}, f32[4,1536]{1,0:T(4,128)S(1)}, f32[512,1536]{1,0:T(8,128)S(1)}) fusion(f32[512]{0:T(512)S(1)} %copy-done.33, bf16[512,1536]{1,0:T(8,128)(2,1)S(1)} %broadcast_multiply_fusion, bf16[15,1536]{1,0:T(8,128)(2,1)S(1)} %collective-permute-done, f32[512]{0:T(512)S(1)} %copy-done.32, ...), kind=kOutput, calls=%fused_computation.217 | convolution fusion | flops 2439493632 | bytes 14283776 | tf_op jit(solution)/shard_map/dot_general | solution.py:103
  103.8 5.5 %bitcast_reduce_fusion.23 = (f32[4,1536]{1,0:T(4,128)S(1)}, f32[4,1536]{1,0:T(4,128)S(1)}, f32[4,1536]{1,0:T(4,128)S(1)}, f32[4,1536]{1,0:T(4,128)S(1)}, f32[4,1536]{1,0:T(4,128)S(1)}, /*index=5*/f32[4,1536]{1,0:T(4,128)S(1)}) fusion(f32[512]{0:T(512)S(1)} %copy-done.8, f32[512,1536]{1,0:T(8,128)S(1)} %get-tuple-element.246, ...), kind=kLoop, calls=%fused_computation.211 | loop fusion | flops 32993280 | bytes 4924416 | tf_op jit(solution)/shard_map/reduce_sum | solution.py:112
  109.6 4.5 bitcast_reduce_fusion.17
  114.2 5.0 bitcast_reduce_fusion.13
  119.4 9.4 %bitcast_reduce_fusion.7 = (f32[4,1536]{1,0:T(4,128)S(1)}, f32[4,1536]{1,0:T(4,128)S(1)}, f32[4,1536]{1,0:T(4,128)S(1)}, f32[4,1536]{1,0:T(4,128)S(1)}, f32[4,1536]{1,0:T(4,128)S(1)}, /*index=5*/f32[4,1536]{1,0:T(4,128)S(1)}) fusion(f32[512]{0:T(512)S(1)} %copy-done.20, f32[512,1536]{1,0:T(8,128)S(1)} %get-tuple-element.246, ...), kind=kLoop, calls=%fused_computation.195 | loop fusion | flops 32993280 | bytes 4924416 | tf_op jit(solution)/shard_map/reduce_sum | solution.py:112
  129.1 7.3 %bitcast_reduce_fusion.1 = (f32[4,1536]{1,0:T(4,128)S(1)}, f32[4,1536]{1,0:T(4,128)S(1)}, f32[4,1536]{1,0:T(4,128)S(1)}, f32[4,1536]{1,0:T(4,128)S(1)}, f32[4,15...) fusion(f32[512,1536]{1,0:T(8,128)S(1)} %get-tuple-element.246, ...), kind=kLoop, calls=%fused_computation.189 | loop fusion | flops 33773568 | bytes 4948992 | tf_op jit(solution)/shard_map/reduce_sum | solution.py:112
  137.4 1.5 fusion.168
  143.0 57.6 %all-reduce = f32[32]{0:T(128)S(1)} all-reduce(f32[32]{0:T(128)S(1)} %dynamic-update-slice.3), channel_id=1, replica_groups=mesh['utt'=8,'tm'=32] {'tm'}, use_global_device_ids=true, to_apply=%add | all-reduce | flops 32 | bytes 256
  200.7 27.4 %all-gather.6.cloned.1.call-done = f32[1024,1536]{1,0:T(8,128)} async-done(((f32[32,1536]{1,0:T(8,128)}), f32[1024,1536]{1,0:T(8,128)}) %all-gather.6.cloned.1.call-update) | async-done | bytes 6291472 | tf_op jit(solution)/shard_map/all_gather | solution.py:26
  228.0 73.9 %while.15 = (s32[]{:T(128)}, f32[32,1536]{1,0:T(8,128)S(1)}, s32[]{:T(128)}, f32[32,32,1536]{2,1,0:T(8,128)}, f32[32]{0:T(128)S(1)}, /*index=5*/s32[]{:T(128)}, f32[1]{0:T(128)}, s32[]{:T(128)}) while((s32[]{:T(128)}, f32[32,1536]{1,0:T(8,128)S(1)}, s32[]{:T(128)}, f32[32,32,1536]{2,1,0:T(8,128)}, f32[32]{0:T(128)S(1)}, ...), condition=%wide.region_39.40_spmd.clone, body=%wide.region_38.39_spmd.clone.sunk | while | flops 196613 | bytes 589969 | solution.py:38
  231.5 1.1 fusion.197
  302.0 1.3 multiply_reduce_fusion
  303.3 1.4 fusion.178
  304.7 1.2 copy.15
  305.9 7.1 %convolution_convert_fusion = bf16[512,1536]{1,0:T(8,128)(2,1)} fusion(bf16[1536,1536]{1,0:T(8,128)(2,1)} %all-gather.4.cloned.1.call-done, f32[512,1536]{1,0:T(8,128)} %fusion.82, f32[512]{0:T(512)S(1)} %copy-done.38), kind=kOutput, calls=%fused_computation.222 | convolution fusion | flops 2421424128 | bytes 9439232 | tf_op jit(solution)/shard_map/dot_general | solution.py:102
  313.0 199.0 %reduce-scatter.4.cloned.1.call-done = f32[48,32]{1,0:T(8,128)} async-done(((f32[1536,32]{1,0:T(8,128)}), f32[48,32]{1,0:T(8,128)}) %reduce-scatter.4.cloned.1.call-update) | async-done | bytes 6160
  512.8 26.2 %all-reduce.1 = f32[32,48]{1,0:T(8,128)S(1)} all-reduce(f32[32,48]{1,0:T(8,128)S(1)} %copy.14), channel_id=4, replica_groups=mesh['utt'=8,'tm'=32] {'utt'}, use_global_device_ids=true, to_apply=%region_42.43.clone | all-reduce | flops 1536 | bytes 12288
  (215 shorter events, 65.7 us)
Async XLA Ops:
  7.2 88.2 %copy-start = (bf16[512,1536]{1,0:T(8,128)(2,1)S(1)}, bf16[512,1536]{1,0:T(8,128)(2,1)}, u32[]{:S(2)}) copy-start(bf16[512,1536]{1,0:T(8,128)(2,1)} %param.14) | copy-start | bytes 4718596
  7.2 14.0 %copy-start.3 = (f32[31,1536]{1,0:T(8,128)S(1)}, f32[31,1536]{1,0:T(8,128)}, u32[]{:S(2)}) copy-start(f32[31,1536]{1,0:T(8,128)} %param.15) | copy-start | bytes 571396
  7.2 88.2 %all-gather.4.cloned.1.call-start = ((), (), s32[]{:S(2)}) async-start(), calls=%async_computation.1 | async-start | bytes 4866048 | tf_op jit(solution)/shard_map/all_gather | solution.py:101
  7.9 220.1 %all-gather.6.cloned.1.call-start = ((), (), s32[]{:S(2)}) async-start(), calls=%async_computation.2 | async-start | bytes 6488064 | tf_op jit(solution)/shard_map/all_gather | solution.py:26
  15.2 11.6 %collective-permute-start.1 = (bf16[15,1536]{1,0:T(8,128)(2,1)S(1)}, bf16[15,1536]{1,0:T(8,128)(2,1)S(1)}, u32[]{:S(2)}, u32[]{:S(2)}) collective-permute-start(bf16[15,1536]{1,0:T(8,128)(2,1)S(1)} %get-tuple-element.206), channel_id=1, source_target_pairs={{1,0},{2,1},{3,2},{4,3},{5,4},{6,5},{7,6},{8,7},{9,8},{10,9},{11,1... | collective-permute-start | bytes 138248 | tf_op jit(solution)/shard_map/ppermute | solution.py:19
  16.5 10.4 %collective-permute-start = (bf16[15,1536]{1,0:T(8,128)(2,1)S(1)}, bf16[15,1536]{1,0:T(8,128)(2,1)S(1)}, u32[]{:S(2)}, u32[]{:S(2)}) collective-permute-start(bf16[15,1536]{1,0:T(8,128)(2,1)S(1)} %get-tuple-element.205), channel_id=1, source_target_pairs={{0,1},{1,2},{2,3},{3,4},{4,5},{5,6},{6,7},{7,8},{8,9},{9,10},{10,1... | collective-permute-start | bytes 138248 | tf_op jit(solution)/shard_map/ppermute | solution.py:16
  26.8 68.6 %copy-start.32 = (f32[512]{0:T(512)S(1)}, f32[512]{0:T(512)}, u32[]{:S(2)}) copy-start(f32[512]{0:T(512)} %get-tuple-element.225) | copy-start | bytes 6148
  26.8 68.6 %copy-start.33 = (f32[512]{0:T(512)S(1)}, f32[512]{0:T(512)}, u32[]{:S(2)}) copy-start(f32[512]{0:T(512)} %get-tuple-element.237) | copy-start | bytes 6148
  26.8 68.6 %copy-start.34 = (f32[512]{0:T(512)S(1)}, f32[512]{0:T(512)}, u32[]{:S(2)}) copy-start(f32[512]{0:T(512)} %get-tuple-element.207) | copy-start | bytes 6148
  119.3 9.7 %copy-start.14 = (f32[512]{0:T(512)S(1)}, f32[512]{0:T(512)}, u32[]{:S(2)}) copy-start(f32[512]{0:T(512)} %get-tuple-element.208) | copy-start | bytes 6148
  119.3 9.7 %copy-start.15 = (f32[512]{0:T(512)S(1)}, f32[512]{0:T(512)}, u32[]{:S(2)}) copy-start(f32[512]{0:T(512)} %get-tuple-element.209) | copy-start | bytes 6148
  119.3 9.7 %copy-start.16 = (f32[512]{0:T(512)S(1)}, f32[512]{0:T(512)}, u32[]{:S(2)}) copy-start(f32[512]{0:T(512)} %get-tuple-element.210) | copy-start | bytes 6148
  119.3 9.7 %copy-start.17 = (f32[512]{0:T(512)S(1)}, f32[512]{0:T(512)}, u32[]{:S(2)}) copy-start(f32[512]{0:T(512)} %get-tuple-element.211) | copy-start | bytes 6148
  119.3 9.7 %copy-start.18 = (f32[512]{0:T(512)S(1)}, f32[512]{0:T(512)}, u32[]{:S(2)}) copy-start(f32[512]{0:T(512)} %get-tuple-element.212) | copy-start | bytes 6148
  119.3 9.7 %copy-start.19 = (f32[512]{0:T(512)S(1)}, f32[512]{0:T(512)}, u32[]{:S(2)}) copy-start(f32[512]{0:T(512)} %get-tuple-element.213) | copy-start | bytes 6148
  129.0 11.2 %copy-start.41 = (u32[256]{0:T(256)S(1)}, u32[256]{0:T(256)}, u32[]{:S(2)}) copy-start(u32[256]{0:T(256)} %constant.171) | copy-start | bytes 3076
  129.0 11.9 %copy-start.40 = (u32[256]{0:T(256)S(1)}, u32[256]{0:T(256)}, u32[]{:S(2)}) copy-start(u32[256]{0:T(256)} %constant.177) | copy-start | bytes 3076
  129.0 71.5 %copy-start.31 = (f32[8,4,48]{2,1,0:T(4,128)S(1)}, f32[8,4,48]{2,1,0:T(4,128)}, u32[]{:S(2)}) copy-start(f32[8,4,48]{2,1,0:T(4,128)} %param.20) | copy-start | bytes 18436
  129.0 71.5 %copy-start.39 = (f32[8]{0:T(128)S(1)}, f32[8]{0:T(128)}, u32[]{:S(2)}) copy-start(f32[8]{0:T(128)} %param.21) | copy-start | bytes 100
  136.4 165.6 %copy-start.36 = (pred[4]{0:T(512)(128)(4,1)S(1)}, pred[4]{0:T(512)(128)(4,1)}, u32[]{:S(2)}) copy-start(pred[4]{0:T(512)(128)(4,1)} %copy-done.35) | copy-start | bytes 16
  136.4 165.6 %copy-start.37 = (f32[4]{0:T(128)S(1)}, f32[4]{0:T(128)}, u32[]{:S(2)}) copy-start(f32[4]{0:T(128)} %get-tuple-element.203) | copy-start | bytes 52
  138.8 163.1 %copy-start.2 = (f32[4,32,1536]{2,0,1:T(4,128)S(1)}, f32[4,32,1536]{2,0,1:T(4,128)}, u32[]{:S(2)}) copy-start(f32[4,32,1536]{2,0,1:T(4,128)} %copy-done.1) | copy-start | bytes 2359300
  139.6 372.4 %reduce-scatter.4.cloned.1.call-start = ((), (), s32[]{:S(2)}) async-start(), calls=%async_computation.3 | async-start | bytes 811008
  228.0 77.9 %copy-start.38 = (f32[512]{0:T(512)S(1)}, f32[512]{0:T(512)}, u32[]{:S(2)}) copy-start(f32[512]{0:T(512)} %get-tuple-element.240) | copy-start | bytes 6148
  (23 other events, 132.2 us)
Sparse Core Ops, SparseCore 0:
  10.6 84.7 all-gather.3
  139.7 88.2 all-gather.5
  306.0 205.9 reduce-scatter.3
where the time goes:
time: 549 us; the launch traced here: 546 us
  waiting for transfers between devices  262 us (48%)
  other arithmetic  110 us (20%)
  blocking collectives  83.7 us (15%)
  local copies, waits for them, and re-layouts  28 us (5%)
  loops' own time  20.7 us (4%)
  matrix products  19.5 us (4%)
  between operations  16.5 us (3%)
  starting transfers between devices  5.98 us (1%)
    unnamed x4, waiting for transfers between devices  200 us
    unnamed x2, blocking collectives  83.7 us
    all_gather x1, waiting for transfers between devices, per_device(): full_weight = lax.all_gather(out_weight, 'tm', axis=0, tiled=True)  34.8 us
    select_n x32, other arithmetic, hop(): return jax.tree.map(lambda a, b: jnp.where(reached, a, b), new, before)  34.3 us
    add x1, other arithmetic, per_device(): conv_out + kernel[tap_idx][None, :] * padded_in[tap_idx:tap_idx + frames]...  33.8 us
    reduce_sum x5, other arithmetic, per_device(): tap_rows.append(jnp.sum(product.reshape(blk_count, BLOCK, width), axis=1))  31.8 us
    all_gather x1, waiting for transfers between devices, carried_in(): everything = jax.tree.map(lambda part: lax.all_gather(part, axis), value)  27.4 us
    another operation x1, loops' own time, carried_in(): return lax.fori_loop(0, length, hop, start)  20.7 us
  transfers between devices with their start and end apart: 5, of which 3 were waited for; matrix products, arithmetic and copies ran while one was open for 10% of the time, Pallas kernels for 0%

commit v1 on v0

v1 whole, which is shorter than its diff:
```python
import math

import jax
import jax.numpy as jnp
from jax import lax
from jax.experimental import pallas as pl
from jax.experimental.pallas import tpu as pltpu
from jax.sharding import PartitionSpec as P

BLOCK = 128
LANES = 128
RIM = 16
PADDED = BLOCK + 2 * RIM
STEP = 256
TILES = STEP // LANES


def block_facts(counts, fills, utts, index):
    utt, limit, cumul = jnp.int32(0), jnp.int32(BLOCK), jnp.int32(0)
    for i in range(utts):
        cumul = cumul + counts[i]
        utt = utt + (cumul <= index).astype(jnp.int32)
        limit = jnp.where(cumul - 1 == index, fills[i], limit)
    return utt, limit


def conv_body(first, counts, fills, x, low, high, kernel, bias, hidden, slope, padded):
    taps = kernel.shape[0]
    frames = x.shape[0]
    blks = frames // BLOCK
    utts = counts.shape[0]
    facts = [block_facts(counts, fills, utts, first[0] + b) for b in range(-1, blks + 1)]
    row = lax.broadcasted_iota(jnp.int32, (BLOCK, LANES), 0)
    rim_row = lax.broadcasted_iota(jnp.int32, (RIM, LANES), 0)
    for tile in range(TILES):
        lanes = slice(tile * LANES, (tile + 1) * LANES)
        for b in range(blks):
            utt, limit = facts[b + 1]
            before = (facts[b][0] == utt) & (first[0] + b > 0)
            after = facts[b + 2][0] == utt
            keep = row < limit
            here = x[b * BLOCK : (b + 1) * BLOCK, lanes].astype(jnp.float32)
            left = low[:, lanes] if b == 0 else x[b * BLOCK - RIM : b * BLOCK, lanes]
            right = high[:, lanes] if b == blks - 1 else x[(b + 1) * BLOCK : (b + 1) * BLOCK + RIM, lanes]
            padded[tile, b, :RIM] = jnp.where(
                rim_row < jnp.where(before, RIM, 0), left.astype(jnp.float32), 0.0
            )
            padded[tile, b, RIM : RIM + BLOCK] = jnp.where(keep, here, 0.0)
            padded[tile, b, RIM + BLOCK :] = jnp.where(
                rim_row < jnp.where(after, facts[b + 2][1], 0), right.astype(jnp.float32), 0.0
            )
            total = jnp.broadcast_to(bias[:, lanes], (BLOCK, LANES))
            for k in range(taps):
                total = total + kernel[k : k + 1, lanes] * padded[tile, b, k + 1 : k + 1 + BLOCK]
            logistic = jax.nn.sigmoid(total)
            rows = slice(b * BLOCK, (b + 1) * BLOCK)
            hidden[rows, lanes] = jnp.where(keep, total * logistic, 0.0).astype(jnp.bfloat16)
            slope[rows, lanes] = jnp.where(
                keep, logistic * (1.0 + total * (1.0 - logistic)), 0.0
            )


def conv(first, counts, fills, x, low, high, kernel, bias):
    frames, width = x.shape
    blks = frames // BLOCK
    scalars = pl.BlockSpec(memory_space=pltpu.SMEM)
    column = lambda rows: pl.BlockSpec((rows, STEP), lambda c: (0, c))
    return pl.pallas_call(
        conv_body,
        grid=(width // STEP,),
        in_specs=[scalars] * 3
        + [column(frames), column(RIM), column(RIM), column(kernel.shape[0]), column(1)],
        out_specs=[
            column(frames),
            column(frames),
            pl.BlockSpec((TILES, blks, PADDED, LANES), lambda c: (c, 0, 0, 0)),
        ],
        out_shape=[
            jax.ShapeDtypeStruct((frames, width), jnp.bfloat16),
            jax.ShapeDtypeStruct((frames, width), jnp.float32),
            jax.ShapeDtypeStruct((width // LANES, blks, PADDED, LANES), jnp.float32),
        ],
        compiler_params=pltpu.CompilerParams(vmem_limit_bytes=24 << 20),
        cost_estimate=pl.CostEstimate(
            flops=2 * 31 * frames * width, bytes_accessed=12 * frames * width, transcendentals=frames * width
        ),
        name="conv",
    )(first, counts, fills, x, low, high, kernel, bias)


def grads_body(cot, weight, slope, padded, out, grad, parts):
    taps = 31
    blks = padded.shape[1]
    slots = 32
    hidden_grad = lax.dot_general(
        cot[...], weight[...], (((1,), (1,)), ((), ())), preferred_element_type=jnp.float32
    )
    for tile in range(TILES):
        lanes = slice(tile * LANES, (tile + 1) * LANES)
        grad[tile] = hidden_grad[:, lanes] * slope[:, lanes]
    for tile in range(TILES):
        for b in range(blks):
            own = grad[tile, b * BLOCK : (b + 1) * BLOCK]
            for k in range(taps + 1):
                term = own * padded[tile, b, k + 1 : k + 1 + BLOCK] if k < taps else own
                at = (b * slots + k) * 8
                parts[at : at + 8] = jnp.sum(term.reshape(BLOCK // 8, 8, LANES), axis=0)
        total = parts[pl.ds(0, blks * slots, stride=8)]
        for s in range(1, 8):
            total = total + parts[pl.ds(s, blks * slots, stride=8)]
        out[tile * LANES : (tile + 1) * LANES] = total.T.astype(out.dtype)


def grads(cot, weight, slope, padded):
    frames, width = cot.shape
    channels = weight.shape[0]
    blks = frames // BLOCK
    return pl.pallas_call(
        grads_body,
        grid=(channels // STEP,),
        in_specs=[
            pl.BlockSpec((frames, width), lambda c: (0, 0)),
            pl.BlockSpec((STEP, width), lambda c: (c, 0)),
            pl.BlockSpec((frames, STEP), lambda c: (0, c)),
            pl.BlockSpec((TILES, blks, PADDED, LANES), lambda c: (c, 0, 0, 0)),
        ],
        out_specs=pl.BlockSpec((STEP, blks * 32), lambda c: (c, 0)),
        out_shape=jax.ShapeDtypeStruct((channels, blks * 32), jnp.bfloat16),
        scratch_shapes=[
            pltpu.VMEM((TILES, frames, LANES), jnp.float32),
            pltpu.VMEM((blks * 32 * 8, LANES), jnp.float32),
        ],
        compiler_params=pltpu.CompilerParams(vmem_limit_bytes=32 << 20),
        cost_estimate=pl.CostEstimate(
            flops=2 * frames * width * channels, bytes_accessed=12 * frames * channels, transcendentals=0
        ),
        name="grads",
    )(cot, weight, slope, padded)


def sums_body(counts, parts, sums, norms):
    senders, channels, lanes = parts.shape
    utts = counts.shape[0]
    per = lanes // 32
    blk = lax.broadcasted_iota(jnp.int32, (senders, lanes), 0) * per + (
        lax.broadcasted_iota(jnp.int32, (senders, lanes), 1) // 32
    )
    utt_of, cumul = jnp.zeros((senders, lanes), jnp.int32), jnp.int32(0)
    for i in range(utts):
        cumul = cumul + counts[i]
        utt_of = utt_of + (cumul <= blk).astype(jnp.int32)
    spot = lax.broadcasted_iota(jnp.int32, (1, lanes), 1)
    row = jnp.zeros((1, lanes), jnp.float32)
    totals = [jnp.zeros((channels, lanes), jnp.float32) for _ in range(utts)]
    for s in range(senders):
        part = parts[s].astype(jnp.float32)
        owner = utt_of[s : s + 1]
        for u in range(utts):
            totals[u] = totals[u] + jnp.where(owner == u, part, 0.0)
    for u in range(utts):
        total = totals[u]
        total = total + pltpu.roll(total, 64, 1)
        total = total + pltpu.roll(total, 32, 1)
        sums[u] = total
        square = jnp.sum(jnp.sum(total * total, axis=0, keepdims=True), axis=1, keepdims=True)
        row = row + jnp.where(spot == u, square * (1.0 / per), 0.0)
    norms[...] = jnp.broadcast_to(row[None], norms.shape)


def sums_and_norms(counts, parts):
    senders, channels, lanes = parts.shape
    utts = counts.shape[0]
    vmem = pl.BlockSpec(memory_space=pltpu.VMEM)
    return pl.pallas_call(
        sums_body,
        in_specs=[pl.BlockSpec(memory_space=pltpu.SMEM), vmem],
        out_specs=[vmem, vmem],
        out_shape=[
            jax.ShapeDtypeStruct((utts, channels, lanes), jnp.float32),
            jax.ShapeDtypeStruct((senders, 1, lanes), jnp.float32),
        ],
        name="sums",
    )(counts, parts)


def clip_body(clip_bound, sums, norms, out):
    utts, channels, lanes = sums.shape
    square = jnp.sum(norms[...], axis=0)
    factor = clip_bound / jnp.maximum(jnp.sqrt(square), clip_bound)
    spot = lax.broadcasted_iota(jnp.int32, (1, lanes), 1)
    total = jnp.zeros((channels, lanes), jnp.float32)
    for u in range(utts):
        own = jnp.sum(jnp.where(spot == u, factor, 0.0), axis=1, keepdims=True)
        total = total + own * sums[u]
    wide = jnp.concatenate([total, jnp.zeros((lanes - channels, lanes), jnp.float32)], axis=0).T
    groups, rows, _ = out.shape
    for g in range(groups):
        out[g] = wide[g * rows : (g + 1) * rows]


def clipped(sums, norms, clip_bound, groups):
    vmem = pl.BlockSpec(memory_space=pltpu.VMEM)
    return pl.pallas_call(
        lambda *refs: clip_body(clip_bound, *refs),
        in_specs=[vmem, vmem],
        out_specs=vmem,
        out_shape=jax.ShapeDtypeStruct((groups, 32 // groups, LANES), jnp.float32),
        name="clip",
    )(sums, norms)


def per_device(
    glu_out, cotangent, kernel, conv_bias, out_weight, blocks, last_fill, noise_draws, band_coef
):
    frames, width = glu_out.shape
    blk_count = frames // BLOCK
    shards = lax.axis_size("tm")
    groups = lax.axis_size("utt")
    counts = blocks[0]
    fills = last_fill[0]
    first = (lax.axis_index("tm") * blk_count).astype(jnp.int32).reshape(1)
    full_weight = lax.all_gather(out_weight, "tm", axis=0, tiled=True)
    forward = [(i, i + 1) for i in range(shards - 1)]
    backward = [(target, source) for source, target in forward]
    low = lax.ppermute(glu_out[frames - RIM :], "tm", forward)
    high = lax.ppermute(glu_out[:RIM], "tm", backward)
    hidden, slope, padded = conv(first, counts, fills, glu_out, low, high, kernel, conv_bias[None])
    parts = grads(cotangent, full_weight, slope, padded)
    parts = lax.all_to_all(parts.reshape(shards, width // shards, parts.shape[1]), "tm", 0, 0, tiled=True)
    block_out = jnp.dot(hidden, full_weight, preferred_element_type=jnp.float32).astype(jnp.bfloat16)
    sums, norms = sums_and_norms(counts, parts)
    norms = lax.all_to_all(norms, "tm", 0, 0, tiled=True)
    clip_bound = 300.0 * math.sqrt(width)
    contrib = clipped(sums, norms, clip_bound, groups)
    contrib = lax.all_to_all(contrib, "utt", 0, 0, tiled=True)
    own_share = jnp.sum(contrib, axis=0)[:, : width // shards]
    mixture = jnp.sum(band_coef[:, None, None] * noise_draws, axis=0)
    mean_grad = (own_share + 0.1 * clip_bound * mixture) / (counts.shape[0] * groups)
    return (block_out, mean_grad)


def solution(mesh):
    return jax.shard_map(
        per_device,
        mesh=mesh,
        in_specs=(
            P(("utt", "tm"), None),
            P(("utt", "tm"), None),
            P(),
            P(),
            P("tm", None),
            P("utt", None),
            P("utt", None),
            P(None, "utt", "tm"),
            P(),
        ),
        out_specs=(P(("utt", "tm"), None), P("utt", "tm")),
        check_vma=False,
    )
```

time: 549 us -> 171 us (0.31)
  waiting for transfers between devices: 262 us -> 72.7 us
  other arithmetic: 110 us -> 0.69 us
  blocking collectives: 83.7 us -> 16.8 us
  Pallas kernels: 0 us -> 25.3 us
  loops' own time: 20.7 us -> 0 us
  starting transfers between devices: 5.98 us -> 19.7 us
  local copies, waits for them, and re-layouts: 28 us -> 14.7 us
  matrix products: 19.5 us -> 6.56 us
    unnamed x4 -> x1, waiting for transfers between devices: 200 us -> 0.68 us
    unnamed x2 -> x0, blocking collectives: 83.7 us -> none
    select_n x35 -> x0, other arithmetic: 34.3 us -> none  [the longest x32 34.3 us: hop(): return jax.tree.map(lambda a, b: jnp.where(reached, a, b), new, before)]
    add x3 -> x0, other arithmetic: 33.8 us -> none  [the longest x1 33.8 us: per_device(): conv_out + kernel[tap_idx][None, :] * padded_in[tap_idx:tap_idx + frames]...]
    reduce_sum x8 -> x1, other arithmetic: 32.9 us -> 0.02 us  [per_device(): own_share = jnp.sum(contrib, axis=0)[:, :width // shards]]
    all_gather x1 -> x0, waiting for transfers between devices: 27.4 us -> none  [carried_in(): everything = jax.tree.map(lambda part: lax.all_gather(part, axis), value)]
    all_gather x1, waiting for transfers between devices: 34.8 us -> 60.7 us  [per_device(): full_weight = lax.all_gather(out_weight, 'tm', axis=0, tiled=True)]
    pallas_call x0 -> x4, Pallas kernels: none -> 25.3 us  [the longest x1 10.8 us: grads(): pl.pallas_call(grads_body, grid=(channels // STEP,), in_specs=[pl.BlockSp...]
  transfers between devices with their start and end apart: 5 -> 5, of which waited for: 3 -> 3; matrix products, arithmetic and copies ran while one was open for 10% -> 5% of each run, Pallas kernels for 0% -> 6%
where the time goes in v1:
time: 171 us
  waiting for transfers between devices  72.7 us (43%)
  Pallas kernels  25.3 us (15%)
  starting transfers between devices  19.7 us (12%)
  blocking collectives  16.8 us (10%)
  local copies, waits for them, and re-layouts  14.7 us (9%)
  between operations  14.1 us (8%)
  matrix products  6.56 us (4%)
    all_gather x1, waiting for transfers between devices, per_device(): full_weight = lax.all_gather(out_weight, 'tm', axis=0, tiled=True)  60.7 us
    all_to_all x1, blocking collectives, per_device(): lax.all_to_all(parts.reshape(shards, width // shards, parts.shape[1]), 't...  16.8 us
    unnamed x24, local copies, waits for them, and re-layouts  13.2 us
    pallas_call x1, Pallas kernels, grads(): pl.pallas_call(grads_body, grid=(channels // STEP,), in_specs=[pl.BlockSp...  10.8 us
    all_to_all x1, starting transfers between devices, per_device(): contrib = lax.all_to_all(contrib, 'utt', 0, 0, tiled=True)  10.3 us
    pallas_call x1, Pallas kernels, conv(): pl.pallas_call(conv_body, grid=(width // STEP,), in_specs=[scalars] * 3 +...  10.2 us
    all_to_all x1, waiting for transfers between devices, per_device(): norms = lax.all_to_all(norms, 'tm', 0, 0, tiled=True)  8.49 us
    dot_general x1, matrix products, per_device(): jnp.dot(hidden, full_weight, preferred_element_type=jnp.float32)  6.56 us
  transfers between devices with their start and end apart: 5, of which 3 were waited for; matrix products, arithmetic and copies ran while one was open for 5% of the time, Pallas kernels for 6%

profile of v1, /device:TPU:1, one launch (start us, length us, event | category | flops | bytes accessed | tf_op | source)
XLA Modules:
  0.0 170.5 jit_solution(12857788068232625480)
XLA Ops:
  7.2 0.7 all-gather.2.cloned.1.call-update
  7.9 0.8 fusion
  8.7 3.9 %collective-permute-start = (bf16[16,1536]{1,0:T(8,128)(2,1)S(1)}, bf16[16,1536]{1,0:T(8,128)(2,1)S(1)}, u32[]{:S(2)}, u32[]{:S(2)}) collective-permute-start(bf16[16,1536]{1,0:T(8,128)(2,1)S(1)} %get-tuple-element.13), channel_id=1, source_target_pairs={{0,1},{1,2},{2,3},{3,4},{4,5},{5,6},{6,7},{7,8},{8,9},{9,10},{10,1... | collective-permute-start | bytes 147464 | tf_op jit(solution)/shard_map/ppermute | solution.py:225
  12.7 1.3 collective-permute-start.1
  14.0 0.7 broadcast_in_dim.4.bias
  14.7 2.8 %collective-permute-done.1.high = bf16[16,1536]{1,0:T(8,128)(2,1)S(1)} collective-permute-done((bf16[16,1536]{1,0:T(8,128)(2,1)S(1)}, bf16[16,1536]{1,0:T(8,128)(2,1)S(1)}, u32[]{:S(2)}, u32[]{:S(2)}) %collective-permute-start.1) | collective-permute-done | bytes 49184 | tf_op jit(solution)/shard_map/ppermute | solution.py:226
  17.5 1.4 copy-done.3
  18.9 0.9 copy-done.5
  19.8 0.7 copy-done.6
  21.2 10.2 %conv.1 = (bf16[512,1536]{1,0:T(8,128)(2,1)S(1)}, f32[512,1536]{1,0:T(8,128)S(1)}, f32[12,4,160,128]{3,2,1,0:T(8,128)S(1)}) custom-call(s32[1]{0:T(128)} %bitcast.first, s32[8]{0:T(128)S(1)} %bitcast.8, s32[8]{0:T(128)S(1)} %bitcast.9, bf16[512,1536]{1,0:T(8,128)(2,1)S(1)} %copy-done.3, bf16[16,1536]{1,0:T(8,128)(2,1)S(1)} %collective-permute-done.low, ...), custom_call_target="tpu_custom_call" | custom-call | flops 48758784 | bytes 9437184 | tf_op jit(solution)/shard_map/conv/pallas_call | solution.py:68
  31.4 1.9 %copy-done.1 = f32[12,4,160,128]{3,2,1,0:T(8,128)} copy-done((f32[12,4,160,128]{3,2,1,0:T(8,128)}, f32[12,4,160,128]{3,2,1,0:T(8,128)S(1)}, u32[]{:S(2)}) %copy-start.1) | copy-done | bytes 3932184
  33.3 1.2 copy-done.8
  34.5 60.7 %all-gather.2.cloned.1.call-done.weight = bf16[1536,1536]{1,0:T(8,128)(2,1)} async-done(((bf16[48,1536]{1,0:T(8,128)(2,1)}), bf16[1536,1536]{1,0:T(8,128)(2,1)}) %all-gather.2.cloned.1.call-update) | async-done | bytes 4718608 | tf_op jit(solution)/shard_map/all_gather | solution.py:222
  95.2 2.3 %copy-done = bf16[1536,1536]{1,0:T(8,128)(2,1)S(1)} copy-done((bf16[1536,1536]{1,0:T(8,128)(2,1)S(1)}, bf16[1536,1536]{1,0:T(8,128)(2,1)}, u32[]{:S(2)}) %copy-start) | copy-done | bytes 4718616
  97.5 2.1 %copy-done.2 = f32[12,4,160,128]{3,2,1,0:T(8,128)S(1)} copy-done((f32[12,4,160,128]{3,2,1,0:T(8,128)S(1)}, f32[12,4,160,128]{3,2,1,0:T(8,128)}, u32[]{:S(2)}) %copy-start.2) | copy-done | bytes 3932184
  99.6 1.4 copy-done.4
  101.0 10.8 %grads.1 = bf16[1536,128]{1,0:T(8,128)(2,1)S(1)} custom-call(bf16[512,1536]{1,0:T(8,128)(2,1)S(1)} %copy-done.4, bf16[1536,1536]{1,0:T(8,128)(2,1)S(1)} %copy-done, f32[512,1536]{1,0:T(8,128)S(1)} %get-tuple-element.8.slope, f32[12,4,160,128]{3,2,1,0:T(8,128)S(1)} %copy-done.2), custom_call_target="tpu_custom_call" | custom-call | flops 2415919104 | bytes 9437184 | tf_op jit(solution)/shard_map/grads/pallas_call | solution.py:118
  111.8 16.8 %all_to_all.15.parts = bf16[32,48,128]{2,1,0:T(8,128)(2,1)} all-to-all(bf16[32,48,128]{2,1,0:T(8,128)(2,1)S(1)} %bitcast.6), channel_id=1, replica_groups=mesh['utt'=8,'tm'=32] {'tm'}, dimensions={0} | all-to-all | bytes 786432 | tf_op jit(solution)/shard_map/all_to_all | solution.py:229
  128.6 2.6 %sums.1 = (f32[8,48,128]{2,1,0:T(8,128)}, f32[32,1,128]{2,1,0:T(1,128)}) custom-call(s32[8]{0:T(128)} %bitcast.7, bf16[32,48,128]{2,1,0:T(8,128)(2,1)} %all_to_all.15.parts), custom_call_target="tpu_custom_call" | custom-call | tf_op jit(solution)/shard_map/sums/pallas_call | solution.py:174
  131.2 4.1 %all-to-all-start.1 = ((f32[32,1,128]{2,1,0:T(1,128)}), f32[32,1,128]{2,1,0:T(1,128)S(1)}, u32[]{:S(2)}, u32[]{:S(2)}) async-start(f32[32,1,128]{2,1,0:T(1,128)} %get-tuple-element.11), calls=%async_computation.1 | async-start | bytes 32768 | tf_op jit(solution)/shard_map/all_to_all | solution.py:232
  135.4 8.5 %all-to-all-done.1.refs_1_ = f32[32,1,128]{2,1,0:T(1,128)S(1)} async-done(((f32[32,1,128]{2,1,0:T(1,128)}), f32[32,1,128]{2,1,0:T(1,128)S(1)}, u32[]{:S(2)}, u32[]{:S(2)}) %all-to-all-start.1) | async-done | bytes 16416 | tf_op jit(solution)/shard_map/all_to_all | solution.py:232
  144.4 1.7 %clip.1 = f32[8,4,128]{2,1,0:T(4,128)} custom-call(f32[8,48,128]{2,1,0:T(8,128)} %get-tuple-element.10.refs_0_, f32[32,1,128]{2,1,0:T(1,128)} %copy-done.9), custom_call_target="tpu_custom_call" | custom-call | tf_op jit(solution)/shard_map/clip/pallas_call | solution.py:203
  146.2 10.3 %all-to-all-start.2 = ((f32[8,4,128]{2,1,0:T(4,128)}), f32[8,4,128]{2,1,0:T(4,128)S(1)}, u32[]{:S(2)}, u32[]{:S(2)}) async-start(f32[8,4,128]{2,1,0:T(4,128)} %clip.1), calls=%async_computation.2 | async-start | bytes 32768 | tf_op jit(solution)/shard_map/all_to_all | solution.py:235
  156.5 6.6 %convolution_convert_fusion = bf16[512,1536]{1,0:T(8,128)(2,1)} fusion(bf16[512,1536]{1,0:T(8,128)(2,1)} %copy-done.8, bf16[1536,1536]{1,0:T(8,128)(2,1)} %all-gather.2.cloned.1.call-done.weight), kind=kOutput, calls=%fused_computation | convolution fusion | flops 2416705536 | bytes 7864320 | tf_op jit(solution)/shard_map/dot_general | solution.py:230
  (22 shorter events, 2.0 us)
Async XLA Ops:
  7.2 88.0 %all-gather.2.cloned.1.call-start = ((), (), s32[]{:S(2)}) async-start(), calls=%async_computation.3 | async-start | bytes 4866048 | tf_op jit(solution)/shard_map/all_gather | solution.py:222
  8.7 6.0 %collective-permute-start = (bf16[16,1536]{1,0:T(8,128)(2,1)S(1)}, bf16[16,1536]{1,0:T(8,128)(2,1)S(1)}, u32[]{:S(2)}, u32[]{:S(2)}) collective-permute-start(bf16[16,1536]{1,0:T(8,128)(2,1)S(1)} %get-tuple-element.13), channel_id=1, source_target_pairs={{0,1},{1,2},{2,3},{3,4},{4,5},{5,6},{6,7},{7,8},{8,9},{9,10},{10,1... | collective-permute-start | bytes 147464 | tf_op jit(solution)/shard_map/ppermute | solution.py:225
  12.7 4.8 %collective-permute-start.1 = (bf16[16,1536]{1,0:T(8,128)(2,1)S(1)}, bf16[16,1536]{1,0:T(8,128)(2,1)S(1)}, u32[]{:S(2)}, u32[]{:S(2)}) collective-permute-start(bf16[16,1536]{1,0:T(8,128)(2,1)S(1)} %get-tuple-element.12), channel_id=1, source_target_pairs={{1,0},{2,1},{3,2},{4,3},{5,4},{6,5},{7,6},{8,7},{9,8},{10,9},{11,1... | collective-permute-start | bytes 147464 | tf_op jit(solution)/shard_map/ppermute | solution.py:226
  17.5 1.4 copy-start.3
  18.9 0.9 copy-start.5
  19.8 0.7 copy-start.6
  20.5 0.7 copy-start.7
  31.4 1.9 %copy-start.1 = (f32[12,4,160,128]{3,2,1,0:T(8,128)}, f32[12,4,160,128]{3,2,1,0:T(8,128)S(1)}, u32[]{:S(2)}) copy-start(f32[12,4,160,128]{3,2,1,0:T(8,128)S(1)} %get-tuple-element.9.padded) | copy-start | bytes 11796484
  33.3 1.2 copy-start.8
  95.2 2.3 %copy-start = (bf16[1536,1536]{1,0:T(8,128)(2,1)S(1)}, bf16[1536,1536]{1,0:T(8,128)(2,1)}, u32[]{:S(2)}) copy-start(bf16[1536,1536]{1,0:T(8,128)(2,1)} %all-gather.2.cloned.1.call-done.weight) | copy-start | bytes 14155780
  97.5 2.1 %copy-start.2 = (f32[12,4,160,128]{3,2,1,0:T(8,128)S(1)}, f32[12,4,160,128]{3,2,1,0:T(8,128)}, u32[]{:S(2)}) copy-start(f32[12,4,160,128]{3,2,1,0:T(8,128)} %copy-done.1) | copy-start | bytes 11796484
  99.6 1.4 copy-start.4
  101.0 34.2 %copy-start.10 = (f32[8,4,48]{2,1,0:T(4,128)S(1)}, f32[8,4,48]{2,1,0:T(4,128)}, u32[]{:S(2)}) copy-start(f32[8,4,48]{2,1,0:T(4,128)} %param.16) | copy-start | bytes 18436
  101.0 34.2 %copy-start.11 = (f32[8]{0:T(128)S(1)}, f32[8]{0:T(128)}, u32[]{:S(2)}) copy-start(f32[8]{0:T(128)} %param.17) | copy-start | bytes 100
  131.2 12.7 %all-to-all-start.1 = ((f32[32,1,128]{2,1,0:T(1,128)}), f32[32,1,128]{2,1,0:T(1,128)S(1)}, u32[]{:S(2)}, u32[]{:S(2)}) async-start(f32[32,1,128]{2,1,0:T(1,128)} %get-tuple-element.11), calls=%async_computation.1 | async-start | bytes 32768 | tf_op jit(solution)/shard_map/all_to_all | solution.py:232
  143.9 0.6 copy-start.9
  146.2 16.9 %all-to-all-start.2 = ((f32[8,4,128]{2,1,0:T(4,128)}), f32[8,4,128]{2,1,0:T(4,128)S(1)}, u32[]{:S(2)}, u32[]{:S(2)}) async-start(f32[8,4,128]{2,1,0:T(4,128)} %clip.1), calls=%async_computation.2 | async-start | bytes 32768 | tf_op jit(solution)/shard_map/all_to_all | solution.py:235
Sparse Core Ops, SparseCore 0:
  10.6 84.5 all-gather.1

commit v2 on v1

v2 whole, which is shorter than its diff:
```python
import math

import jax
import jax.numpy as jnp
from jax import lax
from jax.experimental import pallas as pl
from jax.experimental.pallas import tpu as pltpu
from jax.sharding import PartitionSpec as P

BLOCK = 128
LANES = 128
RIM = 16
PADDED = BLOCK + 2 * RIM
STEP = 256
PART = 384
SLOTS = 32
COLS = 4
UTTS = 8


def block_facts(scalars, utts, index):
    utt, limit, cumul = jnp.int32(0), jnp.int32(BLOCK), jnp.int32(0)
    for i in range(utts):
        cumul = cumul + scalars[i]
        utt = utt + (cumul <= index).astype(jnp.int32)
        limit = jnp.where(cumul - 1 == index, scalars[utts + i], limit)
    return utt, limit


def conv_body(
    scalars, x, low, high, kernel, bias, channel, hidden, slope, padded, stacked, picked
):
    taps = kernel.shape[0]
    frames, width = x.shape
    blks = frames // BLOCK

    @pl.when(pl.program_id(0) == 0)
    def _():
        stacked[:frames] = x[...]
        stacked[frames : frames + RIM] = low[...]
        stacked[frames + RIM : frames + 2 * RIM] = high[...]
        rest = jnp.concatenate([kernel[...], bias[...]], axis=0)
        for part in range(3):
            rounded = rest.astype(jnp.bfloat16)
            at = frames + 2 * RIM + part * (taps + 1)
            stacked[at : at + taps + 1] = rounded
            rest = rest - rounded.astype(jnp.float32)

    chosen = lax.broadcasted_iota(jnp.int32, (width, STEP), 0) == channel[...]
    picked[...] = jnp.dot(
        stacked[...],
        jnp.where(chosen, 1.0, 0.0).astype(jnp.bfloat16),
        preferred_element_type=jnp.float32,
    )
    first = scalars[2 * UTTS]
    facts = [block_facts(scalars, UTTS, first + b) for b in range(-1, blks + 1)]
    row = lax.broadcasted_iota(jnp.int32, (BLOCK, LANES), 0)
    rim_row = lax.broadcasted_iota(jnp.int32, (RIM, LANES), 0)
    for tile in range(STEP // LANES):
        lanes = slice(tile * LANES, (tile + 1) * LANES)
        at = frames + 2 * RIM
        weights = picked[at : at + taps + 1, lanes]
        for part in range(1, 3):
            at = at + taps + 1
            weights = weights + picked[at : at + taps + 1, lanes]
        for b in range(blks):
            utt, limit = facts[b + 1]
            before = (facts[b][0] == utt) & (first + b > 0)
            after = facts[b + 2][0] == utt
            keep = row < limit
            at = b * BLOCK
            here = picked[at : at + BLOCK, lanes]
            left = at - RIM if b else frames
            right = at + BLOCK if b < blks - 1 else frames + RIM
            padded[tile, b, :RIM] = jnp.where(
                rim_row < jnp.where(before, RIM, 0), picked[left : left + RIM, lanes], 0.0
            )
            padded[tile, b, RIM : RIM + BLOCK] = jnp.where(keep, here, 0.0)
            padded[tile, b, RIM + BLOCK :] = jnp.where(
                rim_row < jnp.where(after, facts[b + 2][1], 0),
                picked[right : right + RIM, lanes],
                0.0,
            )
            total = jnp.broadcast_to(weights[taps : taps + 1], (BLOCK, LANES))
            for k in range(taps):
                total = total + weights[k : k + 1] * padded[tile, b, k + 1 : k + 1 + BLOCK]
            logistic = jax.nn.sigmoid(total)
            rows = slice(at, at + BLOCK)
            hidden[rows, lanes] = jnp.where(keep, total * logistic, 0.0).astype(jnp.bfloat16)
            slope[rows, lanes] = jnp.where(
                keep, logistic * (1.0 + total * (1.0 - logistic)), 0.0
            )


def conv(scalars, x, low, high, kernel, bias, channel):
    frames, width = x.shape
    blks = frames // BLOCK
    stacked = frames + 2 * RIM + 3 * (kernel.shape[0] + 1)
    whole = lambda rows: pl.BlockSpec((rows, width), lambda c: (0, 0))
    column = lambda rows: pl.BlockSpec((rows, STEP), lambda c: (0, c))
    return pl.pallas_call(
        conv_body,
        grid=(width // STEP,),
        in_specs=[
            pl.BlockSpec(memory_space=pltpu.SMEM),
            whole(frames),
            whole(RIM),
            whole(RIM),
            whole(kernel.shape[0]),
            whole(1),
            column(1),
        ],
        out_specs=[
            column(frames),
            column(frames),
            pl.BlockSpec((STEP // LANES, blks, PADDED, LANES), lambda c: (c, 0, 0, 0)),
        ],
        out_shape=[
            jax.ShapeDtypeStruct((frames, width), jnp.bfloat16),
            jax.ShapeDtypeStruct((frames, width), jnp.float32),
            jax.ShapeDtypeStruct((width // LANES, blks, PADDED, LANES), jnp.float32),
        ],
        scratch_shapes=[
            pltpu.VMEM((stacked, width), jnp.bfloat16),
            pltpu.VMEM((stacked, STEP), jnp.float32),
        ],
        compiler_params=pltpu.CompilerParams(vmem_limit_bytes=24 << 20),
        cost_estimate=pl.CostEstimate(
            flops=2 * stacked * width * width, bytes_accessed=40 * frames * width, transcendentals=frames * width
        ),
        name="conv",
    )(scalars, x, low, high, kernel, bias, channel)


def tap_sums(own, padded, tile, b, parts):
    for k in range(SLOTS):
        term = own * padded[tile, b, k + 1 : k + 1 + BLOCK] if k < SLOTS - 1 else own
        at = (b * SLOTS + k) * 8
        parts[at : at + 8] = jnp.sum(term.reshape(BLOCK // 8, 8, LANES), axis=0)


def part_grads(cot, slope, padded, weight, grad, parts, store):
    blks = padded.shape[1]
    hidden_grad = lax.dot_general(
        cot[...], weight[...], (((1,), (1,)), ((), ())), preferred_element_type=jnp.float32
    )
    for tile in range(PART // LANES):
        lanes = slice(tile * LANES, (tile + 1) * LANES)
        grad[tile] = hidden_grad[:, lanes] * slope[:, lanes]
    for tile in range(PART // LANES):
        for b in range(blks):
            tap_sums(grad[tile, b * BLOCK : (b + 1) * BLOCK], padded, tile, b, parts)
        total = parts[pl.ds(0, blks * SLOTS, stride=8)]
        for s in range(1, 8):
            total = total + parts[pl.ds(s, blks * SLOTS, stride=8)]
        store(tile, total.T)


def early_body(pieces, cot, slope, padded, *rest):
    rows, out, weight, grad, parts = rest[:-4], rest[-4], rest[-3], rest[-2], rest[-1]
    per = len(rows) // pieces
    for step in range(pieces):

        @pl.when(pl.program_id(0) == step)
        def _():
            at = 0
            for piece in rows[step * per : (step + 1) * per]:
                weight[at : at + piece.shape[0]] = piece[...]
                at = at + piece.shape[0]

    def store(tile, value):
        out[tile * LANES : (tile + 1) * LANES] = value

    part_grads(cot, slope, padded, weight, grad, parts, store)


def last_body(scalars, early, middle, cot, slope, padded, *rest):
    rows, out, late, weight, grad, parts = rest[:-5], rest[-5], rest[-4], rest[-3], rest[-2], rest[-1]
    at = 0
    for piece in rows:
        weight[at : at + piece.shape[0]] = piece[...]
        at = at + piece.shape[0]

    def store(tile, value):
        late[tile * LANES : (tile + 1) * LANES] = value

    part_grads(cot, slope, padded, weight, grad, parts, store)
    col, core = scalars[2 * UTTS + 1], scalars[2 * UTTS + 2]
    half = PART // 2
    share = out.shape[1] // 2
    depth = half // share
    for ref, base, shift in ((early, 0, 0), (middle, 0, COLS - 1), (middle, PART, 1), (late, 0, 2)):
        target = lax.rem(col + shift, COLS)
        for z in range(depth):
            mine = ref[base + z * share : base + (z + 1) * share]
            other = ref[base + half + z * share : base + half + (z + 1) * share]
            is_first = core == 0
            both = jnp.concatenate(
                [jnp.where(is_first, mine, other), jnp.where(is_first, other, mine)], axis=0
            )
            out[z * COLS + target] = both.astype(out.dtype)


def grad_scratch(frames, width, blks):
    return [
        pltpu.VMEM((PART, width), jnp.bfloat16),
        pltpu.VMEM((PART // LANES, frames, LANES), jnp.float32),
        pltpu.VMEM((blks * SLOTS * 8, LANES), jnp.float32),
    ]


def grad_cost(frames, width, channels):
    return pl.CostEstimate(
        flops=2 * frames * width * channels, bytes_accessed=20 * frames * channels, transcendentals=0
    )


def early_grads(cot, slope, padded, rows, start):
    frames, width = cot.shape
    blks = frames // BLOCK
    channels = sum(piece.shape[0] for piece in rows)
    steps = channels // PART
    return pl.pallas_call(
        lambda *refs: early_body(steps, *refs),
        grid=(steps,),
        in_specs=[
            pl.BlockSpec((frames, width), lambda c: (0, 0)),
            pl.BlockSpec((frames, PART), lambda c: (0, c + start)),
            pl.BlockSpec((PART // LANES, blks, PADDED, LANES), lambda c: (c + start, 0, 0, 0)),
        ]
        + [pl.BlockSpec(piece.shape, lambda c: (0, 0)) for piece in rows],
        out_specs=pl.BlockSpec((PART, blks * SLOTS), lambda c: (c, 0)),
        out_shape=jax.ShapeDtypeStruct((channels, blks * SLOTS), jnp.float32),
        scratch_shapes=grad_scratch(frames, width, blks),
        compiler_params=pltpu.CompilerParams(vmem_limit_bytes=24 << 20),
        cost_estimate=grad_cost(frames, width, channels),
        name="grads",
    )(cot, slope, padded, *rows)


def last_grads(scalars, early, middle, cot, slope, padded, rows, start, shards):
    frames, width = cot.shape
    blks = frames // BLOCK
    channels = sum(piece.shape[0] for piece in rows)
    return pl.pallas_call(
        last_body,
        grid=(1,),
        in_specs=[
            pl.BlockSpec(memory_space=pltpu.SMEM),
            pl.BlockSpec(early.shape, lambda c: (0, 0)),
            pl.BlockSpec(middle.shape, lambda c: (0, 0)),
            pl.BlockSpec((frames, width), lambda c: (0, 0)),
            pl.BlockSpec((frames, PART), lambda c: (0, start)),
            pl.BlockSpec((PART // LANES, blks, PADDED, LANES), lambda c: (start, 0, 0, 0)),
        ]
        + [pl.BlockSpec(piece.shape, lambda c: (0, 0)) for piece in rows],
        out_specs=pl.BlockSpec((shards, width // shards, blks * SLOTS), lambda c: (0, 0, 0)),
        out_shape=jax.ShapeDtypeStruct((shards, width // shards, blks * SLOTS), jnp.bfloat16),
        scratch_shapes=[pltpu.VMEM((PART, blks * SLOTS), jnp.float32)]
        + grad_scratch(frames, width, blks),
        compiler_params=pltpu.CompilerParams(vmem_limit_bytes=24 << 20),
        cost_estimate=grad_cost(frames, width, channels),
        name="last_grads",
    )(scalars, early, middle, cot, slope, padded, *rows)


def project_body(hidden, *rest):
    rows, out, weight = rest[:-2], rest[-2], rest[-1]

    @pl.when(pl.program_id(0) == 0)
    def _():
        at = 0
        for piece in rows:
            weight[at : at + piece.shape[0]] = piece[...]
            at = at + piece.shape[0]

    step = out.shape[1]
    lanes = pl.ds(pl.multiple_of(pl.program_id(0) * step, step), step)
    out[...] = jnp.dot(
        hidden[...], weight[:, lanes], preferred_element_type=jnp.float32
    ).astype(out.dtype)


def project(hidden, rows):
    frames, width = hidden.shape
    step = 512
    return pl.pallas_call(
        project_body,
        grid=(width // step,),
        in_specs=[pl.BlockSpec(hidden.shape, lambda c: (0, 0))]
        + [pl.BlockSpec(piece.shape, lambda c: (0, 0), pipeline_mode=pl.Buffered(1)) for piece in rows],
        out_specs=pl.BlockSpec((frames, step), lambda c: (0, c)),
        out_shape=jax.ShapeDtypeStruct((frames, width), jnp.bfloat16),
        scratch_shapes=[pltpu.VMEM((width, width), jnp.bfloat16)],
        compiler_params=pltpu.CompilerParams(vmem_limit_bytes=28 << 20),
        cost_estimate=pl.CostEstimate(
            flops=2 * frames * width * width, bytes_accessed=2 * width * width + 4 * frames * width, transcendentals=0
        ),
        name="project",
    )(hidden, *rows)


def sums_body(scalars, parts, sums, norms):
    senders, channels, lanes = parts.shape
    utts = UTTS
    per = lanes // SLOTS
    blk = lax.broadcasted_iota(jnp.int32, (senders, lanes), 0) * per + (
        lax.broadcasted_iota(jnp.int32, (senders, lanes), 1) // SLOTS
    )
    utt_of, cumul = jnp.zeros((senders, lanes), jnp.int32), jnp.int32(0)
    for i in range(utts):
        cumul = cumul + scalars[i]
        utt_of = utt_of + (cumul <= blk).astype(jnp.int32)
    spot = lax.broadcasted_iota(jnp.int32, (1, lanes), 1)
    row = jnp.zeros((1, lanes), jnp.float32)
    totals = [jnp.zeros((channels, lanes), jnp.float32) for _ in range(utts)]
    for s in range(senders):
        part = parts[s].astype(jnp.float32)
        owner = utt_of[s : s + 1]
        for u in range(utts):
            totals[u] = totals[u] + jnp.where(owner == u, part, 0.0)
    for u in range(utts):
        total = totals[u]
        total = total + pltpu.roll(total, 64, 1)
        total = total + pltpu.roll(total, 32, 1)
        sums[u] = total
        square = jnp.sum(jnp.sum(total * total, axis=0, keepdims=True), axis=1, keepdims=True)
        row = row + jnp.where(spot == u, square * (1.0 / per), 0.0)
    norms[...] = jnp.broadcast_to(row[None], norms.shape)


def sums_and_norms(scalars, parts):
    senders, channels, lanes = parts.shape
    utts = UTTS
    vmem = pl.BlockSpec(memory_space=pltpu.VMEM)
    return pl.pallas_call(
        sums_body,
        in_specs=[pl.BlockSpec(memory_space=pltpu.SMEM), vmem],
        out_specs=[vmem, vmem],
        out_shape=[
            jax.ShapeDtypeStruct((utts, channels, lanes), jnp.float32),
            jax.ShapeDtypeStruct((senders, 1, lanes), jnp.float32),
        ],
        name="sums",
    )(scalars, parts)


def clip_body(clip_bound, sums, norms, out):
    utts, channels, lanes = sums.shape
    square = jnp.sum(norms[...], axis=0)
    factor = clip_bound / jnp.maximum(jnp.sqrt(square), clip_bound)
    spot = lax.broadcasted_iota(jnp.int32, (1, lanes), 1)
    total = jnp.zeros((channels, lanes), jnp.float32)
    for u in range(utts):
        own = jnp.sum(jnp.where(spot == u, factor, 0.0), axis=1, keepdims=True)
        total = total + own * sums[u]
    wide = jnp.concatenate([total, jnp.zeros((lanes - channels, lanes), jnp.float32)], axis=0).T
    groups, rows, _ = out.shape
    for g in range(groups):
        out[g] = wide[g * rows : (g + 1) * rows]


def clipped(sums, norms, clip_bound, groups):
    vmem = pl.BlockSpec(memory_space=pltpu.VMEM)
    return pl.pallas_call(
        lambda *refs: clip_body(clip_bound, *refs),
        in_specs=[vmem, vmem],
        out_specs=vmem,
        out_shape=jax.ShapeDtypeStruct((groups, SLOTS // groups, LANES), jnp.float32),
        name="clip",
    )(sums, norms)


def gathered_rows(out_weight, core, shards, groups):
    depth = shards // COLS
    half = out_weight.shape[0] // 2
    width = out_weight.shape[1]
    mate = [(i, i ^ 1) for i in range(groups)]

    def shifted(value, by):
        pairs = [(z * COLS + x, z * COLS + (x + by) % COLS) for z in range(depth) for x in range(COLS)]
        return lax.ppermute(value, "tm", pairs)

    def swapped(value):
        return lax.ppermute(value, "utt", mate)

    def flat(value):
        return value.reshape(-1, width)

    own = lax.dynamic_slice_in_dim(out_weight, core * half, half, axis=0)
    own = lax.all_to_all(
        jnp.broadcast_to(own[None], (depth, half, width)),
        "tm",
        0,
        0,
        axis_index_groups=[[z * COLS + x for z in range(depth)] for x in range(COLS)],
        tiled=True,
    )
    below, above = shifted(own, 1), shifted(own, -1)
    own_mate = swapped(own)
    far_low, far_high = shifted(below[: depth // 2], 1), shifted(above[depth // 2 :], -1)
    below_mate, above_mate = swapped(below), swapped(above)
    far_low_mate, far_high_mate = swapped(far_low), swapped(far_high)
    return (
        [flat(own), flat(own_mate)],
        [flat(below), flat(below_mate), flat(above), flat(above_mate)],
        [flat(far_low), flat(far_high), flat(far_low_mate), flat(far_high_mate)],
    )


def arrival_channels(col, core, shards, width):
    depth = shards // COLS
    half = width // shards // 2
    place = jnp.arange(width, dtype=jnp.int32)
    inner = place % half
    z = place // half % depth
    mate = place // (half * depth) % 2
    side = place // (half * depth * 2)
    shift = jnp.where(side == 1, COLS - 1, jnp.where(side == 2, 1, jnp.where(side == 3, 2, 0)))
    x = (col + shift) % COLS
    return ((z * COLS + x) * 2 + (core ^ mate)) * half + inner


def per_device(
    glu_out, cotangent, kernel, conv_bias, out_weight, blocks, last_fill, noise_draws, band_coef
):
    frames, width = glu_out.shape
    blk_count = frames // BLOCK
    shards = lax.axis_size("tm")
    groups = lax.axis_size("utt")
    device = lax.axis_index("tm").astype(jnp.int32)
    core = lax.axis_index("utt").astype(jnp.int32) % 2
    col = device % COLS
    scalars = jnp.concatenate(
        [blocks[0], last_fill[0], jnp.stack([device * blk_count, col, core])]
    )
    near, sides, far = gathered_rows(out_weight, core, shards, groups)
    forward = [(i, i + 1) for i in range(shards - 1)]
    backward = [(target, source) for source, target in forward]
    low = lax.ppermute(glu_out[frames - RIM :], "tm", forward)
    high = lax.ppermute(glu_out[:RIM], "tm", backward)
    channel = arrival_channels(col, core, shards, width)[None]
    hidden, slope, padded = conv(scalars, glu_out, low, high, kernel, conv_bias[None], channel)
    early = early_grads(cotangent, slope, padded, near, 0)
    middle = early_grads(cotangent, slope, padded, sides, 1)
    parts = last_grads(scalars, early, middle, cotangent, slope, padded, far, 3, shards)
    parts = lax.all_to_all(parts, "tm", 0, 0, tiled=True)
    block_out = project(hidden, near + sides + far)
    sums, norms = sums_and_norms(scalars, parts)
    norms = lax.all_to_all(norms, "tm", 0, 0, tiled=True)
    clip_bound = 300.0 * math.sqrt(width)
    contrib = clipped(sums, norms, clip_bound, groups)
    contrib = lax.all_to_all(contrib, "utt", 0, 0, tiled=True)
    own_share = jnp.sum(contrib, axis=0)[:, : width // shards]
    mixture = jnp.sum(band_coef[:, None, None] * noise_draws, axis=0)
    mean_grad = (own_share + 0.1 * clip_bound * mixture) / (UTTS * groups)
    return (block_out, mean_grad)


def solution(mesh):
    return jax.shard_map(
        per_device,
        mesh=mesh,
        in_specs=(
            P(("utt", "tm"), None),
            P(("utt", "tm"), None),
            P(),
            P(),
            P("tm", None),
            P("utt", None),
            P("utt", None),
            P(None, "utt", "tm"),
            P(),
        ),
        out_specs=(P(("utt", "tm"), None), P("utt", "tm")),
        check_vma=False,
    )
```

time: 171 us -> 144 us (0.84)
  waiting for transfers between devices: 72.7 us -> 12.4 us
  blocking collectives: 16.8 us -> 48.6 us
  Pallas kernels: 25.3 us -> 39.7 us
  between operations: 14.1 us -> 0.93 us
  starting transfers between devices: 19.7 us -> 31.3 us
  matrix products: 6.56 us -> 0 us
  local copies, waits for them, and re-layouts: 14.7 us -> 9.65 us
    all_gather x1 -> x0, waiting for transfers between devices: 60.7 us -> none  [per_device(): full_weight = lax.all_gather(out_weight, 'tm', axis=0, tiled=True)]
    all_to_all x1 -> x2, blocking collectives: 16.8 us -> 48.6 us  [the longest x1 26.2 us: gathered_rows(): lax.all_to_all(jnp.broadcast_to(own[None], (depth, half, width)), 'tm', 0...]
    ppermute x0 -> x9, starting transfers between devices: none -> 16.6 us  [the longest x5 11.2 us: swapped(): return lax.ppermute(value, 'utt', mate)]
    pallas_call x2 -> x5, Pallas kernels: 21 us -> 35.4 us  [the longest x1 16.6 us: conv(): pl.pallas_call(conv_body, grid=(width // STEP,), in_specs=[pl.BlockSpec(m...]
    dot_general x1 -> x0, matrix products: 6.56 us -> none  [per_device(): jnp.dot(hidden, full_weight, preferred_element_type=jnp.float32)]
    unnamed x24 -> x34, local copies, waits for them, and re-layouts: 13.2 us -> 7.21 us
    ppermute x0 -> x9, waiting for transfers between devices: none -> 3.95 us  [the longest x4 3.93 us: shifted(): return lax.ppermute(value, 'tm', pairs)]
    all_to_all x1, starting transfers between devices: 10.3 us -> 7.1 us  [per_device(): contrib = lax.all_to_all(contrib, 'utt', 0, 0, tiled=True)]
  transfers between devices with their start and end apart: 5 -> 13, of which waited for: 3 -> 2; matrix products, arithmetic and copies ran while one was open for 5% -> 2% of each run, Pallas kernels for 6% -> 22%
where the time goes in v2:
time: 144 us; the launch traced here: 143 us
  blocking collectives  48.6 us (34%)
  Pallas kernels  39.7 us (28%)
  starting transfers between devices  31.3 us (22%)
  waiting for transfers between devices  12.4 us (9%)
  local copies, waits for them, and re-layouts  9.65 us (7%)
    all_to_all x1, blocking collectives, gathered_rows(): lax.all_to_all(jnp.broadcast_to(own[None], (depth, half, width)), 'tm', 0...  26.2 us
    all_to_all x1, blocking collectives, per_device(): parts = lax.all_to_all(parts, 'tm', 0, 0, tiled=True)  22.4 us
    pallas_call x1, Pallas kernels, conv(): pl.pallas_call(conv_body, grid=(width // STEP,), in_specs=[pl.BlockSpec(m...  16.6 us
    ppermute x5, starting transfers between devices, swapped(): return lax.ppermute(value, 'utt', mate)  11.2 us
    pallas_call x2, Pallas kernels, early_grads(): pl.pallas_call(lambda *refs: early_body(steps, *refs), grid=(steps,), in_...  9.63 us
    all_to_all x1, waiting for transfers between devices, per_device(): norms = lax.all_to_all(norms, 'tm', 0, 0, tiled=True)  8.49 us
    unnamed x34, local copies, waits for them, and re-layouts  7.21 us
    all_to_all x1, starting transfers between devices, per_device(): contrib = lax.all_to_all(contrib, 'utt', 0, 0, tiled=True)  7.1 us
  transfers between devices with their start and end apart: 13, of which 2 were waited for; matrix products, arithmetic and copies ran while one was open for 2% of the time, Pallas kernels for 22%

profile of v2, /device:TPU:1, one launch (start us, length us, event | category | flops | bytes accessed | tf_op | source)
XLA Modules:
  0.0 143.4 jit_solution(4817919118150358584)
XLA Ops:
  1.6 26.2 %all_to_all.20 = bf16[8,24,1536]{2,1,0:T(8,128)(2,1)S(1)} all-to-all(bf16[8,24,1536]{2,1,0:T(8,128)(2,1)S(1)} %broadcast_in_dim.22), channel_id=1, replica_groups={{0,4,8,12,16,20,24,28},{1,5,9,13,17,21,25,29},{2,6,10,14,18,22,26,30},{..., dimensions={0} | all-to-all | bytes 1179648 | tf_op jit(solution)/shard_map/all_to_all | solution.py:391
  27.9 1.2 collective-permute-start.3
  29.1 1.5 %collective-permute-start.5 = (bf16[8,24,1536]{2,1,0:T(8,128)(2,1)S(1)}, bf16[8,24,1536]{2,1,0:T(8,128)(2,1)S(1)}, u32[]{:S(2)}, u32[]{:S(2)}) collective-permute-start(bf16[8,24,1536]{2,1,0:T(8,128)(2,1)S(1)} %all_to_all.20), channel_id=1, source_target_pairs={{0,3},{1,0},{2,1},{3,2},{4,7},{5,4},{6,5},{7,6},{8,11},{9,8},{10,9... | collective-permute-start | bytes 1769480 | tf_op jit(solution)/shard_map/ppermute | solution.py:382
  30.6 3.0 %collective-permute-start.2 = (bf16[8,24,1536]{2,1,0:T(8,128)(2,1)S(1)}, bf16[8,24,1536]{2,1,0:T(8,128)(2,1)S(1)}, u32[]{:S(2)}, u32[]{:S(2)}) collective-permute-start(bf16[8,24,1536]{2,1,0:T(8,128)(2,1)S(1)} %all_to_all.20), channel_id=1, source_target_pairs={{0,32},{32,0},{64,96},{96,64},{128,160},{160,128},{192,224},{224,1... | collective-permute-start | bytes 1769480 | tf_op jit(solution)/shard_map/ppermute | solution.py:385
  34.4 1.9 %collective-permute-start = (bf16[16,1536]{1,0:T(8,128)(2,1)S(1)}, bf16[16,1536]{1,0:T(8,128)(2,1)S(1)}, u32[]{:S(2)}, u32[]{:S(2)}) collective-permute-start(bf16[16,1536]{1,0:T(8,128)(2,1)S(1)} %get-tuple-element.13), channel_id=1, source_target_pairs={{0,1},{1,2},{2,3},{3,4},{4,5},{5,6},{6,7},{7,8},{8,9},{9,10},{10,1... | collective-permute-start | bytes 147464 | tf_op jit(solution)/shard_map/ppermute | solution.py:440
  36.3 1.3 collective-permute-start.1
  37.6 3.9 %collective-permute-done.3 = bf16[8,24,1536]{2,1,0:T(8,128)(2,1)S(1)} collective-permute-done((bf16[8,24,1536]{2,1,0:T(8,128)(2,1)S(1)}, bf16[8,24,1536]{2,1,0:T(8,128)(2,1)S(1)}, u32[]{:S(2)}, u32[]{:S(2)}) %collective-permute-start.3) | collective-permute-done | bytes 589856 | tf_op jit(solution)/shard_map/ppermute | solution.py:382
  43.0 2.7 %collective-permute-start.8 = (bf16[4,24,1536]{2,1,0:T(8,128)(2,1)}, bf16[4,24,1536]{2,1,0:T(8,128)(2,1)}, u32[]{:S(2)}, u32[]{:S(2)}) collective-permute-start(bf16[4,24,1536]{2,1,0:T(8,128)(2,1)} %slice.21), channel_id=1, source_target_pairs={{0,3},{1,0},{2,1},{3,2},{4,7},{5,4},{6,5},{7,6},{8,11},{9,8},{10,9... | collective-permute-start | bytes 884744 | tf_op jit(solution)/shard_map/ppermute | solution.py:382
  45.6 3.9 %collective-permute-start.6 = (bf16[8,24,1536]{2,1,0:T(8,128)(2,1)S(1)}, bf16[8,24,1536]{2,1,0:T(8,128)(2,1)S(1)}, u32[]{:S(2)}, u32[]{:S(2)}) collective-permute-start(bf16[8,24,1536]{2,1,0:T(8,128)(2,1)S(1)} %collective-permute-done.5), channel_id=1, source_target_pairs={{0,32},{32,0},{64,96},{96,64},{128,160},{160,128},{192,224},{224,1... | collective-permute-start | bytes 1769480 | tf_op jit(solution)/shard_map/ppermute | solution.py:385
  49.9 3.8 %collective-permute-start.9 = (bf16[4,24,1536]{2,1,0:T(8,128)(2,1)S(1)}, bf16[4,24,1536]{2,1,0:T(8,128)(2,1)S(1)}, u32[]{:S(2)}, u32[]{:S(2)}) collective-permute-start(bf16[4,24,1536]{2,1,0:T(8,128)(2,1)S(1)} %collective-permute-done.7), channel_id=1, source_target_pairs={{0,32},{32,0},{64,96},{96,64},{128,160},{160,128},{192,224},{224,1... | collective-permute-start | bytes 884744 | tf_op jit(solution)/shard_map/ppermute | solution.py:385
  54.2 1.4 copy-done.6
  56.5 16.6 %conv.1 = (bf16[512,1536]{1,0:T(8,128)(2,1)S(1)}, f32[512,1536]{1,0:T(8,128)S(1)}, f32[12,4,160,128]{3,2,1,0:T(8,128)S(1)}) custom-call(s32[19]{0:T(128)S(1)} %concatenate.3.scalars, bf16[512,1536]{1,0:T(8,128)(2,1)S(1)} %copy-done.6, bf16[16,1536]{1,0:T(8,128)(2,1)S(1)} %collective-permute-done.low, bf16[16,1536]{1,0:T(8,128)(2,1)S(1)} %collective-permute-done.1.high, ...), custom_call_target="tpu_custom_call" | custom-call | flops 3019898880 | bytes 31457280 | tf_op jit(solution)/shard_map/conv/pallas_call | solution.py:101
  73.1 2.8 %grads.2.early = f32[384,128]{1,0:T(8,128)S(1)} custom-call(bf16[512,1536]{1,0:T(8,128)(2,1)S(1)} %copy-done.1, f32[512,1536]{1,0:T(8,128)S(1)} %get-tuple-element.8.refs_1_.slope, f32[12,4,160,128]{3,2,1,0:T(8,128)S(1)} %get-tuple-element.9.refs_2_.padded, bf16[192,1536]{1,0:T(8,128)(2,1)S(1)} %bitcast.15, bf16[192,1536]{1,0:T(8,128)(2,1)S(1)} %bitcast.21), custom_call_target="tpu_custom_call" | custom-call | flops 603979776 | bytes 3932160 | tf_op jit(solution)/shard_map/grads/pallas_call | solution.py:223
  75.9 6.9 %grads.3.middle = f32[768,128]{1,0:T(8,128)S(1)} custom-call(bf16[512,1536]{1,0:T(8,128)(2,1)S(1)} %copy-done.1, f32[512,1536]{1,0:T(8,128)S(1)} %get-tuple-element.8.refs_1_.slope, f32[12,4,160,128]{3,2,1,0:T(8,128)S(1)} %get-tuple-element.9.refs_2_.padded, bf16[192,1536]{1,0:T(8,128)(2,1)S(1)} %bitcast.17, bf16[192,1536]{1,0:T(8,128)(2,1)} %bitcast.8.rest_3_.refs_4_, ...), custom_call_target="tpu_custom_call" | custom-call | flops 1207959552 | bytes 7864320 | tf_op jit(solution)/shard_map/grads/pallas_call | solution.py:223
  82.9 3.9 %last_grads.1 = bf16[32,48,128]{2,1,0:T(8,128)(2,1)S(1)} custom-call(s32[19]{0:T(128)S(1)} %concatenate.3.scalars, f32[384,128]{1,0:T(8,128)S(1)} %grads.2.early, f32[768,128]{1,0:T(8,128)S(1)} %grads.3.middle, bf16[512,1536]{1,0:T(8,128)(2,1)S(1)} %copy-done.1, f32[512,1536]{1,0:T(8,128)S(1)} %get-tuple-element.8.refs_1_.slope, ...), custom_call_target="tpu_custom_call" | custom-call | flops 603979776 | bytes 3932160 | tf_op jit(solution)/shard_map/last_grads/pallas_call | solution.py:245
  86.8 22.4 %all_to_all.21.parts = bf16[32,48,128]{2,1,0:T(8,128)(2,1)} all-to-all(bf16[32,48,128]{2,1,0:T(8,128)(2,1)S(1)} %last_grads.1), channel_id=1, replica_groups=mesh['utt'=8,'tm'=32] {'tm'}, dimensions={0} | all-to-all | bytes 786432 | tf_op jit(solution)/shard_map/all_to_all | solution.py:447
  109.2 2.6 %sums.1 = (f32[8,48,128]{2,1,0:T(8,128)}, f32[32,1,128]{2,1,0:T(1,128)}) custom-call(s32[19]{0:T(128)} %copy-done.7, bf16[32,48,128]{2,1,0:T(8,128)(2,1)} %all_to_all.21.parts), custom_call_target="tpu_custom_call" | custom-call | tf_op jit(solution)/shard_map/sums/pallas_call | solution.py:336
  111.8 4.4 %all-to-all-start.2 = ((f32[32,1,128]{2,1,0:T(1,128)}), f32[32,1,128]{2,1,0:T(1,128)S(1)}, u32[]{:S(2)}, u32[]{:S(2)}) async-start(f32[32,1,128]{2,1,0:T(1,128)} %get-tuple-element.11), calls=%async_computation.2 | async-start | bytes 32768 | tf_op jit(solution)/shard_map/all_to_all | solution.py:450
  116.3 8.5 %all-to-all-done.2.refs_1_ = f32[32,1,128]{2,1,0:T(1,128)S(1)} async-done(((f32[32,1,128]{2,1,0:T(1,128)}), f32[32,1,128]{2,1,0:T(1,128)S(1)}, u32[]{:S(2)}, u32[]{:S(2)}) %all-to-all-start.2) | async-done | bytes 16416 | tf_op jit(solution)/shard_map/all_to_all | solution.py:450
  125.4 1.7 %clip.1 = f32[8,4,128]{2,1,0:T(4,128)} custom-call(f32[8,48,128]{2,1,0:T(8,128)} %get-tuple-element.10.refs_0_, f32[32,1,128]{2,1,0:T(1,128)} %copy-done.11), custom_call_target="tpu_custom_call" | custom-call | tf_op jit(solution)/shard_map/clip/pallas_call | solution.py:365
  127.1 7.1 %all-to-all-start.3 = ((f32[8,4,128]{2,1,0:T(4,128)}), f32[8,4,128]{2,1,0:T(4,128)S(1)}, u32[]{:S(2)}, u32[]{:S(2)}) async-start(f32[8,4,128]{2,1,0:T(4,128)} %clip.1), calls=%async_computation.3 | async-start | bytes 32768 | tf_op jit(solution)/shard_map/all_to_all | solution.py:453
  134.2 1.0 copy-done.3
  136.2 1.4 copy-done.10
  137.6 5.2 %project.1 = bf16[512,1536]{1,0:T(8,128)(2,1)} custom-call(bf16[512,1536]{1,0:T(8,128)(2,1)S(1)} %copy-done.10, bf16[192,1536]{1,0:T(8,128)(2,1)S(1)} %bitcast.16, bf16[192,1536]{1,0:T(8,128)(2,1)S(1)} %bitcast.22, bf16[192,1536]{1,0:T(8,128)(2,1)S(1)} %bitcast.18, bf16[192,1536]{1,0:T(8,128)(2,1)} %bitcast.8.rest_3_.refs_4_, ...), custom_call_target="tpu_custom_call" | custom-call | flops 2415919104 | bytes 7864320 | tf_op jit(solution)/shard_map/project/pallas_call | solution.py:287
  (56 shorter events, 7.2 us)
Async XLA Ops:
  1.6 48.1 %copy-start.13 = (f32[1536]{0:T(1024)S(1)}, f32[1536]{0:T(1024)}, u32[]{:S(2)}) copy-start(f32[1536]{0:T(1024)} %param.12) | copy-start | bytes 18436
  1.6 48.1 %copy-start.15 = (s32[1,8]{1,0:T(1,128)S(1)}, s32[1,8]{1,0:T(1,128)}, u32[]{:S(2)}) copy-start(s32[1,8]{1,0:T(1,128)} %param.14) | copy-start | bytes 100
  1.6 48.1 %copy-start.16 = (s32[1,8]{1,0:T(1,128)S(1)}, s32[1,8]{1,0:T(1,128)}, u32[]{:S(2)}) copy-start(s32[1,8]{1,0:T(1,128)} %param.15) | copy-start | bytes 100
  27.9 13.6 %collective-permute-start.3 = (bf16[8,24,1536]{2,1,0:T(8,128)(2,1)S(1)}, bf16[8,24,1536]{2,1,0:T(8,128)(2,1)S(1)}, u32[]{:S(2)}, u32[]{:S(2)}) collective-permute-start(bf16[8,24,1536]{2,1,0:T(8,128)(2,1)S(1)} %all_to_all.20), channel_id=1, source_target_pairs={{0,1},{1,2},{2,3},{3,0},{4,5},{5,6},{6,7},{7,4},{8,9},{9,10},{10,1... | collective-permute-start | bytes 1769480 | tf_op jit(solution)/shard_map/ppermute | solution.py:382
  29.1 13.1 %collective-permute-start.5 = (bf16[8,24,1536]{2,1,0:T(8,128)(2,1)S(1)}, bf16[8,24,1536]{2,1,0:T(8,128)(2,1)S(1)}, u32[]{:S(2)}, u32[]{:S(2)}) collective-permute-start(bf16[8,24,1536]{2,1,0:T(8,128)(2,1)S(1)} %all_to_all.20), channel_id=1, source_target_pairs={{0,3},{1,0},{2,1},{3,2},{4,7},{5,4},{6,5},{7,6},{8,11},{9,8},{10,9... | collective-permute-start | bytes 1769480 | tf_op jit(solution)/shard_map/ppermute | solution.py:382
  30.6 42.6 %collective-permute-start.2 = (bf16[8,24,1536]{2,1,0:T(8,128)(2,1)S(1)}, bf16[8,24,1536]{2,1,0:T(8,128)(2,1)S(1)}, u32[]{:S(2)}, u32[]{:S(2)}) collective-permute-start(bf16[8,24,1536]{2,1,0:T(8,128)(2,1)S(1)} %all_to_all.20), channel_id=1, source_target_pairs={{0,32},{32,0},{64,96},{96,64},{128,160},{160,128},{192,224},{224,1... | collective-permute-start | bytes 1769480 | tf_op jit(solution)/shard_map/ppermute | solution.py:385
  34.4 11.3 %collective-permute-start = (bf16[16,1536]{1,0:T(8,128)(2,1)S(1)}, bf16[16,1536]{1,0:T(8,128)(2,1)S(1)}, u32[]{:S(2)}, u32[]{:S(2)}) collective-permute-start(bf16[16,1536]{1,0:T(8,128)(2,1)S(1)} %get-tuple-element.13), channel_id=1, source_target_pairs={{0,1},{1,2},{2,3},{3,4},{4,5},{5,6},{6,7},{7,8},{8,9},{9,10},{10,1... | collective-permute-start | bytes 147464 | tf_op jit(solution)/shard_map/ppermute | solution.py:440
  36.3 13.3 %collective-permute-start.1 = (bf16[16,1536]{1,0:T(8,128)(2,1)S(1)}, bf16[16,1536]{1,0:T(8,128)(2,1)S(1)}, u32[]{:S(2)}, u32[]{:S(2)}) collective-permute-start(bf16[16,1536]{1,0:T(8,128)(2,1)S(1)} %get-tuple-element.12), channel_id=1, source_target_pairs={{1,0},{2,1},{3,2},{4,3},{5,4},{6,5},{7,6},{8,7},{9,8},{10,9},{11,1... | collective-permute-start | bytes 147464 | tf_op jit(solution)/shard_map/ppermute | solution.py:441
  42.2 7.7 %collective-permute-start.7 = (bf16[4,24,1536]{2,1,0:T(8,128)(2,1)}, bf16[4,24,1536]{2,1,0:T(8,128)(2,1)S(1)}, u32[]{:S(2)}, u32[]{:S(2)}) collective-permute-start(bf16[4,24,1536]{2,1,0:T(8,128)(2,1)} %slice.20), channel_id=1, source_target_pairs={{0,1},{1,2},{2,3},{3,0},{4,5},{5,6},{6,7},{7,4},{8,9},{9,10},{10,1... | collective-permute-start | bytes 884744 | tf_op jit(solution)/shard_map/ppermute | solution.py:382
  43.0 10.7 %collective-permute-start.8 = (bf16[4,24,1536]{2,1,0:T(8,128)(2,1)}, bf16[4,24,1536]{2,1,0:T(8,128)(2,1)}, u32[]{:S(2)}, u32[]{:S(2)}) collective-permute-start(bf16[4,24,1536]{2,1,0:T(8,128)(2,1)} %slice.21), channel_id=1, source_target_pairs={{0,3},{1,0},{2,1},{3,2},{4,7},{5,4},{6,5},{7,6},{8,11},{9,8},{10,9... | collective-permute-start | bytes 884744 | tf_op jit(solution)/shard_map/ppermute | solution.py:382
  45.6 30.3 %collective-permute-start.6 = (bf16[8,24,1536]{2,1,0:T(8,128)(2,1)S(1)}, bf16[8,24,1536]{2,1,0:T(8,128)(2,1)S(1)}, u32[]{:S(2)}, u32[]{:S(2)}) collective-permute-start(bf16[8,24,1536]{2,1,0:T(8,128)(2,1)S(1)} %collective-permute-done.5), channel_id=1, source_target_pairs={{0,32},{32,0},{64,96},{96,64},{128,160},{160,128},{192,224},{224,1... | collective-permute-start | bytes 1769480 | tf_op jit(solution)/shard_map/ppermute | solution.py:385
  49.6 26.3 %collective-permute-start.4 = (bf16[8,24,1536]{2,1,0:T(8,128)(2,1)S(1)}, bf16[8,24,1536]{2,1,0:T(8,128)(2,1)}, u32[]{:S(2)}, u32[]{:S(2)}) collective-permute-start(bf16[8,24,1536]{2,1,0:T(8,128)(2,1)S(1)} %collective-permute-done.3), channel_id=1, source_target_pairs={{0,32},{32,0},{64,96},{96,64},{128,160},{160,128},{192,224},{224,1... | collective-permute-start | bytes 1769480 | tf_op jit(solution)/shard_map/ppermute | solution.py:385
  49.8 33.0 %copy-start.7 = (s32[19]{0:T(128)}, s32[19]{0:T(128)S(1)}, u32[]{:S(2)}) copy-start(s32[19]{0:T(128)S(1)} %concatenate.3.scalars) | copy-start | bytes 232
  49.9 23.2 %copy-start.1 = (bf16[512,1536]{1,0:T(8,128)(2,1)S(1)}, bf16[512,1536]{1,0:T(8,128)(2,1)}, u32[]{:S(2)}) copy-start(bf16[512,1536]{1,0:T(8,128)(2,1)} %cot.1) | copy-start | bytes 4718596
  49.9 32.9 %collective-permute-start.9 = (bf16[4,24,1536]{2,1,0:T(8,128)(2,1)S(1)}, bf16[4,24,1536]{2,1,0:T(8,128)(2,1)S(1)}, u32[]{:S(2)}, u32[]{:S(2)}) collective-permute-start(bf16[4,24,1536]{2,1,0:T(8,128)(2,1)S(1)} %collective-permute-done.7), channel_id=1, source_target_pairs={{0,32},{32,0},{64,96},{96,64},{128,160},{160,128},{192,224},{224,1... | collective-permute-start | bytes 884744 | tf_op jit(solution)/shard_map/ppermute | solution.py:385
  53.7 29.1 %collective-permute-start.10 = (bf16[4,24,1536]{2,1,0:T(8,128)(2,1)}, bf16[4,24,1536]{2,1,0:T(8,128)(2,1)S(1)}, u32[]{:S(2)}, u32[]{:S(2)}) collective-permute-start(bf16[4,24,1536]{2,1,0:T(8,128)(2,1)} %collective-permute-done.8), channel_id=1, source_target_pairs={{0,32},{32,0},{64,96},{96,64},{128,160},{160,128},{192,224},{224,1... | collective-permute-start | bytes 884744 | tf_op jit(solution)/shard_map/ppermute | solution.py:385
  73.1 2.8 %copy-start.9 = (bf16[512,1536]{1,0:T(8,128)(2,1)}, bf16[512,1536]{1,0:T(8,128)(2,1)S(1)}, u32[]{:S(2)}) copy-start(bf16[512,1536]{1,0:T(8,128)(2,1)S(1)} %get-tuple-element.7.hidden) | copy-start | bytes 4718596
  82.8 4.0 %copy-start.2 = (bf16[4,24,1536]{2,1,0:T(8,128)(2,1)}, bf16[4,24,1536]{2,1,0:T(8,128)(2,1)S(1)}, u32[]{:S(2)}) copy-start(bf16[4,24,1536]{2,1,0:T(8,128)(2,1)S(1)} %collective-permute-done.9) | copy-start | bytes 884740
  82.8 4.0 %copy-start.4 = (bf16[4,24,1536]{2,1,0:T(8,128)(2,1)}, bf16[4,24,1536]{2,1,0:T(8,128)(2,1)S(1)}, u32[]{:S(2)}) copy-start(bf16[4,24,1536]{2,1,0:T(8,128)(2,1)S(1)} %collective-permute-done.10) | copy-start | bytes 884740
  82.9 33.3 %copy-start.12 = (f32[8,4,48]{2,1,0:T(4,128)S(1)}, f32[8,4,48]{2,1,0:T(4,128)}, u32[]{:S(2)}) copy-start(f32[8,4,48]{2,1,0:T(4,128)} %param.16) | copy-start | bytes 18436
  82.9 33.3 %copy-start.14 = (f32[8]{0:T(128)S(1)}, f32[8]{0:T(128)}, u32[]{:S(2)}) copy-start(f32[8]{0:T(128)} %param.17) | copy-start | bytes 100
  111.8 13.0 %all-to-all-start.2 = ((f32[32,1,128]{2,1,0:T(1,128)}), f32[32,1,128]{2,1,0:T(1,128)S(1)}, u32[]{:S(2)}, u32[]{:S(2)}) async-start(f32[32,1,128]{2,1,0:T(1,128)} %get-tuple-element.11), calls=%async_computation.2 | async-start | bytes 32768 | tf_op jit(solution)/shard_map/all_to_all | solution.py:450
  127.1 15.7 %all-to-all-start.3 = ((f32[8,4,128]{2,1,0:T(4,128)}), f32[8,4,128]{2,1,0:T(4,128)S(1)}, u32[]{:S(2)}, u32[]{:S(2)}) async-start(f32[8,4,128]{2,1,0:T(4,128)} %clip.1), calls=%async_computation.3 | async-start | bytes 32768 | tf_op jit(solution)/shard_map/all_to_all | solution.py:453
  136.2 1.4 copy-start.10
  (6 other events, 5.8 us)

commit v3 on v1

v3 whole, which is shorter than its diff:
```python
import math

import jax
import jax.numpy as jnp
from jax import lax
from jax.experimental import pallas as pl
from jax.experimental.pallas import tpu as pltpu
from jax.sharding import PartitionSpec as P

BLOCK = 128
LANES = 128
RIM = 16
PADDED = BLOCK + 2 * RIM
STEP = 384
SLOTS = 32
COLS = 4
UTTS = 8
VMEM = 60 << 20


def block_facts(scalars, utts, index):
    utt, limit, cumul = jnp.int32(0), jnp.int32(BLOCK), jnp.int32(0)
    for i in range(utts):
        cumul = cumul + scalars[i]
        utt = utt + (cumul <= index).astype(jnp.int32)
        limit = jnp.where(cumul - 1 == index, scalars[utts + i], limit)
    return utt, limit


def conv_body(blks, scalars, x, *rest):
    rims, (kernel, bias, hidden, slope, padded) = rest[:-5], rest[-5:]
    count = x.shape[0] // BLOCK
    first = scalars[2 * UTTS]
    row = lax.broadcasted_iota(jnp.int32, (BLOCK, LANES), 0)
    rim_row = lax.broadcasted_iota(jnp.int32, (RIM, LANES), 0)
    facts = {}
    for b in blks:
        for near in (b - 1, b, b + 1):
            if near not in facts:
                facts[near] = block_facts(scalars, UTTS, first + near)
    for tile in range(STEP // LANES):
        lanes = slice(tile * LANES, (tile + 1) * LANES)
        for i, b in enumerate(blks):
            utt, limit = facts[b]
            before = (facts[b - 1][0] == utt) & (first + b > 0)
            after = facts[b + 1][0] == utt
            keep = row < limit
            at = b * BLOCK
            left = x[at - RIM : at, lanes] if b else rims[0][:, lanes]
            right = x[at + BLOCK : at + BLOCK + RIM, lanes] if b < count - 1 else rims[1][:, lanes]
            pad = padded.at[tile, i]
            pad[:RIM] = jnp.where(
                rim_row < jnp.where(before, RIM, 0), left.astype(jnp.float32), 0.0
            )
            pad[RIM : RIM + BLOCK] = jnp.where(
                keep, x[at : at + BLOCK, lanes].astype(jnp.float32), 0.0
            )
            pad[RIM + BLOCK :] = jnp.where(
                rim_row < jnp.where(after, facts[b + 1][1], 0), right.astype(jnp.float32), 0.0
            )
            total = jnp.broadcast_to(bias[:, lanes], (BLOCK, LANES))
            for window, taps in windows(pad):
                for q, k in taps:
                    total = total + kernel[k : k + 1, lanes] * window[8 * q : 8 * q + BLOCK]
            logistic = jax.nn.sigmoid(total)
            to = slice(i * BLOCK, (i + 1) * BLOCK)
            hidden[to, lanes] = jnp.where(keep, total * logistic, 0.0).astype(jnp.bfloat16)
            slope[tile, to] = jnp.where(
                keep, logistic * (1.0 + total * (1.0 - logistic)), 0.0
            ).astype(jnp.bfloat16)


def conv(blks, scalars, x, rims, kernel, bias):
    frames, width = x.shape
    own = len(blks) * BLOCK
    column = lambda rows: pl.BlockSpec((rows, STEP), lambda c: (0, c))
    return pl.pallas_call(
        lambda *refs: conv_body(blks, *refs),
        grid=(width // STEP,),
        in_specs=[pl.BlockSpec(memory_space=pltpu.SMEM), column(frames)]
        + [column(RIM)] * len(rims)
        + [column(kernel.shape[0]), column(1)],
        out_specs=[
            column(own),
            pl.BlockSpec((STEP // LANES, own, LANES), lambda c: (c, 0, 0)),
            pl.BlockSpec((STEP // LANES, len(blks), PADDED, LANES), lambda c: (c, 0, 0, 0)),
        ],
        out_shape=[
            jax.ShapeDtypeStruct((own, width), jnp.bfloat16),
            jax.ShapeDtypeStruct((width // LANES, own, LANES), jnp.bfloat16),
            jax.ShapeDtypeStruct((width // LANES, len(blks), PADDED, LANES), jnp.float32),
        ],
        compiler_params=pltpu.CompilerParams(vmem_limit_bytes=VMEM),
        cost_estimate=pl.CostEstimate(
            flops=64 * own * width, bytes_accessed=40 * own * width, transcendentals=own * width
        ),
        name="conv",
    )(scalars, x, *rims, kernel, bias)


class Rows:
    def __init__(self, own, below, above, far_low, far_high):
        self.pieces = [*own, *below, *above, *far_low, *far_high]

    def copies(self, scalars, pieces, weight, sems, part):
        col, core = scalars[2 * UTTS + 1], scalars[2 * UTTS + 2]
        mid, half = pieces[0].shape[0] // 2, pieces[0].shape[2]
        rows = pl.ds(part * mid, mid)
        found = []
        for i in range(2 * COLS):
            piece = pieces[i + 2 * part].at[...] if i >= 6 else pieces[i].at[rows]
            side = 1 - core if i % 2 else core
            shift = (0, COLS - 1, 1, 2)[i // 2]
            found.append(
                pltpu.make_async_copy(
                    piece,
                    weight.at[
                        rows,
                        lax.rem(col + shift, COLS),
                        :,
                        pl.ds(pl.multiple_of(side * half, half), half),
                    ],
                    sems.at[part, i],
                )
            )
        return found

    def scratch(self):
        depth, run, half = self.pieces[0].shape
        return [
            pltpu.VMEM((depth, COLS, run, 2 * half), jnp.bfloat16),
            pltpu.SemaphoreType.DMA((2, 2 * COLS)),
        ]

    def specs(self):
        return [pl.BlockSpec(memory_space=pl.ANY)] * len(self.pieces)


def windows(pad):
    for shift in range(8):
        taps = [(q, 8 * q + shift - 1) for q in range(4) if 0 <= 8 * q + shift - 1 < SLOTS - 1]
        yield pad[shift : shift + BLOCK + 24], taps


def tap_sums(own, pad, b, parts):
    def keep(k, term):
        at = (b * SLOTS + k) * 8
        parts[at : at + 8] = jnp.sum(term.reshape(BLOCK // 8, 8, LANES), axis=0)

    for window, taps in windows(pad):
        for q, k in taps:
            keep(k, own * window[8 * q : 8 * q + BLOCK])
    keep(SLOTS - 1, own)


def grads_body(whole, orders, scalars, cot_far, *rest):
    count = len(orders)
    far, rest = rest[: 2 * count], rest[2 * count :]
    pieces, rest = rest[: len(whole.pieces)], rest[len(whole.pieces) :]
    out, weight, row_sems, cot, *rest = rest
    near, (grad, parts, sems) = rest[: 2 * count], rest[2 * count :]
    depth, cols, run, width = weight.shape
    blks = cot.shape[0] // BLOCK
    steps = 2
    per = depth // steps
    wide_step = per * cols * run
    tiles = wide_step // LANES
    row_copies = [whole.copies(scalars, pieces, weight, row_sems, i) for i in range(steps)]
    head = 3
    first, later = [], []
    for i, (source, target) in enumerate(zip(far, near)):
        for j, (found, low, high) in enumerate(((first, 0, head), (later, head, source.shape[0]))):
            found.append(
                pltpu.make_async_copy(source.at[low:high], target.at[low:high], sems.at[2 * i + j])
            )
    cot_copy = pltpu.make_async_copy(cot_far, cot, sems.at[2 * len(far)])
    for copy in [cot_copy] + row_copies[0]:
        copy.start()

    def taps(step, tile):
        column = step * tiles + tile
        for h, order in enumerate(orders):
            slope, padded = near[2 * h], near[2 * h + 1]
            for i, b in enumerate(order):
                factor = slope[column, i * BLOCK : (i + 1) * BLOCK].astype(jnp.float32)
                tap_sums(grad[tile, b * BLOCK : (b + 1) * BLOCK] * factor, padded.at[column, i], b, parts.at[tile])
        total = parts[tile, pl.ds(0, blks * SLOTS, stride=8)]
        for s in range(1, 8):
            total = total + parts[tile, pl.ds(s, blks * SLOTS, stride=8)]
        out[pl.ds(pl.multiple_of(column * LANES, LANES), LANES)] = total.T.astype(out.dtype)

    def one(step, carry):
        @pl.when(step == 0)
        def _():
            for copy in [cot_copy] + row_copies[0]:
                copy.wait()
            for copy in first + later + row_copies[1]:
                copy.start()

        @pl.when(step == 1)
        def _():
            for copy in row_copies[1]:
                copy.wait()

        hidden_grad = lax.dot_general(
            cot[...],
            weight[pl.ds(step * per, per)].reshape(wide_step, width),
            (((1,), (1,)), ((), ())),
            preferred_element_type=jnp.float32,
        )
        for tile in range(tiles):
            grad[tile] = hidden_grad[:, tile * LANES : (tile + 1) * LANES]

        for low, high, copies in ((0, head, first), (head, tiles, later)):

            @pl.when(step == 0)
            def _():
                for copy in copies:
                    copy.wait()

            for tile in range(low, high):
                taps(step, tile)
        return carry

    lax.fori_loop(0, steps, one, 0)


def grads(scalars, cot, halves, whole):
    frames, width = cot.shape
    blks = frames // BLOCK
    orders = [half[0] for half in halves]
    arrays = [array for half in halves for array in half[1:]]
    anywhere = pl.BlockSpec(memory_space=pl.ANY)
    return pl.pallas_call(
        lambda *refs: grads_body(whole, orders, *refs),
        in_specs=[pl.BlockSpec(memory_space=pltpu.SMEM), anywhere] + [anywhere] * len(arrays) + whole.specs(),
        out_specs=pl.BlockSpec(memory_space=pltpu.VMEM),
        out_shape=jax.ShapeDtypeStruct((width, blks * SLOTS), jnp.bfloat16),
        scratch_shapes=whole.scratch()
        + [pltpu.VMEM(array.shape, array.dtype) for array in [cot] + arrays]
        + [
            pltpu.VMEM((width // 2 // LANES, frames, LANES), jnp.float32),
            pltpu.VMEM((width // 2 // LANES, blks * SLOTS * 8, LANES), jnp.float32),
            pltpu.SemaphoreType.DMA((1 + 2 * len(arrays),)),
        ],
        compiler_params=pltpu.CompilerParams(vmem_limit_bytes=VMEM),
        cost_estimate=pl.CostEstimate(
            flops=2 * frames * width * width, bytes_accessed=20 * frames * width, transcendentals=0
        ),
        name="grads",
    )(scalars, cot, *arrays, *whole.pieces)


def project_body(whole, orders, scalars, *refs):
    hiddens, rest = refs[: len(orders)], refs[len(orders) :]
    pieces, (out, weight, sems) = rest[:-3], rest[-3:]

    @pl.when(pl.program_id(0) == 0)
    def _():
        found = [copy for part in range(2) for copy in whole.copies(scalars, pieces, weight, sems, part)]
        for copy in found:
            copy.start()
        for copy in found:
            copy.wait()

    step = out.shape[1]
    lanes = pl.ds(pl.multiple_of(pl.program_id(0) * step, step), step)
    for order, hidden in zip(orders, hiddens):
        product = jnp.dot(
            hidden[...],
            weight[:, :, :, lanes].reshape(hidden.shape[1], step),
            preferred_element_type=jnp.float32,
        )
        for i, b in enumerate(order):
            out[b * BLOCK : (b + 1) * BLOCK] = product[i * BLOCK : (i + 1) * BLOCK].astype(out.dtype)


def project(scalars, orders, hiddens, whole):
    width = hiddens[0].shape[1]
    frames = sum(hidden.shape[0] for hidden in hiddens)
    step = 512
    return pl.pallas_call(
        lambda *refs: project_body(whole, orders, *refs),
        grid=(width // step,),
        in_specs=[pl.BlockSpec(memory_space=pltpu.SMEM)]
        + [pl.BlockSpec(hidden.shape, lambda c: (0, 0)) for hidden in hiddens]
        + whole.specs(),
        out_specs=pl.BlockSpec((frames, step), lambda c: (0, c)),
        out_shape=jax.ShapeDtypeStruct((frames, width), jnp.bfloat16),
        scratch_shapes=whole.scratch(),
        compiler_params=pltpu.CompilerParams(vmem_limit_bytes=VMEM),
        cost_estimate=pl.CostEstimate(
            flops=2 * frames * width * width, bytes_accessed=2 * width * width + 4 * frames * width, transcendentals=0
        ),
        name="project",
    )(scalars, *hiddens, *whole.pieces)


def sums_body(scalars, parts, sums, norms, chosen):
    senders, channels, lanes = parts.shape
    utts = UTTS
    per = lanes // SLOTS
    blk = lax.broadcasted_iota(jnp.int32, (senders, lanes), 0) * per + (
        lax.broadcasted_iota(jnp.int32, (senders, lanes), 1) // SLOTS
    )
    utt_of, cumul = jnp.zeros((senders, lanes), jnp.int32), jnp.int32(0)
    for i in range(utts):
        cumul = cumul + scalars[i]
        utt_of = utt_of + (cumul <= blk).astype(jnp.int32)
    for u in range(utts):
        chosen[u] = jnp.where(utt_of == u, 1.0, 0.0)
    spot = lax.broadcasted_iota(jnp.int32, (1, lanes), 1)
    row = jnp.zeros((1, lanes), jnp.float32)
    totals = [jnp.zeros((channels, lanes), jnp.float32) for _ in range(utts)]
    for s in range(senders):
        part = parts[s].astype(jnp.float32)
        for u in range(utts):
            totals[u] = totals[u] + chosen[u, s : s + 1] * part
    for u in range(utts):
        total = totals[u]
        total = total + pltpu.roll(total, 64, 1)
        total = total + pltpu.roll(total, 32, 1)
        sums[u] = total
        square = jnp.sum(jnp.sum(total * total, axis=0, keepdims=True), axis=1, keepdims=True)
        row = row + jnp.where(spot == u, square * (1.0 / per), 0.0)
    norms[...] = jnp.broadcast_to(row[None], norms.shape)


def sums_and_norms(scalars, parts):
    senders, channels, lanes = parts.shape
    whole = lambda shape: pl.BlockSpec(shape, lambda c: (0, 0, 0))
    return pl.pallas_call(
        sums_body,
        grid=(1,),
        in_specs=[pl.BlockSpec(memory_space=pltpu.SMEM), whole(parts.shape)],
        out_specs=[whole((UTTS, channels, lanes)), whole((senders, 1, lanes))],
        out_shape=[
            jax.ShapeDtypeStruct((UTTS, channels, lanes), jnp.float32),
            jax.ShapeDtypeStruct((senders, 1, lanes), jnp.float32),
        ],
        scratch_shapes=[pltpu.VMEM((UTTS, senders, lanes), jnp.float32)],
        name="sums",
    )(scalars, parts)


def clip_body(clip_bound, sums, norms, out):
    utts, channels, lanes = sums.shape
    square = jnp.sum(norms[...], axis=0)
    factor = clip_bound / jnp.maximum(jnp.sqrt(square), clip_bound)
    spot = lax.broadcasted_iota(jnp.int32, (1, lanes), 1)
    total = jnp.zeros((channels, lanes), jnp.float32)
    for u in range(utts):
        own = jnp.sum(jnp.where(spot == u, factor, 0.0), axis=1, keepdims=True)
        total = total + own * sums[u]
    wide = jnp.concatenate([total, jnp.zeros((lanes - channels, lanes), jnp.float32)], axis=0).T
    groups, rows, _ = out.shape
    for g in range(groups):
        out[g] = wide[g * rows : (g + 1) * rows]


def clipped(sums, norms, clip_bound, groups):
    vmem = pl.BlockSpec(memory_space=pltpu.VMEM)
    return pl.pallas_call(
        lambda *refs: clip_body(clip_bound, *refs),
        in_specs=[vmem, vmem],
        out_specs=vmem,
        out_shape=jax.ShapeDtypeStruct((groups, SLOTS // groups, LANES), jnp.float32),
        name="clip",
    )(sums, norms)


def row_moves(shards, groups):
    depth = shards // COLS

    def shifted(value, by):
        pairs = [(z * COLS + x, z * COLS + (x + by) % COLS) for z in range(depth) for x in range(COLS)]
        return lax.ppermute(value, "tm", pairs)

    def swapped(value):
        return lax.ppermute(value, "utt", [(i, i ^ 1) for i in range(groups)])

    return swapped, shifted


def column_rows(own, shards):
    depth = shards // COLS
    return lax.all_to_all(
        jnp.broadcast_to(own[None], (depth,) + own.shape),
        "tm",
        0,
        0,
        axis_index_groups=[[z * COLS + x for z in range(depth)] for x in range(COLS)],
        tiled=True,
    )


def per_device(
    glu_out, cotangent, kernel, conv_bias, out_weight, blocks, last_fill, noise_draws, band_coef
):
    frames, width = glu_out.shape
    blk_count = frames // BLOCK
    shards = lax.axis_size("tm")
    groups = lax.axis_size("utt")
    device = lax.axis_index("tm").astype(jnp.int32)
    core = lax.axis_index("utt").astype(jnp.int32) % 2
    col = device % COLS
    scalars = jnp.concatenate(
        [blocks[0], last_fill[0], jnp.stack([device * blk_count, col, core])]
    )
    swapped, shifted = row_moves(shards, groups)
    half = width // 2
    own = column_rows(lax.dynamic_slice_in_dim(out_weight, core * half, half, axis=1), shards)
    forward = [(i, i + 1) for i in range(shards - 1)]
    backward = [(target, source) for source, target in forward]
    low = lax.ppermute(glu_out[frames - RIM :], "tm", forward)
    high = lax.ppermute(glu_out[:RIM], "tm", backward)
    inner, outer = tuple(range(1, blk_count - 1)), (0, blk_count - 1)
    bias = conv_bias[None]
    hidden_in, *half_in = conv(inner, scalars, glu_out, [], kernel, bias)
    own, hidden_in, low, high = lax.optimization_barrier((own, hidden_in, low, high))
    below, above = shifted(own, 1), shifted(own, -1)
    own_mate = swapped(own)
    hidden_out, *half_out = conv(outer, scalars, glu_out, [low, high], kernel, bias)
    below, above, own_mate, hidden_out = lax.optimization_barrier((below, above, own_mate, hidden_out))
    halves = [(inner, *half_in), (outer, *half_out)]
    mid = shards // COLS // 2
    far_low, far_high = shifted(below[:mid], 1), shifted(above[mid:], -1)
    whole = Rows(
        (own, own_mate), (below, swapped(below)), (above, swapped(above)),
        (far_low, swapped(far_low)), (far_high, swapped(far_high)),
    )
    parts = grads(scalars, cotangent, halves, whole)
    parts = parts.reshape(shards, width // shards, parts.shape[1])
    parts = lax.all_to_all(parts, "tm", 0, 0, tiled=True)
    block_out = project(scalars, [inner, outer], [hidden_in, hidden_out], whole)
    parts, block_out = lax.optimization_barrier((parts, block_out))
    sums, norms = sums_and_norms(scalars, parts)
    norms = lax.all_to_all(norms, "tm", 0, 0, tiled=True)
    clip_bound = 300.0 * math.sqrt(width)
    contrib = clipped(sums, norms, clip_bound, groups)
    contrib = lax.all_to_all(contrib, "utt", 0, 0, tiled=True)
    own_share = jnp.sum(contrib, axis=0)[:, : width // shards]
    mixture = jnp.sum(band_coef[:, None, None] * noise_draws, axis=0)
    mean_grad = (own_share + 0.1 * clip_bound * mixture) / (UTTS * groups)
    return (block_out, mean_grad)


def solution(mesh):
    return jax.shard_map(
        per_device,
        mesh=mesh,
        in_specs=(
            P(("utt", "tm"), None),
            P(("utt", "tm"), None),
            P(),
            P(),
            P("tm", None),
            P("utt", None),
            P("utt", None),
            P(None, "utt", "tm"),
            P(),
        ),
        out_specs=(P(("utt", "tm"), None), P("utt", "tm")),
        check_vma=False,
    )
```

time: 171 us -> 127 us (0.74)
  waiting for transfers between devices: 72.7 us -> 27.3 us
  starting transfers between devices: 19.7 us -> 39.1 us
  Pallas kernels: 25.3 us -> 39.1 us
  between operations: 14.1 us -> 0.87 us
  local copies, waits for them, and re-layouts: 14.7 us -> 5.75 us
  matrix products: 6.56 us -> 0 us
  blocking collectives: 16.8 us -> 13.5 us
    all_gather x1 -> x0, waiting for transfers between devices: 60.7 us -> none  [per_device(): full_weight = lax.all_gather(out_weight, 'tm', axis=0, tiled=True)]
    pallas_call x3 -> x5, Pallas kernels: 23.6 us -> 37.4 us  [the longest x1 14.1 us: grads(): pl.pallas_call(lambda *refs: grads_body(whole, orders, *refs), in_specs=[...]
    all_to_all x1 -> x2, starting transfers between devices: 4.09 us -> 16.4 us  [the longest x1 9.01 us: column_rows(): lax.all_to_all(jnp.broadcast_to(own[None], (depth,) + own.shape), 'tm', 0...]
    ppermute x0 -> x9, starting transfers between devices: none -> 11 us  [the longest x4 5.51 us: shifted(): return lax.ppermute(value, 'tm', pairs)]
    unnamed x24 -> x38, local copies, waits for them, and re-layouts: 13.2 us -> 2.73 us
    ppermute x0 -> x9, waiting for transfers between devices: none -> 10.4 us  [the longest x4 9.02 us: shifted(): return lax.ppermute(value, 'tm', pairs)]
    dot_general x1 -> x0, matrix products: 6.56 us -> none  [per_device(): jnp.dot(hidden, full_weight, preferred_element_type=jnp.float32)]
    all_to_all x1, waiting for transfers between devices: 0.01 us -> 4.56 us  [per_device(): contrib = lax.all_to_all(contrib, 'utt', 0, 0, tiled=True)]
  transfers between devices with their start and end apart: 5 -> 14, of which waited for: 3 -> 7; matrix products, arithmetic and copies ran while one was open for 5% -> 2% of each run, Pallas kernels for 6% -> 17%
where the time goes in v3:
time: 127 us; the launch traced here: 126 us
  starting transfers between devices  39.1 us (31%)
  Pallas kernels  39.1 us (31%)
  waiting for transfers between devices  27.3 us (21%)
  blocking collectives  13.5 us (11%)
  local copies, waits for them, and re-layouts  5.75 us (5%)
    pallas_call x1, Pallas kernels, grads(): pl.pallas_call(lambda *refs: grads_body(whole, orders, *refs), in_specs=[...  14.1 us
    all_to_all x1, blocking collectives, per_device(): norms = lax.all_to_all(norms, 'tm', 0, 0, tiled=True)  13.5 us
    pallas_call x2, Pallas kernels, conv(): pl.pallas_call(lambda *refs: conv_body(blks, *refs), grid=(width // STEP,...  13.2 us
    ppermute x4, waiting for transfers between devices, shifted(): return lax.ppermute(value, 'tm', pairs)  9.02 us
    all_to_all x1, starting transfers between devices, column_rows(): lax.all_to_all(jnp.broadcast_to(own[None], (depth,) + own.shape), 'tm', 0...  9.01 us
    pallas_call x1, Pallas kernels, project(): pl.pallas_call(lambda *refs: project_body(whole, orders, *refs), grid=(wi...  7.7 us
    all_to_all x1, starting transfers between devices, per_device(): parts = lax.all_to_all(parts, 'tm', 0, 0, tiled=True)  7.39 us
    all_to_all x1, starting transfers between devices, per_device(): contrib = lax.all_to_all(contrib, 'utt', 0, 0, tiled=True)  7.32 us
  transfers between devices with their start and end apart: 14, of which 7 were waited for; matrix products, arithmetic and copies ran while one was open for 2% of the time, Pallas kernels for 17%

profile of v3, /device:TPU:1, one launch (start us, length us, event | category | flops | bytes accessed | tf_op | source)
XLA Modules:
  0.0 126.3 jit_solution(5516049193610534848)
XLA Ops:
  2.4 9.0 %all-to-all-start = ((bf16[8,48,768]{2,1,0:T(8,128)(2,1)}), bf16[8,48,768]{2,1,0:T(8,128)(2,1)S(1)}, u32[]{:S(2)}, u32[]{:S(2)}) async-start(bf16[8,48,768]{2,1,0:T(8,128)(2,1)} %broadcast_in_dim.5), calls=%async_computation | async-start | bytes 1179648 | tf_op jit(solution)/shard_map/all_to_all | solution.py:387
  12.3 3.1 %collective-permute-start = (bf16[16,1536]{1,0:T(8,128)(2,1)S(1)}, bf16[16,1536]{1,0:T(8,128)(2,1)S(1)}, u32[]{:S(2)}, u32[]{:S(2)}) collective-permute-start(bf16[16,1536]{1,0:T(8,128)(2,1)S(1)} %get-tuple-element.39), channel_id=1, source_target_pairs={{0,1},{1,2},{2,3},{3,4},{4,5},{5,6},{6,7},{7,8},{8,9},{9,10},{10,1... | collective-permute-start | bytes 147464 | tf_op jit(solution)/shard_map/ppermute | solution.py:415
  15.4 1.3 %collective-permute-start.1 = (bf16[16,1536]{1,0:T(8,128)(2,1)S(1)}, bf16[16,1536]{1,0:T(8,128)(2,1)S(1)}, u32[]{:S(2)}, u32[]{:S(2)}) collective-permute-start(bf16[16,1536]{1,0:T(8,128)(2,1)S(1)} %get-tuple-element.38), channel_id=1, source_target_pairs={{1,0},{2,1},{3,2},{4,3},{5,4},{6,5},{7,6},{8,7},{9,8},{10,9},{11,1... | collective-permute-start | bytes 147464 | tf_op jit(solution)/shard_map/ppermute | solution.py:416
  18.0 6.6 %conv.2 = (bf16[256,1536]{1,0:T(8,128)(2,1)}, bf16[12,256,128]{2,1,0:T(8,128)(2,1)}, f32[12,2,160,128]{3,2,1,0:T(8,128)}) custom-call(s32[19]{0:T(128)} %concatenate.3.refs_0_.scalars, bf16[512,1536]{1,0:T(8,128)(2,1)} %refs_1_.4, f32[31,1536]{1,0:T(8,128)} %refs_4_.1, f32[1,1536]{1,0:T(1,128)} %broadcast_in_dim.4.refs_3_.refs_5_), custom_call_target="tpu_custom_call" | custom-call | flops 25165824 | bytes 15728640 | tf_op jit(solution)/shard_map/conv/pallas_call | solution.py:77
  24.6 6.2 %all-to-all-done.refs_6_.refs_3_ = bf16[8,48,768]{2,1,0:T(8,128)(2,1)S(1)} async-done(((bf16[8,48,768]{2,1,0:T(8,128)(2,1)}), bf16[8,48,768]{2,1,0:T(8,128)(2,1)S(1)}, u32[]{:S(2)}, u32[]{:S(2)}) %all-to-all-start) | async-done | bytes 589856 | tf_op jit(solution)/shard_map/all_to_all | solution.py:387
  30.8 1.2 collective-permute-start.2
  32.0 1.5 %collective-permute-start.3 = (bf16[8,48,768]{2,1,0:T(8,128)(2,1)S(1)}, bf16[8,48,768]{2,1,0:T(8,128)(2,1)S(1)}, u32[]{:S(2)}, u32[]{:S(2)}) collective-permute-start(bf16[8,48,768]{2,1,0:T(8,128)(2,1)S(1)} %all-to-all-done.refs_6_.refs_3_), channel_id=1, source_target_pairs={{0,3},{1,0},{2,1},{3,2},{4,7},{5,4},{6,5},{7,6},{8,11},{9,8},{10,9... | collective-permute-start | bytes 1769480 | tf_op jit(solution)/shard_map/ppermute | solution.py:377
  33.5 1.1 collective-permute-start.4
  34.5 6.6 %conv.3 = (bf16[256,1536]{1,0:T(8,128)(2,1)}, bf16[12,256,128]{2,1,0:T(8,128)(2,1)}, f32[12,2,160,128]{3,2,1,0:T(8,128)}) custom-call(s32[19]{0:T(128)} %concatenate.3.refs_0_.scalars, bf16[512,1536]{1,0:T(8,128)(2,1)} %refs_1_.4, bf16[16,1536]{1,0:T(8,128)(2,1)} %copy-done.12, bf16[16,1536]{1,0:T(8,128)(2,1)} %copy-done.13, f32[31,1536]{1,0:T(8,128)} %refs_4_.1, ...), custom_call_target="tpu_custom_call" | custom-call | flops 25165824 | bytes 15728640 | tf_op jit(solution)/shard_map/conv/pallas_call | solution.py:77
  41.1 5.3 %collective-permute-done.2.refs_8_.refs_5_ = bf16[8,48,768]{2,1,0:T(8,128)(2,1)S(1)} collective-permute-done((bf16[8,48,768]{2,1,0:T(8,128)(2,1)S(1)}, bf16[8,48,768]{2,1,0:T(8,128)(2,1)S(1)}, u32[]{:S(2)}, u32[]{:S(2)}) %collective-permute-start.2) | collective-permute-done | bytes 589856 | tf_op jit(solution)/shard_map/ppermute | solution.py:377
  46.5 0.9 collective-permute-start.7
  47.5 1.9 %collective-permute-start.9 = (bf16[4,48,768]{2,1,0:T(8,128)(2,1)S(1)}, bf16[4,48,768]{2,1,0:T(8,128)(2,1)S(1)}, u32[]{:S(2)}, u32[]{:S(2)}) collective-permute-start(bf16[4,48,768]{2,1,0:T(8,128)(2,1)S(1)} %slice.18), channel_id=1, source_target_pairs={{0,3},{1,0},{2,1},{3,2},{4,7},{5,4},{6,5},{7,6},{8,11},{9,8},{10,9... | collective-permute-start | bytes 884744 | tf_op jit(solution)/shard_map/ppermute | solution.py:377
  49.3 1.9 %collective-permute-start.5 = (bf16[8,48,768]{2,1,0:T(8,128)(2,1)S(1)}, bf16[8,48,768]{2,1,0:T(8,128)(2,1)S(1)}, u32[]{:S(2)}, u32[]{:S(2)}) collective-permute-start(bf16[8,48,768]{2,1,0:T(8,128)(2,1)S(1)} %collective-permute-done.2.refs_8_.refs_5_), channel_id=1, source_target_pairs={{0,32},{32,0},{64,96},{96,64},{128,160},{160,128},{192,224},{224,1... | collective-permute-start | bytes 1769480 | tf_op jit(solution)/shard_map/ppermute | solution.py:380
  51.2 3.7 %collective-permute-done.7.refs_12_.refs_9_ = bf16[4,48,768]{2,1,0:T(8,128)(2,1)S(1)} collective-permute-done((bf16[4,48,768]{2,1,0:T(8,128)(2,1)S(1)}, bf16[4,48,768]{2,1,0:T(8,128)(2,1)S(1)}, u32[]{:S(2)}, u32[]{:S(2)}) %collective-permute-start.7) | collective-permute-done | bytes 294944 | tf_op jit(solution)/shard_map/ppermute | solution.py:377
  54.9 2.3 %collective-permute-start.8 = (bf16[4,48,768]{2,1,0:T(8,128)(2,1)S(1)}, bf16[4,48,768]{2,1,0:T(8,128)(2,1)S(1)}, u32[]{:S(2)}, u32[]{:S(2)}) collective-permute-start(bf16[4,48,768]{2,1,0:T(8,128)(2,1)S(1)} %collective-permute-done.7.refs_12_.refs_9_), channel_id=1, source_target_pairs={{0,32},{32,0},{64,96},{96,64},{128,160},{160,128},{192,224},{224,1... | collective-permute-start | bytes 884744 | tf_op jit(solution)/shard_map/ppermute | solution.py:380
  60.0 14.1 %grads.1 = bf16[1536,128]{1,0:T(8,128)(2,1)} custom-call(s32[19]{0:T(128)} %concatenate.3.refs_0_.scalars, bf16[512,1536]{1,0:T(8,128)(2,1)} %refs_1_.5, bf16[12,256,128]{2,1,0:T(8,128)(2,1)} %get-tuple-element.20.refs_2_, f32[12,2,160,128]{3,2,1,0:T(8,128)} %get-tuple-element.21.refs_3_, bf16[12,256,128]{2,1,0:T(8,128)(2,1)} %get-tuple-element.25.refs_4_, ...), custom_call_target="tpu_custom_call" | custom-call | flops 2415919104 | bytes 15728640 | tf_op jit(solution)/shard_map/grads/pallas_call | solution.py:234
  74.1 7.4 %all-to-all-start.1 = ((bf16[32,48,128]{2,1,0:T(8,128)(2,1)}), bf16[32,48,128]{2,1,0:T(8,128)(2,1)S(1)}, u32[]{:S(2)}, u32[]{:S(2)}) async-start(bf16[32,48,128]{2,1,0:T(8,128)(2,1)} %bitcast.6), calls=%async_computation.1 | async-start | bytes 786432 | tf_op jit(solution)/shard_map/all_to_all | solution.py:434
  81.5 7.7 %project.1 = bf16[512,1536]{1,0:T(8,128)(2,1)} custom-call(s32[19]{0:T(128)} %concatenate.3.refs_0_.scalars, bf16[256,1536]{1,0:T(8,128)(2,1)} %get-tuple-element.32.refs_1_, bf16[256,1536]{1,0:T(8,128)(2,1)} %get-tuple-element.33.refs_2_, bf16[8,48,768]{2,1,0:T(8,128)(2,1)} %copy-done.1, bf16[8,48,768]{2,1,0:T(8,128)(2,1)} %copy-done.5, ...), custom_call_target="tpu_custom_call" | custom-call | flops 2415919104 | bytes 7864320 | tf_op jit(solution)/shard_map/project/pallas_call | solution.py:282
  89.2 6.2 %all-to-all-done.1.parts = bf16[32,48,128]{2,1,0:T(8,128)(2,1)S(1)} async-done(((bf16[32,48,128]{2,1,0:T(8,128)(2,1)}), bf16[32,48,128]{2,1,0:T(8,128)(2,1)S(1)}, u32[]{:S(2)}, u32[]{:S(2)}) %all-to-all-start.1) | async-done | bytes 393248 | tf_op jit(solution)/shard_map/all_to_all | solution.py:434
  96.1 2.4 %sums.1 = (f32[8,48,128]{2,1,0:T(8,128)}, f32[32,1,128]{2,1,0:T(1,128)}) custom-call(s32[19]{0:T(128)} %concatenate.3.refs_0_.scalars, bf16[32,48,128]{2,1,0:T(8,128)(2,1)} %copy-done.2), custom_call_target="tpu_custom_call" | custom-call | tf_op jit(solution)/shard_map/sums/pallas_call | solution.py:332
  98.5 13.5 %all_to_all.20.refs_1_ = f32[32,1,128]{2,1,0:T(1,128)} all-to-all(f32[32,1,128]{2,1,0:T(1,128)} %get-tuple-element.37), channel_id=1, replica_groups=mesh['utt'=8,'tm'=32] {'tm'}, dimensions={0} | all-to-all | bytes 32768 | tf_op jit(solution)/shard_map/all_to_all | solution.py:438
  112.0 1.7 %clip.1 = f32[8,4,128]{2,1,0:T(4,128)} custom-call(f32[8,48,128]{2,1,0:T(8,128)} %get-tuple-element.36.refs_0_, f32[32,1,128]{2,1,0:T(1,128)} %all_to_all.20.refs_1_), custom_call_target="tpu_custom_call" | custom-call | tf_op jit(solution)/shard_map/clip/pallas_call | solution.py:363
  113.7 7.3 %all-to-all-start.3 = ((f32[8,4,128]{2,1,0:T(4,128)}), f32[8,4,128]{2,1,0:T(4,128)S(1)}, u32[]{:S(2)}, u32[]{:S(2)}) async-start(f32[8,4,128]{2,1,0:T(4,128)} %clip.1), calls=%async_computation.3 | async-start | bytes 32768 | tf_op jit(solution)/shard_map/all_to_all | solution.py:441
  121.1 4.6 %all-to-all-done.3 = f32[8,4,128]{2,1,0:T(4,128)S(1)} async-done(((f32[8,4,128]{2,1,0:T(4,128)}), f32[8,4,128]{2,1,0:T(4,128)S(1)}, u32[]{:S(2)}, u32[]{:S(2)}) %all-to-all-start.3) | async-done | bytes 16416 | tf_op jit(solution)/shard_map/all_to_all | solution.py:441
  (59 shorter events, 8.1 us)
Async XLA Ops:
  0.6 16.1 %copy-start.15 = (f32[1536]{0:T(1024)S(1)}, f32[1536]{0:T(1024)}, u32[]{:S(2)}) copy-start(f32[1536]{0:T(1024)} %param.12) | copy-start | bytes 18436
  0.7 16.7 %copy-start.17 = (s32[1,8]{1,0:T(1,128)S(1)}, s32[1,8]{1,0:T(1,128)}, u32[]{:S(2)}) copy-start(s32[1,8]{1,0:T(1,128)} %param.14) | copy-start | bytes 100
  0.7 16.6 %copy-start.18 = (s32[1,8]{1,0:T(1,128)S(1)}, s32[1,8]{1,0:T(1,128)}, u32[]{:S(2)}) copy-start(s32[1,8]{1,0:T(1,128)} %param.15) | copy-start | bytes 100
  2.4 28.4 %all-to-all-start = ((bf16[8,48,768]{2,1,0:T(8,128)(2,1)}), bf16[8,48,768]{2,1,0:T(8,128)(2,1)S(1)}, u32[]{:S(2)}, u32[]{:S(2)}) async-start(bf16[8,48,768]{2,1,0:T(8,128)(2,1)} %broadcast_in_dim.5), calls=%async_computation | async-start | bytes 1179648 | tf_op jit(solution)/shard_map/all_to_all | solution.py:387
  12.3 12.3 %collective-permute-start = (bf16[16,1536]{1,0:T(8,128)(2,1)S(1)}, bf16[16,1536]{1,0:T(8,128)(2,1)S(1)}, u32[]{:S(2)}, u32[]{:S(2)}) collective-permute-start(bf16[16,1536]{1,0:T(8,128)(2,1)S(1)} %get-tuple-element.39), channel_id=1, source_target_pairs={{0,1},{1,2},{2,3},{3,4},{4,5},{5,6},{6,7},{7,8},{8,9},{9,10},{10,1... | collective-permute-start | bytes 147464 | tf_op jit(solution)/shard_map/ppermute | solution.py:415
  15.4 9.2 %collective-permute-start.1 = (bf16[16,1536]{1,0:T(8,128)(2,1)S(1)}, bf16[16,1536]{1,0:T(8,128)(2,1)S(1)}, u32[]{:S(2)}, u32[]{:S(2)}) collective-permute-start(bf16[16,1536]{1,0:T(8,128)(2,1)S(1)} %get-tuple-element.38), channel_id=1, source_target_pairs={{1,0},{2,1},{3,2},{4,3},{5,4},{6,5},{7,6},{8,7},{9,8},{10,9},{11,1... | collective-permute-start | bytes 147464 | tf_op jit(solution)/shard_map/ppermute | solution.py:416
  24.6 10.0 %copy-start.12 = (bf16[16,1536]{1,0:T(8,128)(2,1)}, bf16[16,1536]{1,0:T(8,128)(2,1)S(1)}, u32[]{:S(2)}) copy-start(bf16[16,1536]{1,0:T(8,128)(2,1)S(1)} %collective-permute-done.refs_2_) | copy-start | bytes 147460
  30.8 28.9 %copy-start.1 = (bf16[8,48,768]{2,1,0:T(8,128)(2,1)}, bf16[8,48,768]{2,1,0:T(8,128)(2,1)S(1)}, u32[]{:S(2)}) copy-start(bf16[8,48,768]{2,1,0:T(8,128)(2,1)S(1)} %all-to-all-done.refs_6_.refs_3_) | copy-start | bytes 1769476
  30.8 15.6 %collective-permute-start.2 = (bf16[8,48,768]{2,1,0:T(8,128)(2,1)S(1)}, bf16[8,48,768]{2,1,0:T(8,128)(2,1)S(1)}, u32[]{:S(2)}, u32[]{:S(2)}) collective-permute-start(bf16[8,48,768]{2,1,0:T(8,128)(2,1)S(1)} %all-to-all-done.refs_6_.refs_3_), channel_id=1, source_target_pairs={{0,1},{1,2},{2,3},{3,0},{4,5},{5,6},{6,7},{7,4},{8,9},{9,10},{10,1... | collective-permute-start | bytes 1769480 | tf_op jit(solution)/shard_map/ppermute | solution.py:377
  32.0 14.4 %collective-permute-start.3 = (bf16[8,48,768]{2,1,0:T(8,128)(2,1)S(1)}, bf16[8,48,768]{2,1,0:T(8,128)(2,1)S(1)}, u32[]{:S(2)}, u32[]{:S(2)}) collective-permute-start(bf16[8,48,768]{2,1,0:T(8,128)(2,1)S(1)} %all-to-all-done.refs_6_.refs_3_), channel_id=1, source_target_pairs={{0,3},{1,0},{2,1},{3,2},{4,7},{5,4},{6,5},{7,6},{8,11},{9,8},{10,9... | collective-permute-start | bytes 1769480 | tf_op jit(solution)/shard_map/ppermute | solution.py:377
  33.5 12.9 %collective-permute-start.4 = (bf16[8,48,768]{2,1,0:T(8,128)(2,1)S(1)}, bf16[8,48,768]{2,1,0:T(8,128)(2,1)S(1)}, u32[]{:S(2)}, u32[]{:S(2)}) collective-permute-start(bf16[8,48,768]{2,1,0:T(8,128)(2,1)S(1)} %all-to-all-done.refs_6_.refs_3_), channel_id=1, source_target_pairs={{0,32},{32,0},{64,96},{96,64},{128,160},{160,128},{192,224},{224,1... | collective-permute-start | bytes 1769480 | tf_op jit(solution)/shard_map/ppermute | solution.py:380
  46.4 13.3 %copy-start.3 = (bf16[8,48,768]{2,1,0:T(8,128)(2,1)}, bf16[8,48,768]{2,1,0:T(8,128)(2,1)S(1)}, u32[]{:S(2)}) copy-start(bf16[8,48,768]{2,1,0:T(8,128)(2,1)S(1)} %collective-permute-done.2.refs_8_.refs_5_) | copy-start | bytes 1769476
  46.4 13.3 %copy-start.4 = (bf16[8,48,768]{2,1,0:T(8,128)(2,1)}, bf16[8,48,768]{2,1,0:T(8,128)(2,1)S(1)}, u32[]{:S(2)}) copy-start(bf16[8,48,768]{2,1,0:T(8,128)(2,1)S(1)} %collective-permute-done.3.refs_10_.refs_7_) | copy-start | bytes 1769476
  46.4 13.3 %copy-start.5 = (bf16[8,48,768]{2,1,0:T(8,128)(2,1)}, bf16[8,48,768]{2,1,0:T(8,128)(2,1)S(1)}, u32[]{:S(2)}) copy-start(bf16[8,48,768]{2,1,0:T(8,128)(2,1)S(1)} %collective-permute-done.4.refs_7_.refs_4_) | copy-start | bytes 1769476
  46.5 8.5 %collective-permute-start.7 = (bf16[4,48,768]{2,1,0:T(8,128)(2,1)S(1)}, bf16[4,48,768]{2,1,0:T(8,128)(2,1)S(1)}, u32[]{:S(2)}, u32[]{:S(2)}) collective-permute-start(bf16[4,48,768]{2,1,0:T(8,128)(2,1)S(1)} %slice.17), channel_id=1, source_target_pairs={{0,1},{1,2},{2,3},{3,0},{4,5},{5,6},{6,7},{7,4},{8,9},{9,10},{10,1... | collective-permute-start | bytes 884744 | tf_op jit(solution)/shard_map/ppermute | solution.py:377
  47.5 9.7 %collective-permute-start.9 = (bf16[4,48,768]{2,1,0:T(8,128)(2,1)S(1)}, bf16[4,48,768]{2,1,0:T(8,128)(2,1)S(1)}, u32[]{:S(2)}, u32[]{:S(2)}) collective-permute-start(bf16[4,48,768]{2,1,0:T(8,128)(2,1)S(1)} %slice.18), channel_id=1, source_target_pairs={{0,3},{1,0},{2,1},{3,2},{4,7},{5,4},{6,5},{7,6},{8,11},{9,8},{10,9... | collective-permute-start | bytes 884744 | tf_op jit(solution)/shard_map/ppermute | solution.py:377
  49.3 9.5 %collective-permute-start.5 = (bf16[8,48,768]{2,1,0:T(8,128)(2,1)S(1)}, bf16[8,48,768]{2,1,0:T(8,128)(2,1)S(1)}, u32[]{:S(2)}, u32[]{:S(2)}) collective-permute-start(bf16[8,48,768]{2,1,0:T(8,128)(2,1)S(1)} %collective-permute-done.2.refs_8_.refs_5_), channel_id=1, source_target_pairs={{0,32},{32,0},{64,96},{96,64},{128,160},{160,128},{192,224},{224,1... | collective-permute-start | bytes 1769480 | tf_op jit(solution)/shard_map/ppermute | solution.py:380
  51.2 7.6 %collective-permute-start.6 = (bf16[8,48,768]{2,1,0:T(8,128)(2,1)S(1)}, bf16[8,48,768]{2,1,0:T(8,128)(2,1)S(1)}, u32[]{:S(2)}, u32[]{:S(2)}) collective-permute-start(bf16[8,48,768]{2,1,0:T(8,128)(2,1)S(1)} %collective-permute-done.3.refs_10_.refs_7_), channel_id=1, source_target_pairs={{0,32},{32,0},{64,96},{96,64},{128,160},{160,128},{192,224},{224,1... | collective-permute-start | bytes 1769480 | tf_op jit(solution)/shard_map/ppermute | solution.py:380
  54.9 3.5 %collective-permute-start.8 = (bf16[4,48,768]{2,1,0:T(8,128)(2,1)S(1)}, bf16[4,48,768]{2,1,0:T(8,128)(2,1)S(1)}, u32[]{:S(2)}, u32[]{:S(2)}) collective-permute-start(bf16[4,48,768]{2,1,0:T(8,128)(2,1)S(1)} %collective-permute-done.7.refs_12_.refs_9_), channel_id=1, source_target_pairs={{0,32},{32,0},{64,96},{96,64},{128,160},{160,128},{192,224},{224,1... | collective-permute-start | bytes 884744 | tf_op jit(solution)/shard_map/ppermute | solution.py:380
  57.2 1.6 %collective-permute-start.10 = (bf16[4,48,768]{2,1,0:T(8,128)(2,1)S(1)}, bf16[4,48,768]{2,1,0:T(8,128)(2,1)S(1)}, u32[]{:S(2)}, u32[]{:S(2)}) collective-permute-start(bf16[4,48,768]{2,1,0:T(8,128)(2,1)S(1)} %collective-permute-done.9.refs_14_.refs_11_), channel_id=1, source_target_pairs={{0,32},{32,0},{64,96},{96,64},{128,160},{160,128},{192,224},{224,1... | collective-permute-start | bytes 884744 | tf_op jit(solution)/shard_map/ppermute | solution.py:380
  74.1 21.3 %all-to-all-start.1 = ((bf16[32,48,128]{2,1,0:T(8,128)(2,1)}), bf16[32,48,128]{2,1,0:T(8,128)(2,1)S(1)}, u32[]{:S(2)}, u32[]{:S(2)}) async-start(bf16[32,48,128]{2,1,0:T(8,128)(2,1)} %bitcast.6), calls=%async_computation.1 | async-start | bytes 786432 | tf_op jit(solution)/shard_map/all_to_all | solution.py:434
  81.5 39.5 %copy-start.14 = (f32[8,4,48]{2,1,0:T(4,128)S(1)}, f32[8,4,48]{2,1,0:T(4,128)}, u32[]{:S(2)}) copy-start(f32[8,4,48]{2,1,0:T(4,128)} %param.16) | copy-start | bytes 18436
  81.5 39.5 %copy-start.16 = (f32[8]{0:T(128)S(1)}, f32[8]{0:T(128)}, u32[]{:S(2)}) copy-start(f32[8]{0:T(128)} %param.17) | copy-start | bytes 100
  113.7 12.0 %all-to-all-start.3 = ((f32[8,4,128]{2,1,0:T(4,128)}), f32[8,4,128]{2,1,0:T(4,128)S(1)}, u32[]{:S(2)}, u32[]{:S(2)}) async-start(f32[8,4,128]{2,1,0:T(4,128)} %clip.1), calls=%async_computation.3 | async-start | bytes 32768 | tf_op jit(solution)/shard_map/all_to_all | solution.py:441
  (9 other events, 23.2 us)

commit v4 on v3

--- a/solution.py
+++ b/solution.py
@@ -296,77 +296,101 @@
     )(scalars, *hiddens, *whole.pieces)
 
 
-def sums_body(scalars, parts, sums, norms, chosen):
+def sums_body(scalars, parts, norms, *rest):
+    outs, (chosen, shares) = rest[:-2], rest[-2:]
     senders, channels, lanes = parts.shape
-    utts = UTTS
+    groups = len(outs)
     per = lanes // SLOTS
     blk = lax.broadcasted_iota(jnp.int32, (senders, lanes), 0) * per + (
         lax.broadcasted_iota(jnp.int32, (senders, lanes), 1) // SLOTS
     )
     utt_of, cumul = jnp.zeros((senders, lanes), jnp.int32), jnp.int32(0)
-    for i in range(utts):
+    for i in range(UTTS):
         cumul = cumul + scalars[i]
         utt_of = utt_of + (cumul <= blk).astype(jnp.int32)
-    for u in range(utts):
+    for u in range(UTTS):
         chosen[u] = jnp.where(utt_of == u, 1.0, 0.0)
     spot = lax.broadcasted_iota(jnp.int32, (1, lanes), 1)
     row = jnp.zeros((1, lanes), jnp.float32)
-    totals = [jnp.zeros((channels, lanes), jnp.float32) for _ in range(utts)]
-    for s in range(senders):
-        part = parts[s].astype(jnp.float32)
-        for u in range(utts):
-            totals[u] = totals[u] + chosen[u, s : s + 1] * part
-    for u in range(utts):
-        total = totals[u]
-        total = total + pltpu.roll(total, 64, 1)
-        total = total + pltpu.roll(total, 32, 1)
-        sums[u] = total
-        square = jnp.sum(jnp.sum(total * total, axis=0, keepdims=True), axis=1, keepdims=True)
-        row = row + jnp.where(spot == u, square * (1.0 / per), 0.0)
+    rest = jnp.zeros((lanes - channels, lanes), jnp.float32)
+    for few in range(0, UTTS, 4):
+        totals = [jnp.zeros((channels, lanes), jnp.float32) for _ in range(4)]
+        for s in range(senders):
+            part = parts[s].astype(jnp.float32)
+            for u in range(4):
+                totals[u] = totals[u] + chosen[few + u, s : s + 1] * part
+        for u in range(4):
+            turned = jnp.concatenate([totals[u], rest], axis=0).T
+            total = turned[:SLOTS]
+            for i in range(1, per):
+                total = total + turned[i * SLOTS : (i + 1) * SLOTS]
+            rows = SLOTS // groups
+            at = (few + u) * rows
+            shares[:, at : at + rows, :] = total.reshape(groups, rows, lanes)
+            square = jnp.sum(jnp.sum(total * total, axis=0, keepdims=True), axis=1, keepdims=True)
+            row = row + jnp.where(spot == few + u, square, 0.0)
     norms[...] = jnp.broadcast_to(row[None], norms.shape)
-
-
-def sums_and_norms(scalars, parts):
+    for k, out in enumerate(outs):
+        out[...] = shares[scalars[2 * UTTS + 3] ^ k]
+
+
+def sums_and_norms(scalars, parts, groups):
     senders, channels, lanes = parts.shape
     whole = lambda shape: pl.BlockSpec(shape, lambda c: (0, 0, 0))
+    rows = UTTS * SLOTS // groups
+    norms = (groups * senders, 1, lanes)
     return pl.pallas_call(
         sums_body,
         grid=(1,),
         in_specs=[pl.BlockSpec(memory_space=pltpu.SMEM), whole(parts.shape)],
-        out_specs=[whole((UTTS, channels, lanes)), whole((senders, 1, lanes))],
-        out_shape=[
-            jax.ShapeDtypeStruct((UTTS, channels, lanes), jnp.float32),
-            jax.ShapeDtypeStruct((senders, 1, lanes), jnp.float32),
+        out_specs=[whole(norms)] + [pl.BlockSpec((rows, lanes), lambda c: (0, 0))] * groups,
+        out_shape=[jax.ShapeDtypeStruct(norms, jnp.float32)]
+        + [jax.ShapeDtypeStruct((rows, lanes), jnp.float32)] * groups,
+        scratch_shapes=[
+            pltpu.VMEM((UTTS, senders, lanes), jnp.float32),
+            pltpu.VMEM((groups, rows, lanes), jnp.float32),
         ],
-        scratch_shapes=[pltpu.VMEM((UTTS, senders, lanes), jnp.float32)],
+        compiler_params=pltpu.CompilerParams(vmem_limit_bytes=VMEM),
         name="sums",
     )(scalars, parts)
 
 
-def clip_body(clip_bound, sums, norms, out):
-    utts, channels, lanes = sums.shape
-    square = jnp.sum(norms[...], axis=0)
-    factor = clip_bound / jnp.maximum(jnp.sqrt(square), clip_bound)
-    spot = lax.broadcasted_iota(jnp.int32, (1, lanes), 1)
-    total = jnp.zeros((channels, lanes), jnp.float32)
-    for u in range(utts):
-        own = jnp.sum(jnp.where(spot == u, factor, 0.0), axis=1, keepdims=True)
-        total = total + own * sums[u]
-    wide = jnp.concatenate([total, jnp.zeros((lanes - channels, lanes), jnp.float32)], axis=0).T
-    groups, rows, _ = out.shape
-    for g in range(groups):
-        out[g] = wide[g * rows : (g + 1) * rows]
-
-
-def clipped(sums, norms, clip_bound, groups):
-    vmem = pl.BlockSpec(memory_space=pltpu.VMEM)
+def finish_body(clip_bound, scalars, coef, norms, draws, *rest):
+    shares, out = rest[:-1], rest[-1]
+    groups, (rows, lanes) = len(shares), shares[0].shape
+    senders = norms.shape[0] // groups
+    taps, channels = out.shape
+    owner = lax.broadcasted_iota(jnp.int32, (rows, lanes), 0) // taps
+    mine = owner == lax.broadcasted_iota(jnp.int32, (rows, lanes), 1)
+    total = jnp.zeros((rows, lanes), jnp.float32)
+    for k in range(groups):
+        start = (scalars[2 * UTTS + 3] ^ k) * senders
+        square = jnp.sum(norms[pl.ds(start, senders)], axis=0)
+        factor = clip_bound / jnp.maximum(jnp.sqrt(square), clip_bound)
+        own = jnp.sum(jnp.where(mine, factor, 0.0), axis=1, keepdims=True)
+        total = total + own * shares[k][...]
+    clipped = total[:taps]
+    for u in range(1, UTTS):
+        clipped = clipped + total[u * taps : (u + 1) * taps]
+    mixture = coef[0] * draws[0]
+    for j in range(1, draws.shape[0]):
+        mixture = mixture + coef[j] * draws[j]
+    out[...] = (clipped[:, :channels] + 0.1 * clip_bound * mixture) / (UTTS * groups)
+
+
+def finish(scalars, coef, shares, norms, draws, clip_bound):
+    whole = lambda shape: pl.BlockSpec(shape, lambda c: (0,) * len(shape))
+    out = draws.shape[1:]
     return pl.pallas_call(
-        lambda *refs: clip_body(clip_bound, *refs),
-        in_specs=[vmem, vmem],
-        out_specs=vmem,
-        out_shape=jax.ShapeDtypeStruct((groups, SLOTS // groups, LANES), jnp.float32),
-        name="clip",
-    )(sums, norms)
+        lambda *refs: finish_body(clip_bound, *refs),
+        grid=(1,),
+        in_specs=[pl.BlockSpec(memory_space=pltpu.SMEM)] * 2
+        + [whole(array.shape) for array in (norms, draws, *shares)],
+        out_specs=whole(out),
+        out_shape=jax.ShapeDtypeStruct(out, jnp.float32),
+        compiler_params=pltpu.CompilerParams(vmem_limit_bytes=VMEM),
+        name="finish",
+    )(scalars, coef, norms, draws, *shares)
 
 
 def row_moves(shards, groups):
@@ -402,10 +426,11 @@
     shards = lax.axis_size("tm")
     groups = lax.axis_size("utt")
     device = lax.axis_index("tm").astype(jnp.int32)
-    core = lax.axis_index("utt").astype(jnp.int32) % 2
+    group = lax.axis_index("utt").astype(jnp.int32)
+    core = group % 2
     col = device % COLS
     scalars = jnp.concatenate(
-        [blocks[0], last_fill[0], jnp.stack([device * blk_count, col, core])]
+        [blocks[0], last_fill[0], jnp.stack([device * blk_count, col, core, group])]
     )
     swapped, shifted = row_moves(shards, groups)
     half = width // 2
@@ -434,14 +459,12 @@
     parts = lax.all_to_all(parts, "tm", 0, 0, tiled=True)
     block_out = project(scalars, [inner, outer], [hidden_in, hidden_out], whole)
     parts, block_out = lax.optimization_barrier((parts, block_out))
-    sums, norms = sums_and_norms(scalars, parts)
-    norms = lax.all_to_all(norms, "tm", 0, 0, tiled=True)
-    clip_bound = 300.0 * math.sqrt(width)
-    contrib = clipped(sums, norms, clip_bound, groups)
-    contrib = lax.all_to_all(contrib, "utt", 0, 0, tiled=True)
-    own_share = jnp.sum(contrib, axis=0)[:, : width // shards]
-    mixture = jnp.sum(band_coef[:, None, None] * noise_draws, axis=0)
-    mean_grad = (own_share + 0.1 * clip_bound * mixture) / (UTTS * groups)
+    norms, *shares = sums_and_norms(scalars, parts, groups)
+    norms = lax.all_to_all(norms, ("utt", "tm"), 0, 0, tiled=True)
+    shares = shares[:1] + [
+        lax.ppermute(shares[k], "utt", [(g, g ^ k) for g in range(groups)]) for k in range(1, groups)
+    ]
+    mean_grad = finish(scalars, band_coef, shares, norms, noise_draws, 300.0 * math.sqrt(width))
     return (block_out, mean_grad)
 
 

time: 127 us -> 125 us (0.984)
  blocking collectives: 13.5 us -> 0 us
  starting transfers between devices: 39.1 us -> 49.1 us
  waiting for transfers between devices: 27.3 us -> 28.9 us
    all_to_all x1 -> x0, blocking collectives: 13.5 us -> none  [per_device(): norms = lax.all_to_all(norms, 'tm', 0, 0, tiled=True)]
    ppermute x0 -> x7, starting transfers between devices: none -> 10.2 us  [per_device(): lax.ppermute(shares[k], 'utt', [(g, g ^ k) for g in range(groups)])]
    all_to_all x1, waiting for transfers between devices: 4.56 us -> 0.01 us  [per_device(): norms = lax.all_to_all(norms, ('utt', 'tm'), 0, 0, tiled=True)]
    ppermute x4, waiting for transfers between devices: 9.02 us -> 13.4 us  [shifted(): return lax.ppermute(value, 'tm', pairs)]
    ppermute x0 -> x7, waiting for transfers between devices: none -> 2.79 us  [per_device(): lax.ppermute(shares[k], 'utt', [(g, g ^ k) for g in range(groups)])]
    all_to_all x1, starting transfers between devices: 7.32 us -> 9.52 us  [per_device(): norms = lax.all_to_all(norms, ('utt', 'tm'), 0, 0, tiled=True)]
    all_to_all x1, starting transfers between devices: 7.39 us -> 5.42 us  [per_device(): parts = lax.all_to_all(parts, 'tm', 0, 0, tiled=True)]
    ppermute x4, starting transfers between devices: 5.51 us -> 3.93 us  [shifted(): return lax.ppermute(value, 'tm', pairs)]
  transfers between devices with their start and end apart: 14 -> 21, of which waited for: 7 -> 9; matrix products, arithmetic and copies ran while one was open for 2% -> 2% of each run, Pallas kernels for 17% -> 17%
where the time goes in v4:
time: 125 us
  starting transfers between devices  49.1 us (39%)
  Pallas kernels  39.3 us (31%)
  waiting for transfers between devices  28.9 us (23%)
  local copies, waits for them, and re-layouts  6.39 us (5%)
    pallas_call x1, Pallas kernels, grads(): pl.pallas_call(lambda *refs: grads_body(whole, orders, *refs), in_specs=[...  14.1 us
    ppermute x4, waiting for transfers between devices, shifted(): return lax.ppermute(value, 'tm', pairs)  13.4 us
    pallas_call x2, Pallas kernels, conv(): pl.pallas_call(lambda *refs: conv_body(blks, *refs), grid=(width // STEP,...  13.2 us
    ppermute x7, starting transfers between devices, per_device(): lax.ppermute(shares[k], 'utt', [(g, g ^ k) for g in range(groups)])  10.2 us
    all_to_all x1, starting transfers between devices, per_device(): norms = lax.all_to_all(norms, ('utt', 'tm'), 0, 0, tiled=True)  9.52 us
    all_to_all x1, starting transfers between devices, column_rows(): lax.all_to_all(jnp.broadcast_to(own[None], (depth,) + own.shape), 'tm', 0...  9.01 us
    pallas_call x1, Pallas kernels, project(): pl.pallas_call(lambda *refs: project_body(whole, orders, *refs), grid=(wi...  7.7 us
    all_to_all x1, waiting for transfers between devices, per_device(): parts = lax.all_to_all(parts, 'tm', 0, 0, tiled=True)  6.17 us
  transfers between devices with their start and end apart: 21, of which 9 were waited for; matrix products, arithmetic and copies ran while one was open for 2% of the time, Pallas kernels for 17%

profile of v4, /device:TPU:1, one launch (start us, length us, event | category | flops | bytes accessed | tf_op | source)
XLA Modules:
  0.0 124.6 jit_solution(15907414943523076398)
XLA Ops:
  2.4 9.0 %all-to-all-start = ((bf16[8,48,768]{2,1,0:T(8,128)(2,1)}), bf16[8,48,768]{2,1,0:T(8,128)(2,1)S(1)}, u32[]{:S(2)}, u32[]{:S(2)}) async-start(bf16[8,48,768]{2,1,0:T(8,128)(2,1)} %broadcast_in_dim.10), calls=%async_computation | async-start | bytes 1179648 | tf_op jit(solution)/shard_map/all_to_all | solution.py:411
  13.6 4.0 %collective-permute-start = (bf16[16,1536]{1,0:T(8,128)(2,1)S(1)}, bf16[16,1536]{1,0:T(8,128)(2,1)S(1)}, u32[]{:S(2)}, u32[]{:S(2)}) collective-permute-start(bf16[16,1536]{1,0:T(8,128)(2,1)S(1)} %get-tuple-element.53), channel_id=1, source_target_pairs={{0,1},{1,2},{2,3},{3,4},{4,5},{5,6},{6,7},{7,8},{8,9},{9,10},{10,1... | collective-permute-start | bytes 147464 | tf_op jit(solution)/shard_map/ppermute | solution.py:440
  18.8 6.6 %conv.2 = (bf16[256,1536]{1,0:T(8,128)(2,1)}, bf16[12,256,128]{2,1,0:T(8,128)(2,1)}, f32[12,2,160,128]{3,2,1,0:T(8,128)}) custom-call(s32[20]{0:T(128)} %concatenate.3.refs_0_.scalars, bf16[512,1536]{1,0:T(8,128)(2,1)} %refs_1_.5, f32[31,1536]{1,0:T(8,128)} %refs_4_.1, f32[1,1536]{1,0:T(1,128)} %broadcast_in_dim.4.refs_3_.refs_5_), custom_call_target="tpu_custom_call" | custom-call | flops 25165824 | bytes 15728640 | tf_op jit(solution)/shard_map/conv/pallas_call | solution.py:77
  25.5 5.3 %all-to-all-done.refs_6_.refs_3_ = bf16[8,48,768]{2,1,0:T(8,128)(2,1)S(1)} async-done(((bf16[8,48,768]{2,1,0:T(8,128)(2,1)}), bf16[8,48,768]{2,1,0:T(8,128)(2,1)S(1)}, u32[]{:S(2)}, u32[]{:S(2)}) %all-to-all-start) | async-done | bytes 589856 | tf_op jit(solution)/shard_map/all_to_all | solution.py:411
  31.3 2.3 %collective-permute-start.3 = (bf16[8,48,768]{2,1,0:T(8,128)(2,1)S(1)}, bf16[8,48,768]{2,1,0:T(8,128)(2,1)S(1)}, u32[]{:S(2)}, u32[]{:S(2)}) collective-permute-start(bf16[8,48,768]{2,1,0:T(8,128)(2,1)S(1)} %all-to-all-done.refs_6_.refs_3_), channel_id=1, source_target_pairs={{0,3},{1,0},{2,1},{3,2},{4,7},{5,4},{6,5},{7,6},{8,11},{9,8},{10,9... | collective-permute-start | bytes 1769480 | tf_op jit(solution)/shard_map/ppermute | solution.py:401
  33.6 6.5 %conv.3 = (bf16[256,1536]{1,0:T(8,128)(2,1)}, bf16[12,256,128]{2,1,0:T(8,128)(2,1)}, f32[12,2,160,128]{3,2,1,0:T(8,128)}) custom-call(s32[20]{0:T(128)} %concatenate.3.refs_0_.scalars, bf16[512,1536]{1,0:T(8,128)(2,1)} %refs_1_.5, bf16[16,1536]{1,0:T(8,128)(2,1)} %copy-done.14, bf16[16,1536]{1,0:T(8,128)(2,1)} %copy-done.13, f32[31,1536]{1,0:T(8,128)} %refs_4_.1, ...), custom_call_target="tpu_custom_call" | custom-call | flops 25165824 | bytes 15728640 | tf_op jit(solution)/shard_map/conv/pallas_call | solution.py:77
  40.2 6.2 %collective-permute-done.3.refs_10_.refs_7_ = bf16[8,48,768]{2,1,0:T(8,128)(2,1)S(1)} collective-permute-done((bf16[8,48,768]{2,1,0:T(8,128)(2,1)S(1)}, bf16[8,48,768]{2,1,0:T(8,128)(2,1)S(1)}, u32[]{:S(2)}, u32[]{:S(2)}) %collective-permute-start.3) | collective-permute-done | bytes 589856 | tf_op jit(solution)/shard_map/ppermute | solution.py:401
  46.4 3.1 %collective-permute-done.2.refs_8_.refs_5_ = bf16[8,48,768]{2,1,0:T(8,128)(2,1)S(1)} collective-permute-done((bf16[8,48,768]{2,1,0:T(8,128)(2,1)S(1)}, bf16[8,48,768]{2,1,0:T(8,128)(2,1)S(1)}, u32[]{:S(2)}, u32[]{:S(2)}) %collective-permute-start.2) | collective-permute-done | bytes 589856 | tf_op jit(solution)/shard_map/ppermute | solution.py:401
  51.1 1.7 %collective-permute-start.5 = (bf16[8,48,768]{2,1,0:T(8,128)(2,1)S(1)}, bf16[8,48,768]{2,1,0:T(8,128)(2,1)S(1)}, u32[]{:S(2)}, u32[]{:S(2)}) collective-permute-start(bf16[8,48,768]{2,1,0:T(8,128)(2,1)S(1)} %collective-permute-done.2.refs_8_.refs_5_), channel_id=1, source_target_pairs={{0,32},{32,0},{64,96},{96,64},{128,160},{160,128},{192,224},{224,1... | collective-permute-start | bytes 1769480 | tf_op jit(solution)/shard_map/ppermute | solution.py:404
  52.8 4.2 %collective-permute-done.9.refs_14_.refs_11_ = bf16[4,48,768]{2,1,0:T(8,128)(2,1)S(1)} collective-permute-done((bf16[4,48,768]{2,1,0:T(8,128)(2,1)S(1)}, bf16[4,48,768]{2,1,0:T(8,128)(2,1)S(1)}, u32[]{:S(2)}, u32[]{:S(2)}) %collective-permute-start.9) | collective-permute-done | bytes 294944 | tf_op jit(solution)/shard_map/ppermute | solution.py:401
  57.0 2.0 %collective-permute-start.10 = (bf16[4,48,768]{2,1,0:T(8,128)(2,1)S(1)}, bf16[4,48,768]{2,1,0:T(8,128)(2,1)S(1)}, u32[]{:S(2)}, u32[]{:S(2)}) collective-permute-start(bf16[4,48,768]{2,1,0:T(8,128)(2,1)S(1)} %collective-permute-done.9.refs_14_.refs_11_), channel_id=1, source_target_pairs={{0,32},{32,0},{64,96},{96,64},{128,160},{160,128},{192,224},{224,1... | collective-permute-start | bytes 884744 | tf_op jit(solution)/shard_map/ppermute | solution.py:404
  59.0 1.6 %collective-permute-start.8 = (bf16[4,48,768]{2,1,0:T(8,128)(2,1)S(1)}, bf16[4,48,768]{2,1,0:T(8,128)(2,1)S(1)}, u32[]{:S(2)}, u32[]{:S(2)}) collective-permute-start(bf16[4,48,768]{2,1,0:T(8,128)(2,1)S(1)} %collective-permute-done.7.refs_12_.refs_9_), channel_id=1, source_target_pairs={{0,32},{32,0},{64,96},{96,64},{128,160},{160,128},{192,224},{224,1... | collective-permute-start | bytes 884744 | tf_op jit(solution)/shard_map/ppermute | solution.py:404
  63.0 14.1 %grads.1 = bf16[1536,128]{1,0:T(8,128)(2,1)} custom-call(s32[20]{0:T(128)} %concatenate.3.refs_0_.scalars, bf16[512,1536]{1,0:T(8,128)(2,1)} %refs_1_.6, bf16[12,256,128]{2,1,0:T(8,128)(2,1)} %get-tuple-element.27.refs_2_, f32[12,2,160,128]{3,2,1,0:T(8,128)} %get-tuple-element.28.refs_3_, bf16[12,256,128]{2,1,0:T(8,128)(2,1)} %get-tuple-element.32.refs_4_, ...), custom_call_target="tpu_custom_call" | custom-call | flops 2415919104 | bytes 15728640 | tf_op jit(solution)/shard_map/grads/pallas_call | solution.py:234
  77.1 5.4 %all-to-all-start.1 = ((bf16[32,48,128]{2,1,0:T(8,128)(2,1)}), bf16[32,48,128]{2,1,0:T(8,128)(2,1)S(1)}, u32[]{:S(2)}, u32[]{:S(2)}) async-start(bf16[32,48,128]{2,1,0:T(8,128)(2,1)} %bitcast.7), calls=%async_computation.1 | async-start | bytes 786432 | tf_op jit(solution)/shard_map/all_to_all | solution.py:459
  82.5 7.7 %project.1 = bf16[512,1536]{1,0:T(8,128)(2,1)} custom-call(s32[20]{0:T(128)} %concatenate.3.refs_0_.scalars, bf16[256,1536]{1,0:T(8,128)(2,1)} %get-tuple-element.39.refs_1_, bf16[256,1536]{1,0:T(8,128)(2,1)} %get-tuple-element.40.refs_2_, bf16[8,48,768]{2,1,0:T(8,128)(2,1)} %copy-done.1, bf16[8,48,768]{2,1,0:T(8,128)(2,1)} %copy-done.5, ...), custom_call_target="tpu_custom_call" | custom-call | flops 2415919104 | bytes 7864320 | tf_op jit(solution)/shard_map/project/pallas_call | solution.py:282
  90.3 6.2 %all-to-all-done.1.parts = bf16[32,48,128]{2,1,0:T(8,128)(2,1)S(1)} async-done(((bf16[32,48,128]{2,1,0:T(8,128)(2,1)}), bf16[32,48,128]{2,1,0:T(8,128)(2,1)S(1)}, u32[]{:S(2)}, u32[]{:S(2)}) %all-to-all-start.1) | async-done | bytes 393248 | tf_op jit(solution)/shard_map/all_to_all | solution.py:459
  97.2 2.5 %sums.1 = (f32[256,1,128]{2,1,0:T(1,128)}, f32[32,128]{1,0:T(8,128)}, f32[32,128]{1,0:T(8,128)}, f32[32,128]{1,0:T(8,128)}, f32[32,128]{1,0:T(8,128)}, /*index=5...) custom-call(s32[20]{0:T(128)} %concatenate.3.refs_0_.scalars, bf16[32,48,128]{2,1,0:T(8,128)(2,1)} %copy-done.2), custom_call_target="tpu_custom_call" | custom-call | tf_op jit(solution)/shard_map/sums/pallas_call | solution.py:342
  99.7 9.5 %all-to-all-start.2 = ((f32[256,1,128]{2,1,0:T(1,128)}), f32[256,1,128]{2,1,0:T(1,128)S(1)}, u32[]{:S(2)}, u32[]{:S(2)}) async-start(f32[256,1,128]{2,1,0:T(1,128)} %get-tuple-element.43), calls=%async_computation.2 | async-start | bytes 262144 | tf_op jit(solution)/shard_map/all_to_all | solution.py:463
  109.2 2.2 %collective-permute-start.11 = (f32[32,128]{1,0:T(8,128)}, f32[32,128]{1,0:T(8,128)S(1)}, u32[]{:S(2)}, u32[]{:S(2)}) collective-permute-start(f32[32,128]{1,0:T(8,128)} %get-tuple-element.45), channel_id=1, source_target_pairs={{0,32},{32,0},{64,96},{96,64},{128,160},{160,128},{192,224},{224,1... | collective-permute-start | bytes 49160 | tf_op jit(solution)/shard_map/ppermute | solution.py:465
  111.4 1.7 %collective-permute-start.13 = (f32[32,128]{1,0:T(8,128)}, f32[32,128]{1,0:T(8,128)S(1)}, u32[]{:S(2)}, u32[]{:S(2)}) collective-permute-start(f32[32,128]{1,0:T(8,128)} %get-tuple-element.47), channel_id=1, source_target_pairs={{0,96},{32,64},{64,32},{96,0},{128,224},{160,192},{192,160},{224,1... | collective-permute-start | bytes 49160 | tf_op jit(solution)/shard_map/ppermute | solution.py:465
  114.3 2.1 %collective-permute-start.15 = (f32[32,128]{1,0:T(8,128)}, f32[32,128]{1,0:T(8,128)S(1)}, u32[]{:S(2)}, u32[]{:S(2)}) collective-permute-start(f32[32,128]{1,0:T(8,128)} %get-tuple-element.49), channel_id=1, source_target_pairs={{0,160},{32,128},{64,224},{96,192},{128,32},{160,0},{192,96},{224,... | collective-permute-start | bytes 49160 | tf_op jit(solution)/shard_map/ppermute | solution.py:465
  117.3 2.1 %collective-permute-start.17 = (f32[32,128]{1,0:T(8,128)}, f32[32,128]{1,0:T(8,128)S(1)}, u32[]{:S(2)}, u32[]{:S(2)}) collective-permute-start(f32[32,128]{1,0:T(8,128)} %get-tuple-element.51), channel_id=1, source_target_pairs={{0,224},{32,192},{64,160},{96,128},{128,96},{160,64},{192,32},{224... | collective-permute-start | bytes 49160 | tf_op jit(solution)/shard_map/ppermute | solution.py:465
  120.8 1.4 %collective-permute-done.17.refs_11_ = f32[32,128]{1,0:T(8,128)S(1)} collective-permute-done((f32[32,128]{1,0:T(8,128)}, f32[32,128]{1,0:T(8,128)S(1)}, u32[]{:S(2)}, u32[]{:S(2)}) %collective-permute-start.17) | collective-permute-done | bytes 16416 | tf_op jit(solution)/shard_map/ppermute | solution.py:465
  122.8 1.8 %finish.1 = f32[4,48]{1,0:T(4,128)} custom-call(s32[20]{0:T(128)} %concatenate.3.refs_0_.scalars, f32[8]{0:T(128)} %refs_1_.7, f32[256,1,128]{2,1,0:T(1,128)} %copy-done.8, f32[8,4,48]{2,1,0:T(4,128)} %refs_3_.1, f32[32,128]{1,0:T(8,128)} %get-tuple-element.44.refs_4_, f32[32,128]{1,0:T(8,128)} %copy-done.15, f32[32,128]{1,0:T(8,128)} %copy-done.16, ...), custom_call_target="tpu_custom_call" | custom-call | tf_op jit(solution)/shard_map/finish/pallas_call | solution.py:384
  (81 shorter events, 14.4 us)
Async XLA Ops:
  0.7 17.5 %copy-start.24 = (s32[1,8]{1,0:T(1,128)S(1)}, s32[1,8]{1,0:T(1,128)}, u32[]{:S(2)}) copy-start(s32[1,8]{1,0:T(1,128)} %param.15) | copy-start | bytes 100
  2.4 28.4 %all-to-all-start = ((bf16[8,48,768]{2,1,0:T(8,128)(2,1)}), bf16[8,48,768]{2,1,0:T(8,128)(2,1)S(1)}, u32[]{:S(2)}, u32[]{:S(2)}) async-start(bf16[8,48,768]{2,1,0:T(8,128)(2,1)} %broadcast_in_dim.10), calls=%async_computation | async-start | bytes 1179648 | tf_op jit(solution)/shard_map/all_to_all | solution.py:411
  12.3 13.2 %collective-permute-start.1 = (bf16[16,1536]{1,0:T(8,128)(2,1)S(1)}, bf16[16,1536]{1,0:T(8,128)(2,1)S(1)}, u32[]{:S(2)}, u32[]{:S(2)}) collective-permute-start(bf16[16,1536]{1,0:T(8,128)(2,1)S(1)} %get-tuple-element.52), channel_id=1, source_target_pairs={{1,0},{2,1},{3,2},{4,3},{5,4},{6,5},{7,6},{8,7},{9,8},{10,9},{11,1... | collective-permute-start | bytes 147464 | tf_op jit(solution)/shard_map/ppermute | solution.py:441
  13.6 11.9 %collective-permute-start = (bf16[16,1536]{1,0:T(8,128)(2,1)S(1)}, bf16[16,1536]{1,0:T(8,128)(2,1)S(1)}, u32[]{:S(2)}, u32[]{:S(2)}) collective-permute-start(bf16[16,1536]{1,0:T(8,128)(2,1)S(1)} %get-tuple-element.53), channel_id=1, source_target_pairs={{0,1},{1,2},{2,3},{3,4},{4,5},{5,6},{6,7},{7,8},{8,9},{9,10},{10,1... | collective-permute-start | bytes 147464 | tf_op jit(solution)/shard_map/ppermute | solution.py:440
  30.8 31.9 %copy-start.1 = (bf16[8,48,768]{2,1,0:T(8,128)(2,1)}, bf16[8,48,768]{2,1,0:T(8,128)(2,1)S(1)}, u32[]{:S(2)}) copy-start(bf16[8,48,768]{2,1,0:T(8,128)(2,1)S(1)} %all-to-all-done.refs_6_.refs_3_) | copy-start | bytes 1769476
  30.8 9.4 %collective-permute-start.4 = (bf16[8,48,768]{2,1,0:T(8,128)(2,1)S(1)}, bf16[8,48,768]{2,1,0:T(8,128)(2,1)S(1)}, u32[]{:S(2)}, u32[]{:S(2)}) collective-permute-start(bf16[8,48,768]{2,1,0:T(8,128)(2,1)S(1)} %all-to-all-done.refs_6_.refs_3_), channel_id=1, source_target_pairs={{0,32},{32,0},{64,96},{96,64},{128,160},{160,128},{192,224},{224,1... | collective-permute-start | bytes 1769480 | tf_op jit(solution)/shard_map/ppermute | solution.py:404
  31.3 15.1 %collective-permute-start.3 = (bf16[8,48,768]{2,1,0:T(8,128)(2,1)S(1)}, bf16[8,48,768]{2,1,0:T(8,128)(2,1)S(1)}, u32[]{:S(2)}, u32[]{:S(2)}) collective-permute-start(bf16[8,48,768]{2,1,0:T(8,128)(2,1)S(1)} %all-to-all-done.refs_6_.refs_3_), channel_id=1, source_target_pairs={{0,3},{1,0},{2,1},{3,2},{4,7},{5,4},{6,5},{7,6},{8,11},{9,8},{10,9... | collective-permute-start | bytes 1769480 | tf_op jit(solution)/shard_map/ppermute | solution.py:401
  33.6 15.9 %collective-permute-start.2 = (bf16[8,48,768]{2,1,0:T(8,128)(2,1)S(1)}, bf16[8,48,768]{2,1,0:T(8,128)(2,1)S(1)}, u32[]{:S(2)}, u32[]{:S(2)}) collective-permute-start(bf16[8,48,768]{2,1,0:T(8,128)(2,1)S(1)} %all-to-all-done.refs_6_.refs_3_), channel_id=1, source_target_pairs={{0,1},{1,2},{2,3},{3,0},{4,5},{5,6},{6,7},{7,4},{8,9},{9,10},{10,1... | collective-permute-start | bytes 1769480 | tf_op jit(solution)/shard_map/ppermute | solution.py:401
  40.2 22.6 %copy-start.5 = (bf16[8,48,768]{2,1,0:T(8,128)(2,1)}, bf16[8,48,768]{2,1,0:T(8,128)(2,1)S(1)}, u32[]{:S(2)}) copy-start(bf16[8,48,768]{2,1,0:T(8,128)(2,1)S(1)} %collective-permute-done.4.refs_7_.refs_4_) | copy-start | bytes 1769476
  49.5 7.5 %collective-permute-start.9 = (bf16[4,48,768]{2,1,0:T(8,128)(2,1)S(1)}, bf16[4,48,768]{2,1,0:T(8,128)(2,1)S(1)}, u32[]{:S(2)}, u32[]{:S(2)}) collective-permute-start(bf16[4,48,768]{2,1,0:T(8,128)(2,1)S(1)} %slice.15), channel_id=1, source_target_pairs={{0,3},{1,0},{2,1},{3,2},{4,7},{5,4},{6,5},{7,6},{8,11},{9,8},{10,9... | collective-permute-start | bytes 884744 | tf_op jit(solution)/shard_map/ppermute | solution.py:401
  49.9 9.1 %collective-permute-start.7 = (bf16[4,48,768]{2,1,0:T(8,128)(2,1)S(1)}, bf16[4,48,768]{2,1,0:T(8,128)(2,1)S(1)}, u32[]{:S(2)}, u32[]{:S(2)}) collective-permute-start(bf16[4,48,768]{2,1,0:T(8,128)(2,1)S(1)} %slice.14), channel_id=1, source_target_pairs={{0,1},{1,2},{2,3},{3,0},{4,5},{5,6},{6,7},{7,4},{8,9},{9,10},{10,1... | collective-permute-start | bytes 884744 | tf_op jit(solution)/shard_map/ppermute | solution.py:401
  51.1 10.7 %collective-permute-start.5 = (bf16[8,48,768]{2,1,0:T(8,128)(2,1)S(1)}, bf16[8,48,768]{2,1,0:T(8,128)(2,1)S(1)}, u32[]{:S(2)}, u32[]{:S(2)}) collective-permute-start(bf16[8,48,768]{2,1,0:T(8,128)(2,1)S(1)} %collective-permute-done.2.refs_8_.refs_5_), channel_id=1, source_target_pairs={{0,32},{32,0},{64,96},{96,64},{128,160},{160,128},{192,224},{224,1... | collective-permute-start | bytes 1769480 | tf_op jit(solution)/shard_map/ppermute | solution.py:404
  52.8 9.1 %collective-permute-start.6 = (bf16[8,48,768]{2,1,0:T(8,128)(2,1)S(1)}, bf16[8,48,768]{2,1,0:T(8,128)(2,1)S(1)}, u32[]{:S(2)}, u32[]{:S(2)}) collective-permute-start(bf16[8,48,768]{2,1,0:T(8,128)(2,1)S(1)} %collective-permute-done.3.refs_10_.refs_7_), channel_id=1, source_target_pairs={{0,32},{32,0},{64,96},{96,64},{128,160},{160,128},{192,224},{224,1... | collective-permute-start | bytes 1769480 | tf_op jit(solution)/shard_map/ppermute | solution.py:404
  57.0 3.7 %collective-permute-start.10 = (bf16[4,48,768]{2,1,0:T(8,128)(2,1)S(1)}, bf16[4,48,768]{2,1,0:T(8,128)(2,1)S(1)}, u32[]{:S(2)}, u32[]{:S(2)}) collective-permute-start(bf16[4,48,768]{2,1,0:T(8,128)(2,1)S(1)} %collective-permute-done.9.refs_14_.refs_11_), channel_id=1, source_target_pairs={{0,32},{32,0},{64,96},{96,64},{128,160},{160,128},{192,224},{224,1... | collective-permute-start | bytes 884744 | tf_op jit(solution)/shard_map/ppermute | solution.py:404
  59.0 2.8 %collective-permute-start.8 = (bf16[4,48,768]{2,1,0:T(8,128)(2,1)S(1)}, bf16[4,48,768]{2,1,0:T(8,128)(2,1)S(1)}, u32[]{:S(2)}, u32[]{:S(2)}) collective-permute-start(bf16[4,48,768]{2,1,0:T(8,128)(2,1)S(1)} %collective-permute-done.7.refs_12_.refs_9_), channel_id=1, source_target_pairs={{0,32},{32,0},{64,96},{96,64},{128,160},{160,128},{192,224},{224,1... | collective-permute-start | bytes 884744 | tf_op jit(solution)/shard_map/ppermute | solution.py:404
  77.1 19.3 %all-to-all-start.1 = ((bf16[32,48,128]{2,1,0:T(8,128)(2,1)}), bf16[32,48,128]{2,1,0:T(8,128)(2,1)S(1)}, u32[]{:S(2)}, u32[]{:S(2)}) async-start(bf16[32,48,128]{2,1,0:T(8,128)(2,1)} %bitcast.7), calls=%async_computation.1 | async-start | bytes 786432 | tf_op jit(solution)/shard_map/all_to_all | solution.py:459
  99.7 22.5 %all-to-all-start.2 = ((f32[256,1,128]{2,1,0:T(1,128)}), f32[256,1,128]{2,1,0:T(1,128)S(1)}, u32[]{:S(2)}, u32[]{:S(2)}) async-start(f32[256,1,128]{2,1,0:T(1,128)} %get-tuple-element.43), calls=%async_computation.2 | async-start | bytes 262144 | tf_op jit(solution)/shard_map/all_to_all | solution.py:463
  109.2 7.3 %collective-permute-start.11 = (f32[32,128]{1,0:T(8,128)}, f32[32,128]{1,0:T(8,128)S(1)}, u32[]{:S(2)}, u32[]{:S(2)}) collective-permute-start(f32[32,128]{1,0:T(8,128)} %get-tuple-element.45), channel_id=1, source_target_pairs={{0,32},{32,0},{64,96},{96,64},{128,160},{160,128},{192,224},{224,1... | collective-permute-start | bytes 49160 | tf_op jit(solution)/shard_map/ppermute | solution.py:465
  111.4 5.9 %collective-permute-start.12 = (f32[32,128]{1,0:T(8,128)}, f32[32,128]{1,0:T(8,128)S(1)}, u32[]{:S(2)}, u32[]{:S(2)}) collective-permute-start(f32[32,128]{1,0:T(8,128)} %get-tuple-element.46), channel_id=1, source_target_pairs={{0,64},{32,96},{64,0},{96,32},{128,192},{160,224},{192,128},{224,1... | collective-permute-start | bytes 49160 | tf_op jit(solution)/shard_map/ppermute | solution.py:465
  111.4 8.0 %collective-permute-start.13 = (f32[32,128]{1,0:T(8,128)}, f32[32,128]{1,0:T(8,128)S(1)}, u32[]{:S(2)}, u32[]{:S(2)}) collective-permute-start(f32[32,128]{1,0:T(8,128)} %get-tuple-element.47), channel_id=1, source_target_pairs={{0,96},{32,64},{64,32},{96,0},{128,224},{160,192},{192,160},{224,1... | collective-permute-start | bytes 49160 | tf_op jit(solution)/shard_map/ppermute | solution.py:465
  113.1 6.2 %collective-permute-start.14 = (f32[32,128]{1,0:T(8,128)}, f32[32,128]{1,0:T(8,128)S(1)}, u32[]{:S(2)}, u32[]{:S(2)}) collective-permute-start(f32[32,128]{1,0:T(8,128)} %get-tuple-element.48), channel_id=1, source_target_pairs={{0,128},{32,160},{64,192},{96,224},{128,0},{160,32},{192,64},{224,... | collective-permute-start | bytes 49160 | tf_op jit(solution)/shard_map/ppermute | solution.py:465
  114.3 5.2 %collective-permute-start.15 = (f32[32,128]{1,0:T(8,128)}, f32[32,128]{1,0:T(8,128)S(1)}, u32[]{:S(2)}, u32[]{:S(2)}) collective-permute-start(f32[32,128]{1,0:T(8,128)} %get-tuple-element.49), channel_id=1, source_target_pairs={{0,160},{32,128},{64,224},{96,192},{128,32},{160,0},{192,96},{224,... | collective-permute-start | bytes 49160 | tf_op jit(solution)/shard_map/ppermute | solution.py:465
  116.4 4.3 %collective-permute-start.16 = (f32[32,128]{1,0:T(8,128)}, f32[32,128]{1,0:T(8,128)S(1)}, u32[]{:S(2)}, u32[]{:S(2)}) collective-permute-start(f32[32,128]{1,0:T(8,128)} %get-tuple-element.50), channel_id=1, source_target_pairs={{0,192},{32,224},{64,128},{96,160},{128,64},{160,96},{192,0},{224,... | collective-permute-start | bytes 49160 | tf_op jit(solution)/shard_map/ppermute | solution.py:465
  117.3 4.9 %collective-permute-start.17 = (f32[32,128]{1,0:T(8,128)}, f32[32,128]{1,0:T(8,128)S(1)}, u32[]{:S(2)}, u32[]{:S(2)}) collective-permute-start(f32[32,128]{1,0:T(8,128)} %get-tuple-element.51), channel_id=1, source_target_pairs={{0,224},{32,192},{64,160},{96,128},{128,96},{160,64},{192,32},{224... | collective-permute-start | bytes 49160 | tf_op jit(solution)/shard_map/ppermute | solution.py:465
  (22 other events, 118.3 us)

commit v5 on v4

--- a/solution.py
+++ b/solution.py
@@ -16,6 +16,7 @@
 COLS = 4
 UTTS = 8
 VMEM = 60 << 20
+SMALL = 8 << 20
 
 
 def block_facts(scalars, utts, index):
@@ -350,7 +351,7 @@
             pltpu.VMEM((UTTS, senders, lanes), jnp.float32),
             pltpu.VMEM((groups, rows, lanes), jnp.float32),
         ],
-        compiler_params=pltpu.CompilerParams(vmem_limit_bytes=VMEM),
+        compiler_params=pltpu.CompilerParams(vmem_limit_bytes=SMALL),
         name="sums",
     )(scalars, parts)
 
@@ -388,7 +389,7 @@
         + [whole(array.shape) for array in (norms, draws, *shares)],
         out_specs=whole(out),
         out_shape=jax.ShapeDtypeStruct(out, jnp.float32),
-        compiler_params=pltpu.CompilerParams(vmem_limit_bytes=VMEM),
+        compiler_params=pltpu.CompilerParams(vmem_limit_bytes=SMALL),
         name="finish",
     )(scalars, coef, norms, draws, *shares)
 
@@ -406,10 +407,30 @@
     return swapped, shifted
 
 
-def column_rows(own, shards):
+def spread_body(start, rows, out):
+    half = out.shape[2]
+    own = rows[:, pl.ds(pl.multiple_of(start[0], half), half)]
+    for z in range(out.shape[0]):
+        out[z] = own
+
+
+def column_rows(out_weight, core, shards):
     depth = shards // COLS
+    run, half = out_weight.shape[0], out_weight.shape[1] // 2
+    copies = pl.pallas_call(
+        spread_body,
+        grid=(1,),
+        in_specs=[
+            pl.BlockSpec(memory_space=pltpu.SMEM),
+            pl.BlockSpec((run, out_weight.shape[1]), lambda c: (0, 0)),
+        ],
+        out_specs=pl.BlockSpec((depth, run, half), lambda c: (0, 0, 0)),
+        out_shape=jax.ShapeDtypeStruct((depth, run, half), out_weight.dtype),
+        compiler_params=pltpu.CompilerParams(vmem_limit_bytes=VMEM),
+        name="spread",
+    )((core * half).reshape(1), out_weight)
     return lax.all_to_all(
-        jnp.broadcast_to(own[None], (depth,) + own.shape),
+        copies,
         "tm",
         0,
         0,
@@ -433,8 +454,7 @@
         [blocks[0], last_fill[0], jnp.stack([device * blk_count, col, core, group])]
     )
     swapped, shifted = row_moves(shards, groups)
-    half = width // 2
-    own = column_rows(lax.dynamic_slice_in_dim(out_weight, core * half, half, axis=1), shards)
+    own = column_rows(out_weight, core, shards)
     forward = [(i, i + 1) for i in range(shards - 1)]
     backward = [(target, source) for source, target in forward]
     low = lax.ppermute(glu_out[frames - RIM :], "tm", forward)
@@ -444,9 +464,9 @@
     hidden_in, *half_in = conv(inner, scalars, glu_out, [], kernel, bias)
     own, hidden_in, low, high = lax.optimization_barrier((own, hidden_in, low, high))
     below, above = shifted(own, 1), shifted(own, -1)
+    hidden_out, *half_out = conv(outer, scalars, glu_out, [low, high], kernel, bias)
+    own, below, above, hidden_out = lax.optimization_barrier((own, below, above, hidden_out))
     own_mate = swapped(own)
-    hidden_out, *half_out = conv(outer, scalars, glu_out, [low, high], kernel, bias)
-    below, above, own_mate, hidden_out = lax.optimization_barrier((below, above, own_mate, hidden_out))
     halves = [(inner, *half_in), (outer, *half_out)]
     mid = shards // COLS // 2
     far_low, far_high = shifted(below[:mid], 1), shifted(above[mid:], -1)

time: 125 us -> 120 us (0.960)
  waiting for transfers between devices: 28.9 us -> 25.5 us
  local copies, waits for them, and re-layouts: 6.39 us -> 3.5 us
    ppermute x4, waiting for transfers between devices: 13.4 us -> 10.2 us  [shifted(): return lax.ppermute(value, 'tm', pairs)]
    unnamed x50 -> x36, local copies, waits for them, and re-layouts: 3.4 us -> 1.35 us
    ppermute x5, starting transfers between devices: 5.81 us -> 7.59 us  [swapped(): return lax.ppermute(value, 'utt', [(i, i ^ 1) for i in range(groups)])]
    pallas_call x0 -> x1, Pallas kernels: none -> 1.77 us  [column_rows(): pl.pallas_call(spread_body, grid=(1,), in_specs=[pl.BlockSpec(memory_spac...]
    all_to_all x1, starting transfers between devices: 5.42 us -> 3.89 us  [per_device(): parts = lax.all_to_all(parts, 'tm', 0, 0, tiled=True)]
  transfers between devices with their start and end apart: 21 -> 21, of which waited for: 9 -> 8; matrix products, arithmetic and copies ran while one was open for 2% -> 2% of each run, Pallas kernels for 17% -> 18%
where the time goes in v5:
time: 120 us; the launch traced here: 119 us
  starting transfers between devices  49 us (41%)
  Pallas kernels  40.2 us (34%)
  waiting for transfers between devices  25.5 us (21%)
  local copies, waits for them, and re-layouts  3.5 us (3%)
    pallas_call x1, Pallas kernels, grads(): pl.pallas_call(lambda *refs: grads_body(whole, orders, *refs), in_specs=[...  14.1 us
    pallas_call x2, Pallas kernels, conv(): pl.pallas_call(lambda *refs: conv_body(blks, *refs), grid=(width // STEP,...  13.2 us
    ppermute x4, waiting for transfers between devices, shifted(): return lax.ppermute(value, 'tm', pairs)  10.2 us
    ppermute x7, starting transfers between devices, per_device(): lax.ppermute(shares[k], 'utt', [(g, g ^ k) for g in range(groups)])  10.2 us
    all_to_all x1, starting transfers between devices, per_device(): norms = lax.all_to_all(norms, ('utt', 'tm'), 0, 0, tiled=True)  9.44 us
    all_to_all x1, starting transfers between devices, column_rows(): lax.all_to_all(copies, 'tm', 0, 0, axis_index_groups=[[z * COLS + x for z...  9.01 us
    pallas_call x1, Pallas kernels, project(): pl.pallas_call(lambda *refs: project_body(whole, orders, *refs), grid=(wi...  7.7 us
    ppermute x5, starting transfers between devices, swapped(): return lax.ppermute(value, 'utt', [(i, i ^ 1) for i in range(groups)])  7.59 us
  transfers between devices with their start and end apart: 21, of which 8 were waited for; matrix products, arithmetic and copies ran while one was open for 2% of the time, Pallas kernels for 18%

profile of v5, /device:TPU:1, one launch (start us, length us, event | category | flops | bytes accessed | tf_op | source)
XLA Modules:
  0.0 119.1 jit_solution(16331857328504853041)
XLA Ops:
  0.7 1.8 %spread.1 = bf16[8,48,768]{2,1,0:T(8,128)(2,1)} custom-call(s32[1]{0:T(128)} %bitcast.6.start, bf16[48,1536]{1,0:T(8,128)(2,1)} %rows.1), custom_call_target="tpu_custom_call" | custom-call | tf_op jit(solution)/shard_map/spread/pallas_call | solution.py:420
  2.4 9.0 %all-to-all-start = ((bf16[8,48,768]{2,1,0:T(8,128)(2,1)}), bf16[8,48,768]{2,1,0:T(8,128)(2,1)S(1)}, u32[]{:S(2)}, u32[]{:S(2)}) async-start(bf16[8,48,768]{2,1,0:T(8,128)(2,1)} %spread.1), calls=%async_computation | async-start | bytes 1179648 | tf_op jit(solution)/shard_map/all_to_all | solution.py:432
  13.6 4.0 %collective-permute-start = (bf16[16,1536]{1,0:T(8,128)(2,1)S(1)}, bf16[16,1536]{1,0:T(8,128)(2,1)S(1)}, u32[]{:S(2)}, u32[]{:S(2)}) collective-permute-start(bf16[16,1536]{1,0:T(8,128)(2,1)S(1)} %get-tuple-element.53), channel_id=1, source_target_pairs={{0,1},{1,2},{2,3},{3,4},{4,5},{5,6},{6,7},{7,8},{8,9},{9,10},{10,1... | collective-permute-start | bytes 147464 | tf_op jit(solution)/shard_map/ppermute | solution.py:460
  18.9 6.6 %conv.2 = (bf16[256,1536]{1,0:T(8,128)(2,1)}, bf16[12,256,128]{2,1,0:T(8,128)(2,1)}, f32[12,2,160,128]{3,2,1,0:T(8,128)}) custom-call(s32[20]{0:T(128)} %concatenate.3.refs_0_.scalars, bf16[512,1536]{1,0:T(8,128)(2,1)} %refs_1_.5, f32[31,1536]{1,0:T(8,128)} %refs_4_.1, f32[1,1536]{1,0:T(1,128)} %broadcast_in_dim.3.refs_3_.refs_5_), custom_call_target="tpu_custom_call" | custom-call | flops 25165824 | bytes 15728640 | tf_op jit(solution)/shard_map/conv/pallas_call | solution.py:78
  25.5 5.3 %all-to-all-done.refs_6_.refs_3_ = bf16[8,48,768]{2,1,0:T(8,128)(2,1)S(1)} async-done(((bf16[8,48,768]{2,1,0:T(8,128)(2,1)}), bf16[8,48,768]{2,1,0:T(8,128)(2,1)S(1)}, u32[]{:S(2)}, u32[]{:S(2)}) %all-to-all-start) | async-done | bytes 589856 | tf_op jit(solution)/shard_map/all_to_all | solution.py:432
  30.8 2.0 %collective-permute-start.3 = (bf16[8,48,768]{2,1,0:T(8,128)(2,1)S(1)}, bf16[8,48,768]{2,1,0:T(8,128)(2,1)S(1)}, u32[]{:S(2)}, u32[]{:S(2)}) collective-permute-start(bf16[8,48,768]{2,1,0:T(8,128)(2,1)S(1)} %all-to-all-done.refs_6_.refs_3_), channel_id=1, source_target_pairs={{0,3},{1,0},{2,1},{3,2},{4,7},{5,4},{6,5},{7,6},{8,11},{9,8},{10,9... | collective-permute-start | bytes 1769480 | tf_op jit(solution)/shard_map/ppermute | solution.py:402
  32.9 6.6 %conv.3 = (bf16[256,1536]{1,0:T(8,128)(2,1)}, bf16[12,256,128]{2,1,0:T(8,128)(2,1)}, f32[12,2,160,128]{3,2,1,0:T(8,128)}) custom-call(s32[20]{0:T(128)} %concatenate.3.refs_0_.scalars, bf16[512,1536]{1,0:T(8,128)(2,1)} %refs_1_.5, bf16[16,1536]{1,0:T(8,128)(2,1)} %copy-done.14, bf16[16,1536]{1,0:T(8,128)(2,1)} %copy-done.13, f32[31,1536]{1,0:T(8,128)} %refs_4_.1, ...), custom_call_target="tpu_custom_call" | custom-call | flops 25165824 | bytes 15728640 | tf_op jit(solution)/shard_map/conv/pallas_call | solution.py:78
  39.5 5.7 %collective-permute-done.3.refs_10_.refs_7_ = bf16[8,48,768]{2,1,0:T(8,128)(2,1)S(1)} collective-permute-done((bf16[8,48,768]{2,1,0:T(8,128)(2,1)S(1)}, bf16[8,48,768]{2,1,0:T(8,128)(2,1)S(1)}, u32[]{:S(2)}, u32[]{:S(2)}) %collective-permute-start.3) | collective-permute-done | bytes 589856 | tf_op jit(solution)/shard_map/ppermute | solution.py:402
  45.2 2.6 %collective-permute-done.2.refs_8_.refs_5_ = bf16[8,48,768]{2,1,0:T(8,128)(2,1)S(1)} collective-permute-done((bf16[8,48,768]{2,1,0:T(8,128)(2,1)S(1)}, bf16[8,48,768]{2,1,0:T(8,128)(2,1)S(1)}, u32[]{:S(2)}, u32[]{:S(2)}) %collective-permute-start.2) | collective-permute-done | bytes 589856 | tf_op jit(solution)/shard_map/ppermute | solution.py:402
  49.5 2.5 %collective-permute-start.4 = (bf16[8,48,768]{2,1,0:T(8,128)(2,1)S(1)}, bf16[8,48,768]{2,1,0:T(8,128)(2,1)S(1)}, u32[]{:S(2)}, u32[]{:S(2)}) collective-permute-start(bf16[8,48,768]{2,1,0:T(8,128)(2,1)S(1)} %all-to-all-done.refs_6_.refs_3_), channel_id=1, source_target_pairs={{0,32},{32,0},{64,96},{96,64},{128,160},{160,128},{192,224},{224,1... | collective-permute-start | bytes 1769480 | tf_op jit(solution)/shard_map/ppermute | solution.py:405
  52.5 1.9 %collective-permute-done.9.refs_14_.refs_11_ = bf16[4,48,768]{2,1,0:T(8,128)(2,1)S(1)} collective-permute-done((bf16[4,48,768]{2,1,0:T(8,128)(2,1)S(1)}, bf16[4,48,768]{2,1,0:T(8,128)(2,1)S(1)}, u32[]{:S(2)}, u32[]{:S(2)}) %collective-permute-start.9) | collective-permute-done | bytes 294944 | tf_op jit(solution)/shard_map/ppermute | solution.py:402
  54.4 2.9 %collective-permute-start.10 = (bf16[4,48,768]{2,1,0:T(8,128)(2,1)S(1)}, bf16[4,48,768]{2,1,0:T(8,128)(2,1)S(1)}, u32[]{:S(2)}, u32[]{:S(2)}) collective-permute-start(bf16[4,48,768]{2,1,0:T(8,128)(2,1)S(1)} %collective-permute-done.9.refs_14_.refs_11_), channel_id=1, source_target_pairs={{0,32},{32,0},{64,96},{96,64},{128,160},{160,128},{192,224},{224,1... | collective-permute-start | bytes 884744 | tf_op jit(solution)/shard_map/ppermute | solution.py:405
  57.3 1.6 %collective-permute-start.8 = (bf16[4,48,768]{2,1,0:T(8,128)(2,1)S(1)}, bf16[4,48,768]{2,1,0:T(8,128)(2,1)S(1)}, u32[]{:S(2)}, u32[]{:S(2)}) collective-permute-start(bf16[4,48,768]{2,1,0:T(8,128)(2,1)S(1)} %collective-permute-done.7.refs_12_.refs_9_), channel_id=1, source_target_pairs={{0,32},{32,0},{64,96},{96,64},{128,160},{160,128},{192,224},{224,1... | collective-permute-start | bytes 884744 | tf_op jit(solution)/shard_map/ppermute | solution.py:405
  61.5 14.1 %grads.1 = bf16[1536,128]{1,0:T(8,128)(2,1)} custom-call(s32[20]{0:T(128)} %concatenate.3.refs_0_.scalars, bf16[512,1536]{1,0:T(8,128)(2,1)} %refs_1_.6, bf16[12,256,128]{2,1,0:T(8,128)(2,1)} %get-tuple-element.27.refs_2_, f32[12,2,160,128]{3,2,1,0:T(8,128)} %get-tuple-element.28.refs_3_, bf16[12,256,128]{2,1,0:T(8,128)(2,1)} %get-tuple-element.32.refs_4_, ...), custom_call_target="tpu_custom_call" | custom-call | flops 2415919104 | bytes 15728640 | tf_op jit(solution)/shard_map/grads/pallas_call | solution.py:235
  75.7 3.9 %all-to-all-start.1 = ((bf16[32,48,128]{2,1,0:T(8,128)(2,1)}), bf16[32,48,128]{2,1,0:T(8,128)(2,1)S(1)}, u32[]{:S(2)}, u32[]{:S(2)}) async-start(bf16[32,48,128]{2,1,0:T(8,128)(2,1)} %bitcast.8), calls=%async_computation.1 | async-start | bytes 786432 | tf_op jit(solution)/shard_map/all_to_all | solution.py:479
  79.6 7.7 %project.1 = bf16[512,1536]{1,0:T(8,128)(2,1)} custom-call(s32[20]{0:T(128)} %concatenate.3.refs_0_.scalars, bf16[256,1536]{1,0:T(8,128)(2,1)} %get-tuple-element.39.refs_1_, bf16[256,1536]{1,0:T(8,128)(2,1)} %get-tuple-element.40.refs_2_, bf16[8,48,768]{2,1,0:T(8,128)(2,1)} %copy-done.3, bf16[8,48,768]{2,1,0:T(8,128)(2,1)} %copy-done.6, ...), custom_call_target="tpu_custom_call" | custom-call | flops 2415919104 | bytes 7864320 | tf_op jit(solution)/shard_map/project/pallas_call | solution.py:283
  87.3 6.2 %all-to-all-done.1.parts = bf16[32,48,128]{2,1,0:T(8,128)(2,1)S(1)} async-done(((bf16[32,48,128]{2,1,0:T(8,128)(2,1)}), bf16[32,48,128]{2,1,0:T(8,128)(2,1)S(1)}, u32[]{:S(2)}, u32[]{:S(2)}) %all-to-all-start.1) | async-done | bytes 393248 | tf_op jit(solution)/shard_map/all_to_all | solution.py:479
  93.5 2.0 %sums.1 = (f32[256,1,128]{2,1,0:T(1,128)}, f32[32,128]{1,0:T(8,128)S(1)}, f32[32,128]{1,0:T(8,128)S(1)}, f32[32,128]{1,0:T(8,128)S(1)}, f32[32,128]{1,0:T(8,128)...) custom-call(s32[20]{0:T(128)S(1)} %copy-done, ...), custom_call_target="tpu_custom_call" | custom-call | tf_op jit(solution)/shard_map/sums/pallas_call | solution.py:343
  95.5 9.4 %all-to-all-start.2 = ((f32[256,1,128]{2,1,0:T(1,128)}), f32[256,1,128]{2,1,0:T(1,128)S(1)}, u32[]{:S(2)}, u32[]{:S(2)}) async-start(f32[256,1,128]{2,1,0:T(1,128)} %get-tuple-element.43), calls=%async_computation.2 | async-start | bytes 262144 | tf_op jit(solution)/shard_map/all_to_all | solution.py:483
  105.0 2.2 %collective-permute-start.11 = (f32[32,128]{1,0:T(8,128)S(1)}, f32[32,128]{1,0:T(8,128)S(1)}, u32[]{:S(2)}, u32[]{:S(2)}) collective-permute-start(f32[32,128]{1,0:T(8,128)S(1)} %get-tuple-element.45), channel_id=1, source_target_pairs={{0,32},{32,0},{64,96},{96,64},{128,160},{160,128},{192,224},{224,1... | collective-permute-start | bytes 49160 | tf_op jit(solution)/shard_map/ppermute | solution.py:485
  107.2 1.7 %collective-permute-start.13 = (f32[32,128]{1,0:T(8,128)S(1)}, f32[32,128]{1,0:T(8,128)S(1)}, u32[]{:S(2)}, u32[]{:S(2)}) collective-permute-start(f32[32,128]{1,0:T(8,128)S(1)} %get-tuple-element.47), channel_id=1, source_target_pairs={{0,96},{32,64},{64,32},{96,0},{128,224},{160,192},{192,160},{224,1... | collective-permute-start | bytes 49160 | tf_op jit(solution)/shard_map/ppermute | solution.py:485
  110.1 2.1 %collective-permute-start.15 = (f32[32,128]{1,0:T(8,128)S(1)}, f32[32,128]{1,0:T(8,128)S(1)}, u32[]{:S(2)}, u32[]{:S(2)}) collective-permute-start(f32[32,128]{1,0:T(8,128)S(1)} %get-tuple-element.49), channel_id=1, source_target_pairs={{0,160},{32,128},{64,224},{96,192},{128,32},{160,0},{192,96},{224,... | collective-permute-start | bytes 49160 | tf_op jit(solution)/shard_map/ppermute | solution.py:485
  113.1 2.1 %collective-permute-start.17 = (f32[32,128]{1,0:T(8,128)S(1)}, f32[32,128]{1,0:T(8,128)S(1)}, u32[]{:S(2)}, u32[]{:S(2)}) collective-permute-start(f32[32,128]{1,0:T(8,128)S(1)} %get-tuple-element.51), channel_id=1, source_target_pairs={{0,224},{32,192},{64,160},{96,128},{128,96},{160,64},{192,32},{224... | collective-permute-start | bytes 49160 | tf_op jit(solution)/shard_map/ppermute | solution.py:485
  116.3 1.4 %collective-permute-done.17.refs_11_ = f32[32,128]{1,0:T(8,128)S(1)} collective-permute-done((f32[32,128]{1,0:T(8,128)S(1)}, f32[32,128]{1,0:T(8,128)S(1)}, u32[]{:S(2)}, u32[]{:S(2)}) %collective-permute-start.17) | collective-permute-done | bytes 16416 | tf_op jit(solution)/shard_map/ppermute | solution.py:485
  (66 shorter events, 12.7 us)
Async XLA Ops:
  2.4 28.4 %all-to-all-start = ((bf16[8,48,768]{2,1,0:T(8,128)(2,1)}), bf16[8,48,768]{2,1,0:T(8,128)(2,1)S(1)}, u32[]{:S(2)}, u32[]{:S(2)}) async-start(bf16[8,48,768]{2,1,0:T(8,128)(2,1)} %spread.1), calls=%async_computation | async-start | bytes 1179648 | tf_op jit(solution)/shard_map/all_to_all | solution.py:432
  12.3 13.2 %collective-permute-start.1 = (bf16[16,1536]{1,0:T(8,128)(2,1)S(1)}, bf16[16,1536]{1,0:T(8,128)(2,1)S(1)}, u32[]{:S(2)}, u32[]{:S(2)}) collective-permute-start(bf16[16,1536]{1,0:T(8,128)(2,1)S(1)} %get-tuple-element.52), channel_id=1, source_target_pairs={{1,0},{2,1},{3,2},{4,3},{5,4},{6,5},{7,6},{8,7},{9,8},{10,9},{11,1... | collective-permute-start | bytes 147464 | tf_op jit(solution)/shard_map/ppermute | solution.py:461
  13.6 11.9 %collective-permute-start = (bf16[16,1536]{1,0:T(8,128)(2,1)S(1)}, bf16[16,1536]{1,0:T(8,128)(2,1)S(1)}, u32[]{:S(2)}, u32[]{:S(2)}) collective-permute-start(bf16[16,1536]{1,0:T(8,128)(2,1)S(1)} %get-tuple-element.53), channel_id=1, source_target_pairs={{0,1},{1,2},{2,3},{3,4},{4,5},{5,6},{6,7},{7,8},{8,9},{9,10},{10,1... | collective-permute-start | bytes 147464 | tf_op jit(solution)/shard_map/ppermute | solution.py:460
  30.8 30.3 %copy-start.3 = (bf16[8,48,768]{2,1,0:T(8,128)(2,1)}, bf16[8,48,768]{2,1,0:T(8,128)(2,1)S(1)}, u32[]{:S(2)}) copy-start(bf16[8,48,768]{2,1,0:T(8,128)(2,1)S(1)} %all-to-all-done.refs_6_.refs_3_) | copy-start | bytes 1769476
  30.8 14.4 %collective-permute-start.3 = (bf16[8,48,768]{2,1,0:T(8,128)(2,1)S(1)}, bf16[8,48,768]{2,1,0:T(8,128)(2,1)S(1)}, u32[]{:S(2)}, u32[]{:S(2)}) collective-permute-start(bf16[8,48,768]{2,1,0:T(8,128)(2,1)S(1)} %all-to-all-done.refs_6_.refs_3_), channel_id=1, source_target_pairs={{0,3},{1,0},{2,1},{3,2},{4,7},{5,4},{6,5},{7,6},{8,11},{9,8},{10,9... | collective-permute-start | bytes 1769480 | tf_op jit(solution)/shard_map/ppermute | solution.py:402
  32.8 15.0 %collective-permute-start.2 = (bf16[8,48,768]{2,1,0:T(8,128)(2,1)S(1)}, bf16[8,48,768]{2,1,0:T(8,128)(2,1)S(1)}, u32[]{:S(2)}, u32[]{:S(2)}) collective-permute-start(bf16[8,48,768]{2,1,0:T(8,128)(2,1)S(1)} %all-to-all-done.refs_6_.refs_3_), channel_id=1, source_target_pairs={{0,1},{1,2},{2,3},{3,0},{4,5},{5,6},{6,7},{7,4},{8,9},{9,10},{10,1... | collective-permute-start | bytes 1769480 | tf_op jit(solution)/shard_map/ppermute | solution.py:402
  47.8 6.6 %collective-permute-start.9 = (bf16[4,48,768]{2,1,0:T(8,128)(2,1)S(1)}, bf16[4,48,768]{2,1,0:T(8,128)(2,1)S(1)}, u32[]{:S(2)}, u32[]{:S(2)}) collective-permute-start(bf16[4,48,768]{2,1,0:T(8,128)(2,1)S(1)} %slice.15), channel_id=1, source_target_pairs={{0,3},{1,0},{2,1},{3,2},{4,7},{5,4},{6,5},{7,6},{8,11},{9,8},{10,9... | collective-permute-start | bytes 884744 | tf_op jit(solution)/shard_map/ppermute | solution.py:402
  48.3 9.1 %collective-permute-start.7 = (bf16[4,48,768]{2,1,0:T(8,128)(2,1)S(1)}, bf16[4,48,768]{2,1,0:T(8,128)(2,1)S(1)}, u32[]{:S(2)}, u32[]{:S(2)}) collective-permute-start(bf16[4,48,768]{2,1,0:T(8,128)(2,1)S(1)} %slice.14), channel_id=1, source_target_pairs={{0,1},{1,2},{2,3},{3,0},{4,5},{5,6},{6,7},{7,4},{8,9},{9,10},{10,1... | collective-permute-start | bytes 884744 | tf_op jit(solution)/shard_map/ppermute | solution.py:402
  49.5 10.7 %collective-permute-start.4 = (bf16[8,48,768]{2,1,0:T(8,128)(2,1)S(1)}, bf16[8,48,768]{2,1,0:T(8,128)(2,1)S(1)}, u32[]{:S(2)}, u32[]{:S(2)}) collective-permute-start(bf16[8,48,768]{2,1,0:T(8,128)(2,1)S(1)} %all-to-all-done.refs_6_.refs_3_), channel_id=1, source_target_pairs={{0,32},{32,0},{64,96},{96,64},{128,160},{160,128},{192,224},{224,1... | collective-permute-start | bytes 1769480 | tf_op jit(solution)/shard_map/ppermute | solution.py:405
  52.0 8.2 %collective-permute-start.5 = (bf16[8,48,768]{2,1,0:T(8,128)(2,1)S(1)}, bf16[8,48,768]{2,1,0:T(8,128)(2,1)S(1)}, u32[]{:S(2)}, u32[]{:S(2)}) collective-permute-start(bf16[8,48,768]{2,1,0:T(8,128)(2,1)S(1)} %collective-permute-done.2.refs_8_.refs_5_), channel_id=1, source_target_pairs={{0,32},{32,0},{64,96},{96,64},{128,160},{160,128},{192,224},{224,1... | collective-permute-start | bytes 1769480 | tf_op jit(solution)/shard_map/ppermute | solution.py:405
  52.0 8.2 %collective-permute-start.6 = (bf16[8,48,768]{2,1,0:T(8,128)(2,1)S(1)}, bf16[8,48,768]{2,1,0:T(8,128)(2,1)S(1)}, u32[]{:S(2)}, u32[]{:S(2)}) collective-permute-start(bf16[8,48,768]{2,1,0:T(8,128)(2,1)S(1)} %collective-permute-done.3.refs_10_.refs_7_), channel_id=1, source_target_pairs={{0,32},{32,0},{64,96},{96,64},{128,160},{160,128},{192,224},{224,1... | collective-permute-start | bytes 1769480 | tf_op jit(solution)/shard_map/ppermute | solution.py:405
  54.4 4.5 %collective-permute-start.10 = (bf16[4,48,768]{2,1,0:T(8,128)(2,1)S(1)}, bf16[4,48,768]{2,1,0:T(8,128)(2,1)S(1)}, u32[]{:S(2)}, u32[]{:S(2)}) collective-permute-start(bf16[4,48,768]{2,1,0:T(8,128)(2,1)S(1)} %collective-permute-done.9.refs_14_.refs_11_), channel_id=1, source_target_pairs={{0,32},{32,0},{64,96},{96,64},{128,160},{160,128},{192,224},{224,1... | collective-permute-start | bytes 884744 | tf_op jit(solution)/shard_map/ppermute | solution.py:405
  57.3 2.8 %collective-permute-start.8 = (bf16[4,48,768]{2,1,0:T(8,128)(2,1)S(1)}, bf16[4,48,768]{2,1,0:T(8,128)(2,1)S(1)}, u32[]{:S(2)}, u32[]{:S(2)}) collective-permute-start(bf16[4,48,768]{2,1,0:T(8,128)(2,1)S(1)} %collective-permute-done.7.refs_12_.refs_9_), channel_id=1, source_target_pairs={{0,32},{32,0},{64,96},{96,64},{128,160},{160,128},{192,224},{224,1... | collective-permute-start | bytes 884744 | tf_op jit(solution)/shard_map/ppermute | solution.py:405
  75.7 17.8 %all-to-all-start.1 = ((bf16[32,48,128]{2,1,0:T(8,128)(2,1)}), bf16[32,48,128]{2,1,0:T(8,128)(2,1)S(1)}, u32[]{:S(2)}, u32[]{:S(2)}) async-start(bf16[32,48,128]{2,1,0:T(8,128)(2,1)} %bitcast.8), calls=%async_computation.1 | async-start | bytes 786432 | tf_op jit(solution)/shard_map/all_to_all | solution.py:479
  79.6 38.2 %copy-start.1 = (f32[8,4,48]{2,1,0:T(4,128)S(1)}, f32[8,4,48]{2,1,0:T(4,128)}, u32[]{:S(2)}) copy-start(f32[8,4,48]{2,1,0:T(4,128)} %refs_3_.1) | copy-start | bytes 18436
  79.6 38.2 %copy-start.2 = (f32[8]{0:T(128)S(1)}, f32[8]{0:T(128)}, u32[]{:S(2)}) copy-start(f32[8]{0:T(128)} %refs_1_.7) | copy-start | bytes 100
  95.5 22.2 %all-to-all-start.2 = ((f32[256,1,128]{2,1,0:T(1,128)}), f32[256,1,128]{2,1,0:T(1,128)S(1)}, u32[]{:S(2)}, u32[]{:S(2)}) async-start(f32[256,1,128]{2,1,0:T(1,128)} %get-tuple-element.43), calls=%async_computation.2 | async-start | bytes 262144 | tf_op jit(solution)/shard_map/all_to_all | solution.py:483
  105.0 7.3 %collective-permute-start.11 = (f32[32,128]{1,0:T(8,128)S(1)}, f32[32,128]{1,0:T(8,128)S(1)}, u32[]{:S(2)}, u32[]{:S(2)}) collective-permute-start(f32[32,128]{1,0:T(8,128)S(1)} %get-tuple-element.45), channel_id=1, source_target_pairs={{0,32},{32,0},{64,96},{96,64},{128,160},{160,128},{192,224},{224,1... | collective-permute-start | bytes 49160 | tf_op jit(solution)/shard_map/ppermute | solution.py:485
  107.2 5.9 %collective-permute-start.12 = (f32[32,128]{1,0:T(8,128)S(1)}, f32[32,128]{1,0:T(8,128)S(1)}, u32[]{:S(2)}, u32[]{:S(2)}) collective-permute-start(f32[32,128]{1,0:T(8,128)S(1)} %get-tuple-element.46), channel_id=1, source_target_pairs={{0,64},{32,96},{64,0},{96,32},{128,192},{160,224},{192,128},{224,1... | collective-permute-start | bytes 49160 | tf_op jit(solution)/shard_map/ppermute | solution.py:485
  107.2 7.9 %collective-permute-start.13 = (f32[32,128]{1,0:T(8,128)S(1)}, f32[32,128]{1,0:T(8,128)S(1)}, u32[]{:S(2)}, u32[]{:S(2)}) collective-permute-start(f32[32,128]{1,0:T(8,128)S(1)} %get-tuple-element.47), channel_id=1, source_target_pairs={{0,96},{32,64},{64,32},{96,0},{128,224},{160,192},{192,160},{224,1... | collective-permute-start | bytes 49160 | tf_op jit(solution)/shard_map/ppermute | solution.py:485
  108.9 6.2 %collective-permute-start.14 = (f32[32,128]{1,0:T(8,128)S(1)}, f32[32,128]{1,0:T(8,128)S(1)}, u32[]{:S(2)}, u32[]{:S(2)}) collective-permute-start(f32[32,128]{1,0:T(8,128)S(1)} %get-tuple-element.48), channel_id=1, source_target_pairs={{0,128},{32,160},{64,192},{96,224},{128,0},{160,32},{192,64},{224,... | collective-permute-start | bytes 49160 | tf_op jit(solution)/shard_map/ppermute | solution.py:485
  110.1 5.0 %collective-permute-start.15 = (f32[32,128]{1,0:T(8,128)S(1)}, f32[32,128]{1,0:T(8,128)S(1)}, u32[]{:S(2)}, u32[]{:S(2)}) collective-permute-start(f32[32,128]{1,0:T(8,128)S(1)} %get-tuple-element.49), channel_id=1, source_target_pairs={{0,160},{32,128},{64,224},{96,192},{128,32},{160,0},{192,96},{224,... | collective-permute-start | bytes 49160 | tf_op jit(solution)/shard_map/ppermute | solution.py:485
  112.2 4.1 %collective-permute-start.16 = (f32[32,128]{1,0:T(8,128)S(1)}, f32[32,128]{1,0:T(8,128)S(1)}, u32[]{:S(2)}, u32[]{:S(2)}) collective-permute-start(f32[32,128]{1,0:T(8,128)S(1)} %get-tuple-element.50), channel_id=1, source_target_pairs={{0,192},{32,224},{64,128},{96,160},{128,64},{160,96},{192,0},{224,... | collective-permute-start | bytes 49160 | tf_op jit(solution)/shard_map/ppermute | solution.py:485
  113.1 4.7 %collective-permute-start.17 = (f32[32,128]{1,0:T(8,128)S(1)}, f32[32,128]{1,0:T(8,128)S(1)}, u32[]{:S(2)}, u32[]{:S(2)}) collective-permute-start(f32[32,128]{1,0:T(8,128)S(1)} %get-tuple-element.51), channel_id=1, source_target_pairs={{0,224},{32,192},{64,160},{96,128},{128,96},{160,64},{192,32},{224... | collective-permute-start | bytes 49160 | tf_op jit(solution)/shard_map/ppermute | solution.py:485
  (15 other events, 126.6 us)

commit v6 on v5

--- a/solution.py
+++ b/solution.py
@@ -15,7 +15,7 @@
 SLOTS = 32
 COLS = 4
 UTTS = 8
-VMEM = 60 << 20
+VMEM = 52 << 20
 SMALL = 8 << 20
 
 

time: 120 us -> 119 us (level)
  Pallas kernels: 40.2 us -> 37.8 us
  local copies, waits for them, and re-layouts: 3.5 us -> 5.05 us
    unnamed x36, local copies, waits for them, and re-layouts: 1.35 us -> 4.09 us
  transfers between devices with their start and end apart: 21 -> 21, of which waited for: 8 -> 8; matrix products, arithmetic and copies ran while one was open for 2% -> 1% of each run, Pallas kernels for 18% -> 17%
where the time goes in v6:
time: 119 us
  starting transfers between devices  49 us (41%)
  Pallas kernels  37.8 us (32%)
  waiting for transfers between devices  25.9 us (22%)
  local copies, waits for them, and re-layouts  5.05 us (4%)
    pallas_call x1, Pallas kernels, grads(): pl.pallas_call(lambda *refs: grads_body(whole, orders, *refs), in_specs=[...  13.8 us
    pallas_call x2, Pallas kernels, conv(): pl.pallas_call(lambda *refs: conv_body(blks, *refs), grid=(width // STEP,...  12.6 us
    ppermute x4, waiting for transfers between devices, shifted(): return lax.ppermute(value, 'tm', pairs)  10.5 us
    ppermute x7, starting transfers between devices, per_device(): lax.ppermute(shares[k], 'utt', [(g, g ^ k) for g in range(groups)])  10.2 us
    all_to_all x1, starting transfers between devices, per_device(): norms = lax.all_to_all(norms, ('utt', 'tm'), 0, 0, tiled=True)  9.45 us
    all_to_all x1, starting transfers between devices, column_rows(): lax.all_to_all(copies, 'tm', 0, 0, axis_index_groups=[[z * COLS + x for z...  9.01 us
    ppermute x5, starting transfers between devices, swapped(): return lax.ppermute(value, 'utt', [(i, i ^ 1) for i in range(groups)])  7.59 us
    pallas_call x1, Pallas kernels, project(): pl.pallas_call(lambda *refs: project_body(whole, orders, *refs), grid=(wi...  7.18 us
  transfers between devices with their start and end apart: 21, of which 8 were waited for; matrix products, arithmetic and copies ran while one was open for 1% of the time, Pallas kernels for 17%

profile of v6, /device:TPU:1, one launch (start us, length us, event | category | flops | bytes accessed | tf_op | source)
XLA Modules:
  0.0 118.7 jit_solution(18332672165724716680)
XLA Ops:
  2.5 9.0 %all-to-all-start = ((bf16[8,48,768]{2,1,0:T(8,128)(2,1)}), bf16[8,48,768]{2,1,0:T(8,128)(2,1)S(1)}, u32[]{:S(2)}, u32[]{:S(2)}) async-start(bf16[8,48,768]{2,1,0:T(8,128)(2,1)} %spread.1), calls=%async_computation | async-start | bytes 1179648 | tf_op jit(solution)/shard_map/all_to_all | solution.py:432
  13.6 4.0 %collective-permute-start = (bf16[16,1536]{1,0:T(8,128)(2,1)S(1)}, bf16[16,1536]{1,0:T(8,128)(2,1)S(1)}, u32[]{:S(2)}, u32[]{:S(2)}) collective-permute-start(bf16[16,1536]{1,0:T(8,128)(2,1)S(1)} %get-tuple-element.53), channel_id=1, source_target_pairs={{0,1},{1,2},{2,3},{3,4},{4,5},{5,6},{6,7},{7,8},{8,9},{9,10},{10,1... | collective-permute-start | bytes 147464 | tf_op jit(solution)/shard_map/ppermute | solution.py:460
  17.8 6.3 %conv.2 = (bf16[256,1536]{1,0:T(8,128)(2,1)S(1)}, bf16[12,256,128]{2,1,0:T(8,128)(2,1)S(1)}, f32[12,2,160,128]{3,2,1,0:T(8,128)}) custom-call(s32[20]{0:T(128)S(1)} %concatenate.3.refs_0_.scalars, bf16[512,1536]{1,0:T(8,128)(2,1)} %refs_1_.5, f32[31,1536]{1,0:T(8,128)S(1)} %copy-done.4, f32[1,1536]{1,0:T(1,128)S(1)} %broadcast_in_dim.3.refs_3_.refs_5_), custom_call_target="tpu_custom_call" | custom-call | flops 25165824 | bytes 15728640 | tf_op jit(solution)/shard_map/conv/pallas_call | solution.py:78
  25.0 5.9 %all-to-all-done.refs_6_.refs_3_ = bf16[8,48,768]{2,1,0:T(8,128)(2,1)S(1)} async-done(((bf16[8,48,768]{2,1,0:T(8,128)(2,1)}), bf16[8,48,768]{2,1,0:T(8,128)(2,1)S(1)}, u32[]{:S(2)}, u32[]{:S(2)}) %all-to-all-start) | async-done | bytes 589856 | tf_op jit(solution)/shard_map/all_to_all | solution.py:432
  30.8 2.0 %collective-permute-start.3 = (bf16[8,48,768]{2,1,0:T(8,128)(2,1)S(1)}, bf16[8,48,768]{2,1,0:T(8,128)(2,1)S(1)}, u32[]{:S(2)}, u32[]{:S(2)}) collective-permute-start(bf16[8,48,768]{2,1,0:T(8,128)(2,1)S(1)} %all-to-all-done.refs_6_.refs_3_), channel_id=1, source_target_pairs={{0,3},{1,0},{2,1},{3,2},{4,7},{5,4},{6,5},{7,6},{8,11},{9,8},{10,9... | collective-permute-start | bytes 1769480 | tf_op jit(solution)/shard_map/ppermute | solution.py:402
  32.9 6.3 %conv.3 = (bf16[256,1536]{1,0:T(8,128)(2,1)S(1)}, bf16[12,256,128]{2,1,0:T(8,128)(2,1)S(1)}, f32[12,2,160,128]{3,2,1,0:T(8,128)}) custom-call(s32[20]{0:T(128)S(1)} %concatenate.3.refs_0_.scalars, bf16[512,1536]{1,0:T(8,128)(2,1)} %refs_1_.5, bf16[16,1536]{1,0:T(8,128)(2,1)S(1)} %collective-permute-done.refs_2_, ...), custom_call_target="tpu_custom_call" | custom-call | flops 25165824 | bytes 15728640 | tf_op jit(solution)/shard_map/conv/pallas_call | solution.py:78
  39.2 6.1 %collective-permute-done.3.refs_10_.refs_7_ = bf16[8,48,768]{2,1,0:T(8,128)(2,1)S(1)} collective-permute-done((bf16[8,48,768]{2,1,0:T(8,128)(2,1)S(1)}, bf16[8,48,768]{2,1,0:T(8,128)(2,1)S(1)}, u32[]{:S(2)}, u32[]{:S(2)}) %collective-permute-start.3) | collective-permute-done | bytes 589856 | tf_op jit(solution)/shard_map/ppermute | solution.py:402
  45.3 2.6 %collective-permute-done.2.refs_8_.refs_5_ = bf16[8,48,768]{2,1,0:T(8,128)(2,1)S(1)} collective-permute-done((bf16[8,48,768]{2,1,0:T(8,128)(2,1)S(1)}, bf16[8,48,768]{2,1,0:T(8,128)(2,1)S(1)}, u32[]{:S(2)}, u32[]{:S(2)}) %collective-permute-start.2) | collective-permute-done | bytes 589856 | tf_op jit(solution)/shard_map/ppermute | solution.py:402
  49.5 2.5 %collective-permute-start.4 = (bf16[8,48,768]{2,1,0:T(8,128)(2,1)S(1)}, bf16[8,48,768]{2,1,0:T(8,128)(2,1)S(1)}, u32[]{:S(2)}, u32[]{:S(2)}) collective-permute-start(bf16[8,48,768]{2,1,0:T(8,128)(2,1)S(1)} %all-to-all-done.refs_6_.refs_3_), channel_id=1, source_target_pairs={{0,32},{32,0},{64,96},{96,64},{128,160},{160,128},{192,224},{224,1... | collective-permute-start | bytes 1769480 | tf_op jit(solution)/shard_map/ppermute | solution.py:405
  52.6 1.9 %collective-permute-done.9.refs_14_.refs_11_ = bf16[4,48,768]{2,1,0:T(8,128)(2,1)S(1)} collective-permute-done((bf16[4,48,768]{2,1,0:T(8,128)(2,1)S(1)}, bf16[4,48,768]{2,1,0:T(8,128)(2,1)S(1)}, u32[]{:S(2)}, u32[]{:S(2)}) %collective-permute-start.9) | collective-permute-done | bytes 294944 | tf_op jit(solution)/shard_map/ppermute | solution.py:402
  54.5 2.9 %collective-permute-start.10 = (bf16[4,48,768]{2,1,0:T(8,128)(2,1)S(1)}, bf16[4,48,768]{2,1,0:T(8,128)(2,1)S(1)}, u32[]{:S(2)}, u32[]{:S(2)}) collective-permute-start(bf16[4,48,768]{2,1,0:T(8,128)(2,1)S(1)} %collective-permute-done.9.refs_14_.refs_11_), channel_id=1, source_target_pairs={{0,32},{32,0},{64,96},{96,64},{128,160},{160,128},{192,224},{224,1... | collective-permute-start | bytes 884744 | tf_op jit(solution)/shard_map/ppermute | solution.py:405
  57.4 1.6 %collective-permute-start.8 = (bf16[4,48,768]{2,1,0:T(8,128)(2,1)S(1)}, bf16[4,48,768]{2,1,0:T(8,128)(2,1)S(1)}, u32[]{:S(2)}, u32[]{:S(2)}) collective-permute-start(bf16[4,48,768]{2,1,0:T(8,128)(2,1)S(1)} %collective-permute-done.7.refs_12_.refs_9_), channel_id=1, source_target_pairs={{0,32},{32,0},{64,96},{96,64},{128,160},{160,128},{192,224},{224,1... | collective-permute-start | bytes 884744 | tf_op jit(solution)/shard_map/ppermute | solution.py:405
  61.4 13.8 %grads.1 = bf16[1536,128]{1,0:T(8,128)(2,1)} custom-call(s32[20]{0:T(128)S(1)} %concatenate.3.refs_0_.scalars, bf16[512,1536]{1,0:T(8,128)(2,1)} %refs_1_.6, bf16[12,256,128]{2,1,0:T(8,128)(2,1)} %copy-done.2, f32[12,2,160,128]{3,2,1,0:T(8,128)} %get-tuple-element.28.refs_3_, bf16[12,256,128]{2,1,0:T(8,128)(2,1)} %copy-done.3, ...), custom_call_target="tpu_custom_call" | custom-call | flops 2415919104 | bytes 15728640 | tf_op jit(solution)/shard_map/grads/pallas_call | solution.py:235
  75.3 3.9 %all-to-all-start.1 = ((bf16[32,48,128]{2,1,0:T(8,128)(2,1)}), bf16[32,48,128]{2,1,0:T(8,128)(2,1)S(1)}, u32[]{:S(2)}, u32[]{:S(2)}) async-start(bf16[32,48,128]{2,1,0:T(8,128)(2,1)} %bitcast.7), calls=%async_computation.1 | async-start | bytes 786432 | tf_op jit(solution)/shard_map/all_to_all | solution.py:479
  80.3 7.2 %project.1 = bf16[512,1536]{1,0:T(8,128)(2,1)} custom-call(s32[20]{0:T(128)S(1)} %concatenate.3.refs_0_.scalars, bf16[256,1536]{1,0:T(8,128)(2,1)} %copy-done.8, bf16[256,1536]{1,0:T(8,128)(2,1)} %copy-done.9, bf16[8,48,768]{2,1,0:T(8,128)(2,1)S(1)} %copy-done.1, bf16[8,48,768]{2,1,0:T(8,128)(2,1)} %copy-done.12, bf16[8,48,768]{2,1,0:T(8,128)(2,1)} %copy-done.11, ...), custom_call_target="tpu_custom_call" | custom-call | flops 2415919104 | bytes 7864320 | tf_op jit(solution)/shard_map/project/pallas_call | solution.py:283
  87.5 5.6 %all-to-all-done.1.parts = bf16[32,48,128]{2,1,0:T(8,128)(2,1)S(1)} async-done(((bf16[32,48,128]{2,1,0:T(8,128)(2,1)}), bf16[32,48,128]{2,1,0:T(8,128)(2,1)S(1)}, u32[]{:S(2)}, u32[]{:S(2)}) %all-to-all-start.1) | async-done | bytes 393248 | tf_op jit(solution)/shard_map/all_to_all | solution.py:479
  93.1 2.0 %sums.1 = (f32[256,1,128]{2,1,0:T(1,128)}, f32[32,128]{1,0:T(8,128)S(1)}, f32[32,128]{1,0:T(8,128)S(1)}, f32[32,128]{1,0:T(8,128)S(1)}, f32[32,128]{1,0:T(8,128)...) custom-call(s32[20]{0:T(128)S(1)} %concatenate.3.refs_0_.scalars, ...), custom_call_target="tpu_custom_call" | custom-call | tf_op jit(solution)/shard_map/sums/pallas_call | solution.py:343
  95.1 9.5 %all-to-all-start.2 = ((f32[256,1,128]{2,1,0:T(1,128)}), f32[256,1,128]{2,1,0:T(1,128)S(1)}, u32[]{:S(2)}, u32[]{:S(2)}) async-start(f32[256,1,128]{2,1,0:T(1,128)} %get-tuple-element.43), calls=%async_computation.2 | async-start | bytes 262144 | tf_op jit(solution)/shard_map/all_to_all | solution.py:483
  104.6 2.2 %collective-permute-start.11 = (f32[32,128]{1,0:T(8,128)S(1)}, f32[32,128]{1,0:T(8,128)S(1)}, u32[]{:S(2)}, u32[]{:S(2)}) collective-permute-start(f32[32,128]{1,0:T(8,128)S(1)} %get-tuple-element.45), channel_id=1, source_target_pairs={{0,32},{32,0},{64,96},{96,64},{128,160},{160,128},{192,224},{224,1... | collective-permute-start | bytes 49160 | tf_op jit(solution)/shard_map/ppermute | solution.py:485
  106.8 1.7 %collective-permute-start.13 = (f32[32,128]{1,0:T(8,128)S(1)}, f32[32,128]{1,0:T(8,128)S(1)}, u32[]{:S(2)}, u32[]{:S(2)}) collective-permute-start(f32[32,128]{1,0:T(8,128)S(1)} %get-tuple-element.47), channel_id=1, source_target_pairs={{0,96},{32,64},{64,32},{96,0},{128,224},{160,192},{192,160},{224,1... | collective-permute-start | bytes 49160 | tf_op jit(solution)/shard_map/ppermute | solution.py:485
  109.7 2.1 %collective-permute-start.15 = (f32[32,128]{1,0:T(8,128)S(1)}, f32[32,128]{1,0:T(8,128)S(1)}, u32[]{:S(2)}, u32[]{:S(2)}) collective-permute-start(f32[32,128]{1,0:T(8,128)S(1)} %get-tuple-element.49), channel_id=1, source_target_pairs={{0,160},{32,128},{64,224},{96,192},{128,32},{160,0},{192,96},{224,... | collective-permute-start | bytes 49160 | tf_op jit(solution)/shard_map/ppermute | solution.py:485
  112.7 2.1 %collective-permute-start.17 = (f32[32,128]{1,0:T(8,128)S(1)}, f32[32,128]{1,0:T(8,128)S(1)}, u32[]{:S(2)}, u32[]{:S(2)}) collective-permute-start(f32[32,128]{1,0:T(8,128)S(1)} %get-tuple-element.51), channel_id=1, source_target_pairs={{0,224},{32,192},{64,160},{96,128},{128,96},{160,64},{192,32},{224... | collective-permute-start | bytes 49160 | tf_op jit(solution)/shard_map/ppermute | solution.py:485
  115.9 1.4 %collective-permute-done.17.refs_11_ = f32[32,128]{1,0:T(8,128)S(1)} collective-permute-done((f32[32,128]{1,0:T(8,128)S(1)}, f32[32,128]{1,0:T(8,128)S(1)}, u32[]{:S(2)}, u32[]{:S(2)}) %collective-permute-start.17) | collective-permute-done | bytes 16416 | tf_op jit(solution)/shard_map/ppermute | solution.py:485
  117.4 1.3 %finish.1 = f32[4,48]{1,0:T(4,128)} custom-call(s32[20]{0:T(128)S(1)} %concatenate.3.refs_0_.scalars, f32[8]{0:T(128)S(1)} %copy-done.7, f32[256,1,128]{2,1,0:T(1,128)S(1)} %all-to-all-done.2.refs_2_, f32[8,4,48]{2,1,0:T(4,128)S(1)} %copy-done.6, f32[32,128]{1,0:T(8,128)S(1)} %get-tuple-element.44.refs_4_, f32[32,128]{1,0:T(8,128)S(1)} %collective-permute-done.11.refs_5_, ...), custom_call_target="tpu_custom_call" | custom-call | tf_op jit(solution)/shard_map/finish/pallas_call | solution.py:385
  (66 shorter events, 13.8 us)
Async XLA Ops:
  2.5 28.4 %all-to-all-start = ((bf16[8,48,768]{2,1,0:T(8,128)(2,1)}), bf16[8,48,768]{2,1,0:T(8,128)(2,1)S(1)}, u32[]{:S(2)}, u32[]{:S(2)}) async-start(bf16[8,48,768]{2,1,0:T(8,128)(2,1)} %spread.1), calls=%async_computation | async-start | bytes 1179648 | tf_op jit(solution)/shard_map/all_to_all | solution.py:432
  12.3 12.6 %collective-permute-start.1 = (bf16[16,1536]{1,0:T(8,128)(2,1)S(1)}, bf16[16,1536]{1,0:T(8,128)(2,1)S(1)}, u32[]{:S(2)}, u32[]{:S(2)}) collective-permute-start(bf16[16,1536]{1,0:T(8,128)(2,1)S(1)} %get-tuple-element.52), channel_id=1, source_target_pairs={{1,0},{2,1},{3,2},{4,3},{5,4},{6,5},{7,6},{8,7},{9,8},{10,9},{11,1... | collective-permute-start | bytes 147464 | tf_op jit(solution)/shard_map/ppermute | solution.py:461
  13.6 11.4 %collective-permute-start = (bf16[16,1536]{1,0:T(8,128)(2,1)S(1)}, bf16[16,1536]{1,0:T(8,128)(2,1)S(1)}, u32[]{:S(2)}, u32[]{:S(2)}) collective-permute-start(bf16[16,1536]{1,0:T(8,128)(2,1)S(1)} %get-tuple-element.53), channel_id=1, source_target_pairs={{0,1},{1,2},{2,3},{3,4},{4,5},{5,6},{6,7},{7,8},{8,9},{9,10},{10,1... | collective-permute-start | bytes 147464 | tf_op jit(solution)/shard_map/ppermute | solution.py:460
  30.8 14.4 %collective-permute-start.3 = (bf16[8,48,768]{2,1,0:T(8,128)(2,1)S(1)}, bf16[8,48,768]{2,1,0:T(8,128)(2,1)S(1)}, u32[]{:S(2)}, u32[]{:S(2)}) collective-permute-start(bf16[8,48,768]{2,1,0:T(8,128)(2,1)S(1)} %all-to-all-done.refs_6_.refs_3_), channel_id=1, source_target_pairs={{0,3},{1,0},{2,1},{3,2},{4,7},{5,4},{6,5},{7,6},{8,11},{9,8},{10,9... | collective-permute-start | bytes 1769480 | tf_op jit(solution)/shard_map/ppermute | solution.py:402
  32.9 15.0 %collective-permute-start.2 = (bf16[8,48,768]{2,1,0:T(8,128)(2,1)S(1)}, bf16[8,48,768]{2,1,0:T(8,128)(2,1)S(1)}, u32[]{:S(2)}, u32[]{:S(2)}) collective-permute-start(bf16[8,48,768]{2,1,0:T(8,128)(2,1)S(1)} %all-to-all-done.refs_6_.refs_3_), channel_id=1, source_target_pairs={{0,1},{1,2},{2,3},{3,0},{4,5},{5,6},{6,7},{7,4},{8,9},{9,10},{10,1... | collective-permute-start | bytes 1769480 | tf_op jit(solution)/shard_map/ppermute | solution.py:402
  39.2 36.1 %copy-start.9 = (bf16[256,1536]{1,0:T(8,128)(2,1)}, bf16[256,1536]{1,0:T(8,128)(2,1)S(1)}, u32[]{:S(2)}) copy-start(bf16[256,1536]{1,0:T(8,128)(2,1)S(1)} %get-tuple-element.40.refs_2_) | copy-start | bytes 2359300
  47.9 6.6 %collective-permute-start.9 = (bf16[4,48,768]{2,1,0:T(8,128)(2,1)S(1)}, bf16[4,48,768]{2,1,0:T(8,128)(2,1)S(1)}, u32[]{:S(2)}, u32[]{:S(2)}) collective-permute-start(bf16[4,48,768]{2,1,0:T(8,128)(2,1)S(1)} %slice.15), channel_id=1, source_target_pairs={{0,3},{1,0},{2,1},{3,2},{4,7},{5,4},{6,5},{7,6},{8,11},{9,8},{10,9... | collective-permute-start | bytes 884744 | tf_op jit(solution)/shard_map/ppermute | solution.py:402
  48.3 9.1 %collective-permute-start.7 = (bf16[4,48,768]{2,1,0:T(8,128)(2,1)S(1)}, bf16[4,48,768]{2,1,0:T(8,128)(2,1)S(1)}, u32[]{:S(2)}, u32[]{:S(2)}) collective-permute-start(bf16[4,48,768]{2,1,0:T(8,128)(2,1)S(1)} %slice.14), channel_id=1, source_target_pairs={{0,1},{1,2},{2,3},{3,0},{4,5},{5,6},{6,7},{7,4},{8,9},{9,10},{10,1... | collective-permute-start | bytes 884744 | tf_op jit(solution)/shard_map/ppermute | solution.py:402
  49.5 10.7 %collective-permute-start.4 = (bf16[8,48,768]{2,1,0:T(8,128)(2,1)S(1)}, bf16[8,48,768]{2,1,0:T(8,128)(2,1)S(1)}, u32[]{:S(2)}, u32[]{:S(2)}) collective-permute-start(bf16[8,48,768]{2,1,0:T(8,128)(2,1)S(1)} %all-to-all-done.refs_6_.refs_3_), channel_id=1, source_target_pairs={{0,32},{32,0},{64,96},{96,64},{128,160},{160,128},{192,224},{224,1... | collective-permute-start | bytes 1769480 | tf_op jit(solution)/shard_map/ppermute | solution.py:405
  52.1 8.2 %collective-permute-start.5 = (bf16[8,48,768]{2,1,0:T(8,128)(2,1)S(1)}, bf16[8,48,768]{2,1,0:T(8,128)(2,1)S(1)}, u32[]{:S(2)}, u32[]{:S(2)}) collective-permute-start(bf16[8,48,768]{2,1,0:T(8,128)(2,1)S(1)} %collective-permute-done.2.refs_8_.refs_5_), channel_id=1, source_target_pairs={{0,32},{32,0},{64,96},{96,64},{128,160},{160,128},{192,224},{224,1... | collective-permute-start | bytes 1769480 | tf_op jit(solution)/shard_map/ppermute | solution.py:405
  52.1 8.2 %collective-permute-start.6 = (bf16[8,48,768]{2,1,0:T(8,128)(2,1)S(1)}, bf16[8,48,768]{2,1,0:T(8,128)(2,1)S(1)}, u32[]{:S(2)}, u32[]{:S(2)}) collective-permute-start(bf16[8,48,768]{2,1,0:T(8,128)(2,1)S(1)} %collective-permute-done.3.refs_10_.refs_7_), channel_id=1, source_target_pairs={{0,32},{32,0},{64,96},{96,64},{128,160},{160,128},{192,224},{224,1... | collective-permute-start | bytes 1769480 | tf_op jit(solution)/shard_map/ppermute | solution.py:405
  54.5 4.5 %collective-permute-start.10 = (bf16[4,48,768]{2,1,0:T(8,128)(2,1)S(1)}, bf16[4,48,768]{2,1,0:T(8,128)(2,1)S(1)}, u32[]{:S(2)}, u32[]{:S(2)}) collective-permute-start(bf16[4,48,768]{2,1,0:T(8,128)(2,1)S(1)} %collective-permute-done.9.refs_14_.refs_11_), channel_id=1, source_target_pairs={{0,32},{32,0},{64,96},{96,64},{128,160},{160,128},{192,224},{224,1... | collective-permute-start | bytes 884744 | tf_op jit(solution)/shard_map/ppermute | solution.py:405
  57.4 2.8 %collective-permute-start.8 = (bf16[4,48,768]{2,1,0:T(8,128)(2,1)S(1)}, bf16[4,48,768]{2,1,0:T(8,128)(2,1)S(1)}, u32[]{:S(2)}, u32[]{:S(2)}) collective-permute-start(bf16[4,48,768]{2,1,0:T(8,128)(2,1)S(1)} %collective-permute-done.7.refs_12_.refs_9_), channel_id=1, source_target_pairs={{0,32},{32,0},{64,96},{96,64},{128,160},{160,128},{192,224},{224,1... | collective-permute-start | bytes 884744 | tf_op jit(solution)/shard_map/ppermute | solution.py:405
  75.3 17.8 %all-to-all-start.1 = ((bf16[32,48,128]{2,1,0:T(8,128)(2,1)}), bf16[32,48,128]{2,1,0:T(8,128)(2,1)S(1)}, u32[]{:S(2)}, u32[]{:S(2)}) async-start(bf16[32,48,128]{2,1,0:T(8,128)(2,1)} %bitcast.7), calls=%async_computation.1 | async-start | bytes 786432 | tf_op jit(solution)/shard_map/all_to_all | solution.py:479
  80.3 37.1 %copy-start.6 = (f32[8,4,48]{2,1,0:T(4,128)S(1)}, f32[8,4,48]{2,1,0:T(4,128)}, u32[]{:S(2)}) copy-start(f32[8,4,48]{2,1,0:T(4,128)} %refs_3_.1) | copy-start | bytes 18436
  80.3 37.1 %copy-start.7 = (f32[8]{0:T(128)S(1)}, f32[8]{0:T(128)}, u32[]{:S(2)}) copy-start(f32[8]{0:T(128)} %refs_1_.7) | copy-start | bytes 100
  95.1 22.2 %all-to-all-start.2 = ((f32[256,1,128]{2,1,0:T(1,128)}), f32[256,1,128]{2,1,0:T(1,128)S(1)}, u32[]{:S(2)}, u32[]{:S(2)}) async-start(f32[256,1,128]{2,1,0:T(1,128)} %get-tuple-element.43), calls=%async_computation.2 | async-start | bytes 262144 | tf_op jit(solution)/shard_map/all_to_all | solution.py:483
  104.6 7.3 %collective-permute-start.11 = (f32[32,128]{1,0:T(8,128)S(1)}, f32[32,128]{1,0:T(8,128)S(1)}, u32[]{:S(2)}, u32[]{:S(2)}) collective-permute-start(f32[32,128]{1,0:T(8,128)S(1)} %get-tuple-element.45), channel_id=1, source_target_pairs={{0,32},{32,0},{64,96},{96,64},{128,160},{160,128},{192,224},{224,1... | collective-permute-start | bytes 49160 | tf_op jit(solution)/shard_map/ppermute | solution.py:485
  106.8 5.9 %collective-permute-start.12 = (f32[32,128]{1,0:T(8,128)S(1)}, f32[32,128]{1,0:T(8,128)S(1)}, u32[]{:S(2)}, u32[]{:S(2)}) collective-permute-start(f32[32,128]{1,0:T(8,128)S(1)} %get-tuple-element.46), channel_id=1, source_target_pairs={{0,64},{32,96},{64,0},{96,32},{128,192},{160,224},{192,128},{224,1... | collective-permute-start | bytes 49160 | tf_op jit(solution)/shard_map/ppermute | solution.py:485
  106.8 7.9 %collective-permute-start.13 = (f32[32,128]{1,0:T(8,128)S(1)}, f32[32,128]{1,0:T(8,128)S(1)}, u32[]{:S(2)}, u32[]{:S(2)}) collective-permute-start(f32[32,128]{1,0:T(8,128)S(1)} %get-tuple-element.47), channel_id=1, source_target_pairs={{0,96},{32,64},{64,32},{96,0},{128,224},{160,192},{192,160},{224,1... | collective-permute-start | bytes 49160 | tf_op jit(solution)/shard_map/ppermute | solution.py:485
  108.5 6.2 %collective-permute-start.14 = (f32[32,128]{1,0:T(8,128)S(1)}, f32[32,128]{1,0:T(8,128)S(1)}, u32[]{:S(2)}, u32[]{:S(2)}) collective-permute-start(f32[32,128]{1,0:T(8,128)S(1)} %get-tuple-element.48), channel_id=1, source_target_pairs={{0,128},{32,160},{64,192},{96,224},{128,0},{160,32},{192,64},{224,... | collective-permute-start | bytes 49160 | tf_op jit(solution)/shard_map/ppermute | solution.py:485
  109.7 5.0 %collective-permute-start.15 = (f32[32,128]{1,0:T(8,128)S(1)}, f32[32,128]{1,0:T(8,128)S(1)}, u32[]{:S(2)}, u32[]{:S(2)}) collective-permute-start(f32[32,128]{1,0:T(8,128)S(1)} %get-tuple-element.49), channel_id=1, source_target_pairs={{0,160},{32,128},{64,224},{96,192},{128,32},{160,0},{192,96},{224,... | collective-permute-start | bytes 49160 | tf_op jit(solution)/shard_map/ppermute | solution.py:485
  111.8 4.1 %collective-permute-start.16 = (f32[32,128]{1,0:T(8,128)S(1)}, f32[32,128]{1,0:T(8,128)S(1)}, u32[]{:S(2)}, u32[]{:S(2)}) collective-permute-start(f32[32,128]{1,0:T(8,128)S(1)} %get-tuple-element.50), channel_id=1, source_target_pairs={{0,192},{32,224},{64,128},{96,160},{128,64},{160,96},{192,0},{224,... | collective-permute-start | bytes 49160 | tf_op jit(solution)/shard_map/ppermute | solution.py:485
  112.7 4.7 %collective-permute-start.17 = (f32[32,128]{1,0:T(8,128)S(1)}, f32[32,128]{1,0:T(8,128)S(1)}, u32[]{:S(2)}, u32[]{:S(2)}) collective-permute-start(f32[32,128]{1,0:T(8,128)S(1)} %get-tuple-element.51), channel_id=1, source_target_pairs={{0,224},{32,192},{64,160},{96,128},{128,96},{160,64},{192,32},{224... | collective-permute-start | bytes 49160 | tf_op jit(solution)/shard_map/ppermute | solution.py:485
  (15 other events, 172.4 us)
